TPU v7x, 32 devices: a whole 2x2x4 slice. The times are simulated.
32 devices in a mesh: groups: 2 (over y), ctx: 4 (over z), pair: 2 (over x), tp: 2 (over core).
Axes of the slice: x: 2, y: 2, z: 4, core: 2. Of those that a mesh axis runs over, the one named last changes fastest.
Arguments:
- queries: bfloat16 [4096, 16, 128], P(('groups', 'ctx'), ('pair', 'tp')), parts along dimension 0, may hold values from -5 to 5
- keys: bfloat16 [4096, 4, 128], P(('groups', 'ctx', 'tp'), 'pair'), parts along dimension 0, may hold values from -5 to 5
- values: bfloat16 [4096, 4, 128], P(('groups', 'ctx', 'tp'), 'pair'), parts along dimension 0, may hold values from -6 to 6
- span_order: int32 [8], P('groups'), parts along dimension 0, may hold values from 0 to 3, each once
- lengths: int32 [8], P('groups'), parts along dimension 0, may hold values from 1 to 1024, 2048 in all
- kv_partner: int32 [32, 1], P('groups'), parts along dimension 0, may hold values from 0 to 3; in each aligned block of 16 rows (0 to 15, 16 to 31, ...) at most 8 rows name the same one
Outputs:
- attended: bfloat16 [4096, 16, 128], P(('groups', 'ctx'), ('pair', 'tp')), parts along dimension 0
- decode_cache: bfloat16 [64, 2, 128, 4, 128], P(('groups', 'ctx'), None, ('pair', 'tp')), parts along dimension 0
There are 2 independent parts, one for each index of `groups`. A program takes and returns all parts, laid end to end along the dimension named above; each array names one. Nothing has to cross between parts.
Inputs may be any that keep to these rules, and one draw needn't show every extreme that they name: The lengths sum to 2048; the largest is exactly 1024. `kv_partner`: no decode partner is named by more than 8 blocks, a bound that some block reaches.
All inputs are finite; a program needn't handle non-finite values.
Results may differ from a plain program's by a relative error of at most 0.0037.
Values may be sent and summed in bfloat16 or wider, within the bound.
No kernel may reach another device: no remote copies, remote signals or barrier semaphores. Data moves between devices by JAX's collectives and lax.ppermute only.
A program may use at most 64 MiB of HBM per device.

v0:
```python
import jax
import jax.numpy as jnp
from jax import lax
from jax.sharding import PartitionSpec as P

GROUP = 4
BLK = 128
CAP = 8


neg_big = -1e30
key_block = 1024


def lookup(entries, where_at):
    entry_count = entries.shape[0]
    matches = where_at[..., None] == jnp.arange(entry_count, dtype=jnp.int32)
    return jnp.sum(jnp.where(matches, entries, 0), axis=-1)


def row_position(row_index, span_order, span_total, half_rows):
    block_index = row_index // half_rows
    leading = lookup(span_order, block_index // 2)
    span_index = jnp.where(block_index % 2 == 0, leading, span_total - 1 - leading)
    return span_index * half_rows + row_index % half_rows


def position_row(position, span_order, span_total, half_rows):
    span_index = position // half_rows
    shard_index = jnp.arange(span_order.shape[0], dtype=jnp.int32)
    even_match = span_order == span_index[..., None]
    odd_match = span_total - 1 - span_order == span_index[..., None]
    block_index = jnp.sum(
        jnp.where(even_match, 2 * shard_index, 0) + jnp.where(odd_match, 2 * shard_index + 1, 0),
        axis=-1,
    )
    return block_index * half_rows + position % half_rows


def request_of(position, lengths):
    boundary = jnp.cumsum(lengths)
    return jnp.sum((boundary <= position[..., None]).astype(jnp.int32), axis=-1)


def keep_state(inner):
    return inner


def shards(queries, keys, values, span_order, lengths, kv_partner):
    pair_count = lax.axis_size("pair")
    core_count = lax.axis_size("tp")
    span_total = 2 * lax.axis_size("ctx")
    ctx_index = lax.axis_index("ctx")
    core_index = lax.axis_index("tp")
    query_rows, local_heads, head_width = queries.shape
    half_rows = query_rows // 2
    local_groups = keys.shape[1]
    scale = head_width ** (-0.5)
    query_pos = row_position(
        ctx_index * query_rows + jnp.arange(query_rows, dtype=jnp.int32),
        span_order,
        span_total,
        half_rows,
    )
    query_req = request_of(query_pos, lengths)
    partner = kv_partner[:, 0]
    block_index = jnp.arange(partner.shape[0], dtype=jnp.int32)
    earlier = (partner[None, :] == partner[:, None]) & (block_index[None, :] < block_index[:, None])
    rank = jnp.sum(earlier.astype(jnp.int32), axis=1)
    slot_index = jnp.arange(CAP, dtype=jnp.int32)
    taken = (partner[None, :] == ctx_index) & (rank[None, :] == slot_index[:, None])
    slot_live = jnp.any(taken, axis=1)
    slot_block = jnp.sum(jnp.where(taken, block_index[None, :], 0), axis=1)
    token_share = BLK // (pair_count * core_count)
    pair_index = jnp.arange(pair_count, dtype=jnp.int32)

    def make_absorb(query_block, kv_pick, gathered_row, target, live):

        def attend(state, block_keys, block_values, key_rows):
            key_pos = row_position(key_rows, span_order, span_total, half_rows)
            key_req = request_of(key_pos, lengths)
            visible = (key_pos[None, :] <= query_pos[:, None]) & (
                key_req[None, :] == query_req[:, None]
            )

            def update(inner):
                peak, total, summed = inner
                head_keys = jnp.take(block_keys, kv_pick, axis=1)
                head_values = jnp.take(block_values, kv_pick, axis=1)
                scores = (
                    jnp.einsum(
                        "rhd,nhd->rhn", query_block, head_keys, preferred_element_type=jnp.float32
                    )
                    * scale
                )
                scores = jnp.where(visible[:, None, :], scores, neg_big)
                new_peak = jnp.maximum(peak, jnp.max(scores, axis=2))
                weights = jnp.where(
                    visible[:, None, :], jnp.exp(scores - new_peak[:, :, None]), 0.0
                )
                factor = jnp.exp(peak - new_peak)
                new_total = total * factor + jnp.sum(weights, axis=2)
                product = jnp.einsum(
                    "rhn,nhd->rhd",
                    weights.astype(jnp.bfloat16),
                    head_values,
                    preferred_element_type=jnp.float32,
                )
                return (new_peak, new_total, summed * factor[:, :, None] + product)

            return lax.cond(jnp.any(visible), update, keep_state, state)

        def absorb(carry, piece, start):
            state, selected = carry
            piece_keys, piece_values = piece
            count = piece_keys.shape[0]
            inside = live & (target >= 0) & (target < count)
            safe = jnp.clip(target, 0, count - 1)
            picked = jnp.stack(
                [jnp.take(piece_keys, safe, axis=0), jnp.take(piece_values, safe, axis=0)], axis=1
            )
            selected = jnp.where(
                inside[:, None, :, :, :, None, None], picked, jnp.zeros((), jnp.bfloat16)
            )
            turns = count // key_block
            shaped_keys = piece_keys.reshape(turns, key_block, local_groups, head_width)
            shaped_values = piece_values.reshape(turns, key_block, local_groups, head_width)
            block_starts = key_block * jnp.arange(turns, dtype=jnp.int32)

            def one_block(inner, items):
                block_keys, block_values, block_start = items
                key_rows = gathered_row(block_start + jnp.arange(key_block, dtype=jnp.int32))
                return (attend(inner, block_keys, block_values, key_rows), None)

            state, _ = lax.scan(one_block, state, (shaped_keys, shaped_values, block_starts))
            return (state, selected)

        return absorb

    def same_rows(row_index):
        return row_index

    kv_pick = (core_index * local_heads + jnp.arange(local_heads, dtype=jnp.int32)) // GROUP
    ranges = pair_index[:, None] * core_count + jnp.reshape(core_index, (1,))[None, :]
    wanted = (
        slot_block[:, None, None, None] * BLK
        + ranges[None, :, :, None] * token_share
        + jnp.arange(token_share, dtype=jnp.int32)[None, None, None, :]
    )
    target = position_row(wanted, span_order, span_total, half_rows)
    live = jnp.broadcast_to(slot_live[:, None, None, None], target.shape)
    absorb = make_absorb(queries, kv_pick, same_rows, target, live)
    state = (
        jnp.full((query_rows, local_heads), neg_big, jnp.float32),
        jnp.zeros((query_rows, local_heads), jnp.float32),
        jnp.zeros((query_rows, local_heads, head_width), jnp.float32),
    )
    selected = jnp.zeros(
        target.shape[:1] + (2,) + target.shape[1:] + (local_groups, head_width), jnp.bfloat16
    )
    (peak, total, summed), selected = absorb(
        (state, selected),
        (
            lax.all_gather(keys, ("ctx", "tp"), axis=0, tiled=True),
            lax.all_gather(values, ("ctx", "tp"), axis=0, tiled=True),
        ),
        jnp.int32(0),
    )
    selected = selected[:, :, :, 0]
    attended = (summed / total[:, :, None]).astype(jnp.bfloat16)
    received = lax.all_to_all(selected, "pair", split_axis=2, concat_axis=4, tiled=True)
    decode_cache = received.reshape(CAP, 2, token_share, pair_count * local_groups, head_width)
    return (attended, decode_cache)


def solution(mesh):
    return jax.shard_map(
        shards,
        mesh=mesh,
        in_specs=(
            P(("groups", "ctx"), ("pair", "tp"), None),
            P(("groups", "ctx", "tp"), "pair", None),
            P(("groups", "ctx", "tp"), "pair", None),
            P("groups"),
            P("groups"),
            P("groups", None),
        ),
        out_specs=(
            P(("groups", "ctx"), ("pair", "tp"), None),
            P(("groups", "ctx"), None, ("pair", "tp"), None, None),
        ),
        check_vma=False,
    )
```

profile of v0, /device:TPU:0, one launch (start us, length us, event | category | flops | bytes accessed | tf_op | source)
XLA Modules:
  0.0 128.9 jit_solution(18232661217825183087)
XLA Ops:
  13.0 1.9 %copy.80 = bf16[512,4,128]{2,0,1:T(8,128)(2,1)} copy(bf16[512,4,128]{2,1,0:T(4,128)(2,1)} %param.14) | data formatting | bytes 1048576
  16.0 18.5 %all-gather.3.cloned.1.call-done = bf16[2048,2,128]{2,1,0:T(2,128)(2,1)} async-done(((bf16[256,2,128]{2,1,0:T(2,128)(2,1)}), bf16[2048,2,128]{2,1,0:T(2,128)(2,1)}) %all-gather.3.cloned.1.call-update) | async-done | bytes 1048592 | tf_op jit(solution)/shard_map/all_gather | solution.py:164
  34.4 2.6 %gather_fusion.2 = bf16[512,2,128]{2,1,0:T(2,128)(2,1)S(1)} fusion(bf16[2048,2,128]{2,1,0:T(2,128)(2,1)} %all-gather.3.cloned.1.call-done, s32[1024]{0:T(1024)S(1)} %pad_clamp_fusion.1), kind=kCustom, calls=%fused_computation.1.clone | custom fusion | bytes 526336 | tf_op jit(solution)/shard_map/jit(_take)/gather | solution.py:120
  37.0 20.8 %all-gather.5.cloned.1.call-done = bf16[2048,2,128]{2,1,0:T(2,128)(2,1)} async-done(((bf16[256,2,128]{2,1,0:T(2,128)(2,1)}), bf16[2048,2,128]{2,1,0:T(2,128)(2,1)}) %all-gather.5.cloned.1.call-update) | async-done | bytes 1048592 | tf_op jit(solution)/shard_map/all_gather | solution.py:165
  57.8 2.6 %gather_fusion.3 = bf16[512,2,128]{2,1,0:T(2,128)(2,1)S(1)} fusion(bf16[2048,2,128]{2,1,0:T(2,128)(2,1)} %all-gather.5.cloned.1.call-done, s32[1024]{0:T(1024)S(1)} %pad_clamp_fusion.1), kind=kCustom, calls=%fused_computation.3.clone | custom fusion | bytes 526336 | tf_op jit(solution)/shard_map/jit(_take)/gather | solution.py:120
  61.1 2.1 %broadcast_select_fusion = bf16[8,2,2,32,2,128]{5,4,3,0,1,2:T(2,128)(2,1)} fusion(pred[8,2,32]{2,0,1:T(8,128)(4,1)S(1)} %compare_and_fusion.3, bf16[8,1,2,32,2,128]{5,4,3,0,1,2:T(2,128)(2,1)S(1)} %get-tuple-element.500, bf16[8,1,2,32,2,128]{5,4,3,0,1,2:T(2,128)(2,1)S(1)} %get-tuple-element.499), kind=kLoop, calls=%fused_computation.72 | loop fusion | flops 524288 | bytes 1049088 | tf_op jit(solution)/shard_map/jit(_where)/select_n | solution.py:122
  63.2 3.5 %all-to-all-start = ((bf16[8,2,2,32,2,128]{5,4,3,0,1,2:T(2,128)(2,1)}), bf16[8,2,2,32,2,128]{5,4,3,0,1,2:T(2,128)(2,1)S(1)}, u32[]{:S(2)}, u32[]{:S(2)}) async-start(bf16[8,2,2,32,2,128]{5,4,3,0,1,2:T(2,128)(2,1)} %broadcast_select_fusion), calls=%async_computation | async-start | bytes 1048576 | tf_op jit(solution)/shard_map/all_to_all | solution.py:171
  66.7 2.4 %copy.79 = bf16[2,1024,2,128]{3,1,2,0:T(8,128)(2,1)} copy(bf16[2,1024,2,128]{3,2,1,0:T(2,128)(2,1)} %bitcast.64) | data formatting | bytes 2097152
  69.2 2.3 %copy.81 = bf16[2,1024,2,128]{3,1,2,0:T(8,128)(2,1)} copy(bf16[2,1024,2,128]{3,2,1,0:T(2,128)(2,1)} %bitcast.65) | data formatting | bytes 2097152
  72.6 45.1 %while.18 = (s32[]{:T(128)}, f32[512,4]{0,1:T(4,128)S(1)}, f32[512,4]{0,1:T(4,128)S(1)}, f32[512,4,128]{0,2,1:T(8,128)}, s32[2]{0:T(128)S(1)}, /*index=5*/s32[4]...) while((s32[]{:T(128)}, f32[512,4]{0,1:T(4,128)S(1)}, ...), condition=%wide.region_11.13_spmd.clone, body=%wide.region_3.12_spmd.clone.sunk | while | flops 1104771072 | bytes 72004280 | solution.py:135
  74.9 1.4 %fusion.68 = (pred[]{:T(512)}, pred[512,1024]{0,1:T(8,128)(4,1)S(1)}) fusion(s32[512]{0:T(512)S(1)} %get-tuple-element.642, s32[1024]{0:T(1024)S(1)} %convert_reduce_fusion.4, s32[512]{0:T(512)S(1)} %get-tuple-element.640, s32[1024]{0:T(1024)S(1)} %fusion.67), kind=kLoop, calls=%fused_computation.144.clone.1 | loop fusion | flops 2097151 | bytes 536577 | tf_op jit(solution)/shard_map/while/body/eval_jaxpr/reduce_or | solution.py:111
  77.0 18.1 %conditional.3 = ((f32[512,4]{0,1:T(4,128)S(1)}, f32[512,4]{0,1:T(4,128)S(1)}, f32[512,4,128]{0,2,1:T(8,128)})) conditional(s32[]{:T(128)} %convert_element_type.46, (f32[512,4]{0,1:T(4,128)S(1)}, f32[512,4]{0,1:T(4,128)S(1)}, f32[512,4,128]{0,2,1:T(8,128)}) %tuple.78, (pred[512,1024]{0,1:T(8,128)(4,1)S(1)}, bf16[2,1024,2,128]{3,1,2,0:T(8,128)(2,1)}, ...), branch_computations={%region_7.7_spmd, %region_8.11_spmd} | conditional | flops 1102582784 | bytes 71438584 | solution.py:111
  79.1 2.8 %fusion.2 = (f32[512,4]{0,1:T(4,128)S(1)}, f32[4,1024,512]{2,1,0:T(8,128)S(1)}) fusion(pred[512,1024]{0,1:T(8,128)(4,1)S(1)} %get-tuple-element.283, bf16[512,4,128]{2,0,1:T(8,128)(2,1)} %get-tuple-element.287, bf16[4,1024,128]{2,1,0:T(8,128)(2,1)S(1)} %gather_fusion, pred[4]{0:T(512)(128)(4,1)S(1)} %get-tuple-element.487), kind=kOutput, calls=%fused_computation.7 | convolution fusion | flops 543684608 | bytes 10493956 | tf_op jit(solution)/shard_map/while/body/eval_jaxpr/cond/branch_1_fun/rhd,nhd->rhn/dot_general | solution.py:91
  81.9 3.2 %copy-done = f32[4,1024,512]{2,1,0:T(8,128)} copy-done((f32[4,1024,512]{2,1,0:T(8,128)}, f32[4,1024,512]{2,1,0:T(8,128)S(1)}, u32[]{:S(2)}) %copy-start) | copy-done | bytes 8388632 | tf_op jit(solution)/shard_map/while/body/eval_jaxpr/cond
  85.1 2.1 %fusion.4 = f32[512,4]{0,1:T(4,128)S(1)} fusion(f32[4,1024,512]{2,1,0:T(8,128)S(1)} %get-tuple-element.494, f32[512,4]{0,1:T(4,128)S(1)} %max.8, pred[512,1024]{0,1:T(8,128)(4,1)S(1)} %get-tuple-element.283), kind=kLoop, calls=%fused_computation.9 | loop fusion | flops 10483712 | bytes 8929280 | tf_op jit(solution)/shard_map/while/body/eval_jaxpr/cond/branch_1_fun/reduce_sum | solution.py:102
  88.0 7.2 %fusion.11 = f32[512,4,128]{0,2,1:T(8,128)} fusion(f32[4,1024,512]{2,1,0:T(8,128)} %copy-done, f32[512,4]{0,1:T(4,128)S(1)} %max.8, pred[512,1024]{0,1:T(8,128)(4,1)S(1)} %get-tuple-element.283, bf16[4,1024,128]{2,1,0:T(8,128)(2,1)S(1)} %gather_fusion.1, f32[512,4,128]{0,2,1:T(8,128)} %get-tuple-element.289, pred[4]{0:T(512)(128)(4,1)S(1)} %get-tuple-element.487, ...), kind=kOutput, calls=%fused_computation.13 | convolution fusion | flops 548405248 | bytes 12075012 | tf_op jit(solution)/shard_map/while/body/eval_jaxpr/cond/branch_1_fun/rhn,nhd->rhd/dot_general | solution.py:103
  97.4 1.4 %fusion.68 = (pred[]{:T(512)}, pred[512,1024]{0,1:T(8,128)(4,1)S(1)}) fusion(s32[512]{0:T(512)S(1)} %get-tuple-element.642, s32[1024]{0:T(1024)S(1)} %convert_reduce_fusion.4, s32[512]{0:T(512)S(1)} %get-tuple-element.640, s32[1024]{0:T(1024)S(1)} %fusion.67), kind=kLoop, calls=%fused_computation.144.clone.1 | loop fusion | flops 2097151 | bytes 536577 | tf_op jit(solution)/shard_map/while/body/eval_jaxpr/reduce_or | solution.py:111
  99.6 18.1 %conditional.3 = ((f32[512,4]{0,1:T(4,128)S(1)}, f32[512,4]{0,1:T(4,128)S(1)}, f32[512,4,128]{0,2,1:T(8,128)})) conditional(s32[]{:T(128)} %convert_element_type.46, (f32[512,4]{0,1:T(4,128)S(1)}, f32[512,4]{0,1:T(4,128)S(1)}, f32[512,4,128]{0,2,1:T(8,128)}) %tuple.78, (pred[512,1024]{0,1:T(8,128)(4,1)S(1)}, bf16[2,1024,2,128]{3,1,2,0:T(8,128)(2,1)}, ...), branch_computations={%region_7.7_spmd, %region_8.11_spmd} | conditional | flops 1102582784 | bytes 71438584 | solution.py:111
  101.6 2.8 %fusion.2 = (f32[512,4]{0,1:T(4,128)S(1)}, f32[4,1024,512]{2,1,0:T(8,128)S(1)}) fusion(pred[512,1024]{0,1:T(8,128)(4,1)S(1)} %get-tuple-element.283, bf16[512,4,128]{2,0,1:T(8,128)(2,1)} %get-tuple-element.287, bf16[4,1024,128]{2,1,0:T(8,128)(2,1)S(1)} %gather_fusion, pred[4]{0:T(512)(128)(4,1)S(1)} %get-tuple-element.487), kind=kOutput, calls=%fused_computation.7 | convolution fusion | flops 543684608 | bytes 10493956 | tf_op jit(solution)/shard_map/while/body/eval_jaxpr/cond/branch_1_fun/rhd,nhd->rhn/dot_general | solution.py:91
  104.5 3.2 %copy-done = f32[4,1024,512]{2,1,0:T(8,128)} copy-done((f32[4,1024,512]{2,1,0:T(8,128)}, f32[4,1024,512]{2,1,0:T(8,128)S(1)}, u32[]{:S(2)}) %copy-start) | copy-done | bytes 8388632 | tf_op jit(solution)/shard_map/while/body/eval_jaxpr/cond
  107.7 2.1 %fusion.4 = f32[512,4]{0,1:T(4,128)S(1)} fusion(f32[4,1024,512]{2,1,0:T(8,128)S(1)} %get-tuple-element.494, f32[512,4]{0,1:T(4,128)S(1)} %max.8, pred[512,1024]{0,1:T(8,128)(4,1)S(1)} %get-tuple-element.283), kind=kLoop, calls=%fused_computation.9 | loop fusion | flops 10483712 | bytes 8929280 | tf_op jit(solution)/shard_map/while/body/eval_jaxpr/cond/branch_1_fun/reduce_sum | solution.py:102
  110.5 7.2 %fusion.11 = f32[512,4,128]{0,2,1:T(8,128)} fusion(f32[4,1024,512]{2,1,0:T(8,128)} %copy-done, f32[512,4]{0,1:T(4,128)S(1)} %max.8, pred[512,1024]{0,1:T(8,128)(4,1)S(1)} %get-tuple-element.283, bf16[4,1024,128]{2,1,0:T(8,128)(2,1)S(1)} %gather_fusion.1, f32[512,4,128]{0,2,1:T(8,128)} %get-tuple-element.289, pred[4]{0:T(512)(128)(4,1)S(1)} %get-tuple-element.487, ...), kind=kOutput, calls=%fused_computation.13 | convolution fusion | flops 548405248 | bytes 12075012 | tf_op jit(solution)/shard_map/while/body/eval_jaxpr/cond/branch_1_fun/rhn,nhd->rhd/dot_general | solution.py:103
  117.7 1.6 %copy.83 = f32[512,4,128]{2,1,0:T(4,128)S(1)} copy(f32[512,4,128]{0,2,1:T(8,128)} %get-tuple-element.312) | data formatting | bytes 2097152 | tf_op jit(solution)/shard_map/while | solution.py:135
  119.5 1.4 %divide_convert_fusion = bf16[512,4,128]{2,1,0:T(4,128)(2,1)} fusion(f32[512,4,128]{2,1,0:T(4,128)S(1)} %copy.83, f32[512,4]{1,0:T(8,128)S(1)} %copy.82), kind=kLoop, calls=%fused_computation.71 | loop fusion | flops 524288 | bytes 1581056 | tf_op jit(solution)/shard_map/convert_element_type | solution.py:170
  (72 shorter events, 20.2 us)
Async XLA Ops:
  7.2 65.5 %copy-start.1 = (s32[4]{0:T(128)S(1)}, s32[4]{0:T(128)}, u32[]{:S(2)}) copy-start(s32[4]{0:T(128)} %param.17) | copy-start | bytes 52
  7.2 27.3 %all-gather.3.cloned.1.call-start = ((), (), s32[]{:S(2)}) async-start(), calls=%async_computation.1 | async-start | bytes 1179648 | tf_op jit(solution)/shard_map/all_gather | solution.py:164
  7.9 49.9 %all-gather.5.cloned.1.call-start = ((), (), s32[]{:S(2)}) async-start(), calls=%async_computation.2 | async-start | bytes 1179648 | tf_op jit(solution)/shard_map/all_gather | solution.py:165
  63.2 57.6 %all-to-all-start = ((bf16[8,2,2,32,2,128]{5,4,3,0,1,2:T(2,128)(2,1)}), bf16[8,2,2,32,2,128]{5,4,3,0,1,2:T(2,128)(2,1)S(1)}, u32[]{:S(2)}, u32[]{:S(2)}) async-start(bf16[8,2,2,32,2,128]{5,4,3,0,1,2:T(2,128)(2,1)} %broadcast_select_fusion), calls=%async_computation | async-start | bytes 1048576 | tf_op jit(solution)/shard_map/all_to_all | solution.py:171
  81.9 3.2 %copy-start = (f32[4,1024,512]{2,1,0:T(8,128)}, f32[4,1024,512]{2,1,0:T(8,128)S(1)}, u32[]{:S(2)}) copy-start(f32[4,1024,512]{2,1,0:T(8,128)S(1)} %get-tuple-element.494) | copy-start | bytes 25165828 | tf_op jit(solution)/shard_map/while/body/eval_jaxpr/cond
  104.4 3.2 %copy-start = (f32[4,1024,512]{2,1,0:T(8,128)}, f32[4,1024,512]{2,1,0:T(8,128)S(1)}, u32[]{:S(2)}) copy-start(f32[4,1024,512]{2,1,0:T(8,128)S(1)} %get-tuple-element.494) | copy-start | bytes 25165828 | tf_op jit(solution)/shard_map/while/body/eval_jaxpr/cond
Sparse Core Ops, SparseCore 0:
  9.6 24.7 all-gather.2
  36.0 21.7 all-gather.4
where the time goes:
time: 130 us; the launch traced here: 129 us
  waiting for transfers between devices  40.6 us (31%)
  local copies, waits for them, and re-layouts  29.2 us (22%)
  matrix products  19.9 us (15%)
  other arithmetic  19.8 us (15%)
  between operations  14.2 us (11%)
  starting transfers between devices  3.56 us (3%)
  loops' own time  1.6 us (1%)
    all_gather x1, waiting for transfers between devices, shards(): lax.all_gather(values, ('ctx', 'tp'), axis=0, tiled=True)  20.8 us
    all_gather x1, waiting for transfers between devices, shards(): lax.all_gather(keys, ('ctx', 'tp'), axis=0, tiled=True)  18.5 us
    dot_general x2, matrix products, update(): jnp.einsum('rhn,nhd->rhd', weights.astype(jnp.bfloat16), head_values, pre...  14.3 us
    unnamed x6, local copies, waits for them, and re-layouts  7.74 us
    cond x6, local copies, waits for them, and re-layouts  6.4 us
    dot_general x2, matrix products, update(): jnp.einsum('rhd,nhd->rhn', query_block, head_keys, preferred_element_type...  5.57 us
    reduce_sum x2, other arithmetic, update(): new_total = total * factor + jnp.sum(weights, axis=2)  4.18 us
    all_to_all x1, starting transfers between devices, shards(): lax.all_to_all(selected, 'pair', split_axis=2, concat_axis=4, tiled=True)  3.49 us
  transfers between devices with their start and end apart: 3, of which 2 were waited for; matrix products, arithmetic and copies ran while one was open for 43% of the time, Pallas kernels for 0%

commit v1 on v0

--- a/solution.py
+++ b/solution.py
@@ -1,6 +1,10 @@
+import functools
+
 import jax
 import jax.numpy as jnp
 from jax import lax
+from jax.experimental import pallas as pl
+from jax.experimental.pallas import tpu as pltpu
 from jax.sharding import PartitionSpec as P
 
 GROUP = 4
@@ -173,9 +177,349 @@
     return (attended, decode_cache)
 
 
+HALF_TOKENS = BLK // 2
+LOG2E = 1.4426950408889634
+MASKED = -1e30
+FLOOR = -1e29
+Q_TILE = 512
+
+
+def span_of(order_ref, shard, half, span_total):
+    leading = order_ref[shard]
+    return leading if half == 0 else span_total - 1 - leading
+
+
+def split_kernel(key_a, key_b, value_a, value_b, cross_ref, stay_ref, wide):
+    pair = lax.axis_index("pair")
+    core = lax.axis_index("tp")
+    for kind, (own, other) in enumerate(((key_a, key_b), (value_a, value_b))):
+        wide[kind, core] = own[...].astype(jnp.float32)
+        wide[kind, 1 - core] = other[...].astype(jnp.float32)
+    for kind in range(2):
+        for block in range(4):
+            for out, part in ((cross_ref, 1 - pair), (stay_ref, pair)):
+                first = (block % 2) * 2 * BLK + part * 2 * HALF_TOKENS + core
+                rows = wide[kind, block // 2, pl.ds(first, HALF_TOKENS, stride=2), :]
+                out[kind, pl.ds(block * HALF_TOKENS, HALF_TOKENS), :] = rows.astype(jnp.bfloat16)
+
+
+def split_heads(keys, keys_other, values, values_other):
+    rows = keys.shape[0]
+    piece = jax.ShapeDtypeStruct((2, rows // 2, keys.shape[1]), jnp.bfloat16)
+    return pl.pallas_call(
+        split_kernel,
+        out_shape=(piece, piece),
+        scratch_shapes=[pltpu.VMEM((2, 2, rows, keys.shape[1]), jnp.float32)],
+        name="split_heads",
+    )(keys, keys_other, values, values_other)
+
+
+def attend_kernel(sources, first, last, shard_count, heads, *refs):
+    order_ref, lengths_ref, query_ref = refs[:3]
+    refs = refs[3:]
+    pieces, refs = refs[: len(sources)], refs[len(sources) :]
+    if not first:
+        peak_in, total_in, summed_in = refs[:3]
+        refs = refs[3:]
+    if last:
+        out_ref, peak_ref, total_ref, summed_ref = refs
+    else:
+        peak_ref, total_ref, summed_ref = refs
+    shard = lax.axis_index("ctx")
+    pair = lax.axis_index("pair")
+    span_total = 2 * shard_count
+    rows, width = query_ref.shape
+    tokens = rows // heads
+    half_rows = tokens // 2
+    factor = LOG2E * width**-0.5
+    starts = [jnp.int32(0)]
+    for r in range(lengths_ref.shape[0] - 1):
+        starts.append(starts[-1] + lengths_ref[r])
+
+    def begin_of(position):
+        begin = jnp.zeros_like(position)
+        for start in starts[1:]:
+            begin = jnp.where(start <= position, start, begin)
+        return begin
+
+    if first:
+        peak_ref[...] = jnp.full(peak_ref.shape, FLOOR, jnp.float32)
+        total_ref[...] = jnp.zeros(total_ref.shape, jnp.float32)
+        summed_ref[...] = jnp.zeros(summed_ref.shape, jnp.float32)
+    else:
+        peak_ref[...] = peak_in[...]
+        total_ref[...] = total_in[...]
+        summed_ref[...] = summed_in[...]
+
+    tile_tokens = Q_TILE // heads
+    tiles_half = half_rows // tile_tokens
+
+    def tile(index, _):
+        at = pl.multiple_of(index * Q_TILE, Q_TILE)
+        columns = pl.ds(at, Q_TILE)
+        own_lead = order_ref[shard]
+        query_span = jnp.where(index < tiles_half, own_lead, span_total - 1 - own_lead)
+        first_pos = query_span * half_rows + lax.rem(index, tiles_half) * tile_tokens
+        offset = lax.broadcasted_iota(jnp.int32, (1, Q_TILE), 1) // heads
+        query_pos = first_pos + offset
+        query_begin = begin_of(query_pos)
+        begin_low = begin_of(first_pos)
+        for (shift, cross), piece in zip(sources, pieces):
+            source = lax.rem(shard + shift, shard_count)
+            lead = order_ref[source]
+            part = (1 - pair) if cross else pair
+            piece_half = piece.shape[1] // 2
+            for half in range(2):
+                key_span = lead if half == 0 else span_total - 1 - lead
+                key_first = key_span * half_rows
+                near = (key_first <= first_pos + tile_tokens - 1) & (
+                    key_first + half_rows - 1 >= begin_low
+                )
+
+                @pl.when(near)
+                def _():
+                    key_rows = piece[0, pl.ds(half * piece_half, piece_half), :]
+                    value_rows = piece[1, pl.ds(half * piece_half, piece_half), :]
+                    scores = lax.dot_general(
+                        key_rows,
+                        query_ref[columns, :],
+                        (((1,), (1,)), ((), ())),
+                        preferred_element_type=jnp.float32,
+                    )
+                    local = lax.broadcasted_iota(jnp.int32, (piece_half, 1), 0)
+                    key_pos = (
+                        key_first
+                        + part * HALF_TOKENS
+                        + local
+                        + jnp.where(local >= HALF_TOKENS, BLK - HALF_TOKENS, 0)
+                    )
+                    visible = (key_pos <= query_pos) & (key_pos >= query_begin)
+                    scores = jnp.where(visible, scores, MASKED)
+                    old_peak = peak_ref[:, columns]
+                    peak = jnp.maximum(old_peak, jnp.max(scores, axis=0, keepdims=True))
+                    weights = jnp.exp2((scores - peak) * factor)
+                    fade = jnp.exp2((old_peak - peak) * factor)
+                    peak_ref[:, columns] = peak
+                    total_ref[:, columns] = total_ref[:, columns] * fade + jnp.sum(
+                        weights, axis=0, keepdims=True
+                    )
+                    product = lax.dot_general(
+                        value_rows,
+                        weights.astype(jnp.bfloat16),
+                        (((0,), (0,)), ((), ())),
+                        preferred_element_type=jnp.float32,
+                    )
+                    summed_ref[:, columns] = summed_ref[:, columns] * fade + product
+
+        if last:
+            result = summed_ref[:, columns] / total_ref[:, columns]
+            out_ref[columns, :] = jnp.transpose(result).astype(jnp.bfloat16)
+        return 0
+
+    lax.fori_loop(0, rows // Q_TILE, tile, 0)
+
+
+def attend(order, lengths, query, pieces, sources, state, last, shard_count, heads):
+    rows, width = query.shape
+    first = state is None
+    smem = pl.BlockSpec(memory_space=pltpu.SMEM)
+    vmem = pl.BlockSpec(memory_space=pltpu.VMEM)
+    shapes = [((1, rows), jnp.float32), ((1, rows), jnp.float32), ((width, rows), jnp.float32)]
+    state = () if first else state
+    if last:
+        out_shape = jax.ShapeDtypeStruct((rows, width), jnp.bfloat16)
+        scratch = [pltpu.VMEM(s, d) for s, d in shapes]
+        out_specs = vmem
+    else:
+        out_shape = tuple(jax.ShapeDtypeStruct(s, d) for s, d in shapes)
+        scratch = []
+        out_specs = (vmem,) * 3
+    keys_seen = sum(p.shape[1] for p in pieces)
+    return pl.pallas_call(
+        functools.partial(attend_kernel, sources, first, last, shard_count, heads),
+        out_shape=out_shape,
+        in_specs=[smem, smem] + [vmem] * (1 + len(pieces) + len(state)),
+        out_specs=out_specs,
+        scratch_shapes=scratch,
+        cost_estimate=pl.CostEstimate(
+            flops=2 * rows * width * keys_seen,
+            bytes_accessed=4 * rows * width,
+            transcendentals=rows * keys_seen // 2,
+        ),
+        name="attend",
+    )(order, lengths, query, *pieces, *state)
+
+
+def find_slots(order_ref, partner_ref, block_at, shard, shard_count):
+    for slot in range(CAP):
+        block_at[slot] = -1
+    taken = jnp.int32(0)
+    for block in range(partner_ref.shape[0]):
+        mine = partner_ref[block] == shard
+
+        @pl.when(mine)
+        def _():
+            block_at[taken] = block
+
+        taken = taken + mine.astype(jnp.int32)
+
+
+def locate(order_ref, block, shard, shard_count):
+    span = block // 2
+    source = jnp.int32(0)
+    half = jnp.int32(0)
+    for index in range(shard_count):
+        lead = order_ref[index]
+        source = jnp.where((lead == span) | (2 * shard_count - 1 - lead == span), index, source)
+        half = jnp.where(2 * shard_count - 1 - lead == span, 1, half)
+    return lax.rem(source - shard + shard_count, shard_count), half * 2 + lax.rem(block, 2)
+
+
+def pick_kernel(shard_count, order_ref, partner_ref, *refs):
+    stay, cross = refs[:shard_count], refs[shard_count : 2 * shard_count]
+    out_ref, block_at = refs[2 * shard_count :]
+    shard = lax.axis_index("ctx")
+    core = lax.axis_index("tp")
+    share = HALF_TOKENS // 2
+    find_slots(order_ref, partner_ref, block_at, shard, shard_count)
+    for slot in range(CAP):
+        block = block_at[slot]
+        shift, place = locate(order_ref, jnp.maximum(block, 0), shard, shard_count)
+        begin = pl.multiple_of(place * HALF_TOKENS + (1 - core) * share, share)
+
+        for index in range(shard_count):
+
+            @pl.when((block >= 0) & (shift == index))
+            def _():
+                for which, group in enumerate((stay, cross)):
+                    for kind in range(2):
+                        out_ref[slot, kind, which] = group[index][kind, pl.ds(begin, share), :]
+
+        @pl.when(block < 0)
+        def _():
+            out_ref[slot] = jnp.zeros(out_ref.shape[1:], out_ref.dtype)
+
+
+def pick(order, partner, stay, cross, shard_count):
+    smem = pl.BlockSpec(memory_space=pltpu.SMEM)
+    vmem = pl.BlockSpec(memory_space=pltpu.VMEM)
+    share = HALF_TOKENS // 2
+    return pl.pallas_call(
+        functools.partial(pick_kernel, shard_count),
+        out_shape=jax.ShapeDtypeStruct((CAP, 2, 2, share, stay[0].shape[2]), jnp.bfloat16),
+        in_specs=[smem, smem] + [vmem] * (2 * shard_count),
+        out_specs=vmem,
+        scratch_shapes=[pltpu.SMEM((CAP,), jnp.int32)],
+        name="pick_slots",
+    )(order, partner, *stay, *cross)
+
+
+def place_kernel(shard_count, order_ref, partner_ref, *refs):
+    stay, cross = refs[:shard_count], refs[shard_count : 2 * shard_count]
+    given_ref, out_ref, block_at, wide = refs[2 * shard_count :]
+    shard = lax.axis_index("ctx")
+    pair = lax.axis_index("pair")
+    core = lax.axis_index("tp")
+    share = HALF_TOKENS // 2
+    find_slots(order_ref, partner_ref, block_at, shard, shard_count)
+    for slot in range(CAP):
+        block = block_at[slot]
+        shift, place = locate(order_ref, jnp.maximum(block, 0), shard, shard_count)
+        begin = pl.multiple_of(place * HALF_TOKENS + core * share, share)
+        for kind in range(2):
+            base = (slot * 2 + kind) * share * 4
+            for which in range(2):
+                group = 2 * (pair if which == 0 else 1 - pair)
+                wide[pl.ds(base + group + 1 - core, share, stride=4), :] = given_ref[
+                    slot, kind, which
+                ].astype(jnp.float32)
+                for index in range(shard_count):
+
+                    @pl.when((block >= 0) & (shift == index))
+                    def _():
+                        rows = (stay, cross)[which][index][kind, pl.ds(begin, share), :]
+                        wide[pl.ds(base + group + core, share, stride=4), :] = rows.astype(
+                            jnp.float32
+                        )
+
+                @pl.when(block < 0)
+                def _():
+                    wide[pl.ds(base + group + core, share, stride=4), :] = jnp.zeros(
+                        (share, wide.shape[1]), jnp.float32
+                    )
+
+    out_ref[...] = wide[...].astype(jnp.bfloat16)
+
+
+def place(order, partner, stay, cross, given, shard_count):
+    smem = pl.BlockSpec(memory_space=pltpu.SMEM)
+    vmem = pl.BlockSpec(memory_space=pltpu.VMEM)
+    rows = CAP * 2 * (HALF_TOKENS // 2) * 4
+    width = stay[0].shape[2]
+    return pl.pallas_call(
+        functools.partial(place_kernel, shard_count),
+        out_shape=jax.ShapeDtypeStruct((rows, width), jnp.bfloat16),
+        in_specs=[smem, smem] + [vmem] * (2 * shard_count + 1),
+        out_specs=vmem,
+        scratch_shapes=[pltpu.SMEM((CAP,), jnp.int32), pltpu.VMEM((rows, width), jnp.float32)],
+        name="place_slots",
+    )(order, partner, *stay, *cross, given)
+
+
+def ring(array, step, count):
+    return lax.ppermute(array, "ctx", [(i, (i + step) % count) for i in range(count)])
+
+
+def swap(array, axis):
+    return lax.ppermute(array, axis, [(0, 1), (1, 0)])
+
+
+def pieces_program(queries, keys, values, span_order, lengths, kv_partner):
+    count = lax.axis_size("ctx")
+    query_rows, heads, width = queries.shape
+    partner = kv_partner[:, 0]
+    query = queries.reshape(query_rows * heads, width)
+    keys_flat = keys.reshape(-1, width)
+    values_flat = values.reshape(-1, width)
+    cross0, stay0 = split_heads(
+        keys_flat,
+        swap(keys, "tp").reshape(-1, width),
+        values_flat,
+        swap(values, "tp").reshape(-1, width),
+    )
+    cross3 = ring(cross0, 1, count)
+    cross1 = ring(cross0, -1, count)
+    stay3 = ring(stay0, 1, count)
+    cross2 = ring(cross3, 1, count)
+    stay1 = ring(stay0, -1, count)
+    stay2 = ring(stay1, -1, count)
+    over = [swap(piece, "pair") for piece in (cross0, cross1, cross2, cross3)]
+    state = None
+    steps = (
+        ((cross0, stay0), ((0, True), (0, False))),
+        ((cross1, cross3, stay3), ((1, True), (3, True), (3, False))),
+        ((cross2, stay1), ((2, True), (1, False))),
+        ((stay2,), ((2, False),)),
+    )
+    for number, (pieces, sources) in enumerate(steps):
+        last = number == len(steps) - 1
+        state = attend(span_order, lengths, query, pieces, sources, state, last, count, heads)
+    attended = state.reshape(queries.shape)
+    stay = (stay0, stay1, stay2, stay3)
+    given = swap(pick(span_order, partner, stay, over, count), "tp")
+    cache = place(span_order, partner, stay, over, given, count)
+    return attended, cache.reshape(CAP, 2, HALF_TOKENS // 2, 4, width)
+
+
+def pick_program(mesh):
+    sizes = mesh.shape
+    fits = sizes["ctx"] == 4 and sizes["pair"] == 2 and sizes["tp"] == 2
+    return pieces_program if fits else shards
+
+
 def solution(mesh):
     return jax.shard_map(
-        shards,
+        pick_program(mesh),
         mesh=mesh,
         in_specs=(
             P(("groups", "ctx"), ("pair", "tp"), None),

time: 130 us -> 60.6 us (0.47)
  the two profiles are of different devices: /device:TPU:0 before, /device:TPU:9 now
where the time goes in v1:
time: 60.6 us; the launch traced here: 60.3 us
  Pallas kernels  30.2 us (50%)
  starting transfers between devices  13.8 us (23%)
  waiting for transfers between devices  13.7 us (23%)
  local copies, waits for them, and re-layouts  2 us (3%)
  between operations  0.71 us (1%)
    pallas_call x4, Pallas kernels, attend(): pl.pallas_call(functools.partial(attend_kernel, sources, first, last, sha...  22.8 us
    ppermute x6, waiting for transfers between devices, ring(): lax.ppermute(array, 'ctx', [(i, (i + step) % count) for i in range(count)])  9.56 us
    ppermute x7, starting transfers between devices, swap(): return lax.ppermute(array, axis, [(0, 1), (1, 0)])  8.87 us
    ppermute x6, starting transfers between devices, ring(): lax.ppermute(array, 'ctx', [(i, (i + step) % count) for i in range(count)])  4.9 us
    ppermute x7, waiting for transfers between devices, swap(): return lax.ppermute(array, axis, [(0, 1), (1, 0)])  4.14 us
    pallas_call x1, Pallas kernels, place(): pl.pallas_call(functools.partial(place_kernel, shard_count), out_shape=ja...  3.06 us
    pallas_call x1, Pallas kernels, pick(): pl.pallas_call(functools.partial(pick_kernel, shard_count), out_shape=jax...  2.39 us
    unnamed x26, local copies, waits for them, and re-layouts  2 us
  transfers between devices with their start and end apart: 13, of which 9 were waited for; matrix products, arithmetic and copies ran while one was open for 0% of the time, Pallas kernels for 38%

profile of v1, /device:TPU:9, one launch (start us, length us, event | category | flops | bytes accessed | tf_op | source)
XLA Modules:
  0.0 60.3 jit_solution(12286973684404114807)
XLA Ops:
  0.6 0.7 %collective-permute-start = (bf16[256,2,128]{2,1,0:T(2,128)(2,1)}, bf16[256,2,128]{2,1,0:T(2,128)(2,1)S(1)}, u32[]{:S(2)}, u32[]{:S(2)}) collective-permute-start(bf16[256,2,128]{2,1,0:T(2,128)(2,1)} %param.7), channel_id=1, source_target_pairs={{0,1},{1,0},{2,3},{3,2},{4,5},{5,4},{6,7},{7,6},{8,9},{9,8},{10,11... | collective-permute-start | bytes 393224 | tf_op jit(solution)/shard_map/ppermute | solution.py:474
  1.4 1.1 %collective-permute-done = bf16[256,2,128]{2,1,0:T(2,128)(2,1)S(1)} collective-permute-done((bf16[256,2,128]{2,1,0:T(2,128)(2,1)}, bf16[256,2,128]{2,1,0:T(2,128)(2,1)S(1)}, u32[]{:S(2)}, u32[]{:S(2)}) %collective-permute-start) | collective-permute-done | bytes 131104 | tf_op jit(solution)/shard_map/ppermute | solution.py:474
  3.6 1.9 %split_heads.1 = (bf16[2,256,128]{2,1,0:T(8,128)(2,1)}, bf16[2,256,128]{2,1,0:T(8,128)(2,1)}) custom-call(bf16[512,128]{1,0:T(8,128)(2,1)} %bitcast.14, bf16[512,128]{1,0:T(8,128)(2,1)} %bitcast.16, bf16[512,128]{1,0:T(8,128)(2,1)} %bitcast.15, bf16[512,128]{1,0:T(8,128)(2,1)} %bitcast.17), custom_call_target="tpu_custom_call" | custom-call | tf_op jit(solution)/shard_map/split_heads/pallas_call | solution.py:209
  5.5 1.3 %collective-permute-start.4 = (bf16[2,256,128]{2,1,0:T(8,128)(2,1)}, bf16[2,256,128]{2,1,0:T(8,128)(2,1)S(1)}, u32[]{:S(2)}, u32[]{:S(2)}) collective-permute-start(bf16[2,256,128]{2,1,0:T(8,128)(2,1)} %get-tuple-element.14.refs_3_), channel_id=1, source_target_pairs={{0,4},{4,8},{8,12},{12,0},{1,5},{5,9},{9,13},{13,1},{2,6},{6,10},{... | collective-permute-start | bytes 393224 | tf_op jit(solution)/shard_map/ppermute | solution.py:470
  6.9 2.0 %collective-permute-start.6 = (bf16[2,256,128]{2,1,0:T(8,128)(2,1)}, bf16[2,256,128]{2,1,0:T(8,128)(2,1)S(1)}, u32[]{:S(2)}, u32[]{:S(2)}) collective-permute-start(bf16[2,256,128]{2,1,0:T(8,128)(2,1)} %get-tuple-element.14.refs_3_), channel_id=1, source_target_pairs={{0,12},{4,0},{8,4},{12,8},{1,13},{5,1},{9,5},{13,9},{2,14},{6,2},{... | collective-permute-start | bytes 393224 | tf_op jit(solution)/shard_map/ppermute | solution.py:470
  9.0 1.6 %collective-permute-done.4.refs_4_ = bf16[2,256,128]{2,1,0:T(8,128)(2,1)S(1)} collective-permute-done((bf16[2,256,128]{2,1,0:T(8,128)(2,1)}, bf16[2,256,128]{2,1,0:T(8,128)(2,1)S(1)}, u32[]{:S(2)}, u32[]{:S(2)}) %collective-permute-start.4) | collective-permute-done | bytes 131104 | tf_op jit(solution)/shard_map/ppermute | solution.py:470
  10.6 1.4 %collective-permute-start.5 = (bf16[2,256,128]{2,1,0:T(8,128)(2,1)S(1)}, bf16[2,256,128]{2,1,0:T(8,128)(2,1)S(1)}, u32[]{:S(2)}, u32[]{:S(2)}) collective-permute-start(bf16[2,256,128]{2,1,0:T(8,128)(2,1)S(1)} %collective-permute-done.4.refs_4_), channel_id=1, source_target_pairs={{0,4},{4,8},{8,12},{12,0},{1,5},{5,9},{9,13},{13,1},{2,6},{6,10},{... | collective-permute-start | bytes 393224 | tf_op jit(solution)/shard_map/ppermute | solution.py:470
  12.0 1.2 %collective-permute-start.8 = (bf16[2,256,128]{2,1,0:T(8,128)(2,1)}, bf16[2,256,128]{2,1,0:T(8,128)(2,1)S(1)}, u32[]{:S(2)}, u32[]{:S(2)}) collective-permute-start(bf16[2,256,128]{2,1,0:T(8,128)(2,1)} %get-tuple-element.14.refs_3_), channel_id=1, source_target_pairs={{0,2},{2,0},{1,3},{3,1},{4,6},{6,4},{5,7},{7,5},{8,10},{10,8},{9,1... | collective-permute-start | bytes 393224 | tf_op jit(solution)/shard_map/ppermute | solution.py:474
  13.2 1.5 %collective-permute-done.2.refs_4_.refs_1_ = bf16[2,256,128]{2,1,0:T(8,128)(2,1)S(1)} collective-permute-done((bf16[2,256,128]{2,1,0:T(8,128)(2,1)}, bf16[2,256,128]{2,1,0:T(8,128)(2,1)S(1)}, u32[]{:S(2)}, u32[]{:S(2)}) %collective-permute-start.2) | collective-permute-done | bytes 131104 | tf_op jit(solution)/shard_map/ppermute | solution.py:470
  14.8 1.2 %collective-permute-start.11 = (bf16[2,256,128]{2,1,0:T(8,128)(2,1)S(1)}, bf16[2,256,128]{2,1,0:T(8,128)(2,1)S(1)}, u32[]{:S(2)}, u32[]{:S(2)}) collective-permute-start(bf16[2,256,128]{2,1,0:T(8,128)(2,1)S(1)} %collective-permute-done.4.refs_4_), channel_id=1, source_target_pairs={{0,2},{2,0},{1,3},{3,1},{4,6},{6,4},{5,7},{7,5},{8,10},{10,8},{9,1... | collective-permute-start | bytes 393224 | tf_op jit(solution)/shard_map/ppermute | solution.py:474
  16.0 1.7 %collective-permute-done.6.refs_3_ = bf16[2,256,128]{2,1,0:T(8,128)(2,1)S(1)} collective-permute-done((bf16[2,256,128]{2,1,0:T(8,128)(2,1)}, bf16[2,256,128]{2,1,0:T(8,128)(2,1)S(1)}, u32[]{:S(2)}, u32[]{:S(2)}) %collective-permute-start.6) | collective-permute-done | bytes 131104 | tf_op jit(solution)/shard_map/ppermute | solution.py:470
  17.7 1.4 %collective-permute-done.7.refs_5_.refs_3_ = bf16[2,256,128]{2,1,0:T(8,128)(2,1)S(1)} collective-permute-done((bf16[2,256,128]{2,1,0:T(8,128)(2,1)}, bf16[2,256,128]{2,1,0:T(8,128)(2,1)S(1)}, u32[]{:S(2)}, u32[]{:S(2)}) %collective-permute-start.7) | collective-permute-done | bytes 131104 | tf_op jit(solution)/shard_map/ppermute | solution.py:470
  19.1 1.2 %collective-permute-start.9 = (bf16[2,256,128]{2,1,0:T(8,128)(2,1)S(1)}, bf16[2,256,128]{2,1,0:T(8,128)(2,1)S(1)}, u32[]{:S(2)}, u32[]{:S(2)}) collective-permute-start(bf16[2,256,128]{2,1,0:T(8,128)(2,1)S(1)} %collective-permute-done.6.refs_3_), channel_id=1, source_target_pairs={{0,2},{2,0},{1,3},{3,1},{4,6},{6,4},{5,7},{7,5},{8,10},{10,8},{9,1... | collective-permute-start | bytes 393224 | tf_op jit(solution)/shard_map/ppermute | solution.py:474
  20.3 1.6 %collective-permute-done.5.refs_3_ = bf16[2,256,128]{2,1,0:T(8,128)(2,1)S(1)} collective-permute-done((bf16[2,256,128]{2,1,0:T(8,128)(2,1)S(1)}, bf16[2,256,128]{2,1,0:T(8,128)(2,1)S(1)}, u32[]{:S(2)}, u32[]{:S(2)}) %collective-permute-start.5) | collective-permute-done | bytes 131104 | tf_op jit(solution)/shard_map/ppermute | solution.py:470
  21.9 1.2 %collective-permute-start.10 = (bf16[2,256,128]{2,1,0:T(8,128)(2,1)S(1)}, bf16[2,256,128]{2,1,0:T(8,128)(2,1)S(1)}, u32[]{:S(2)}, u32[]{:S(2)}) collective-permute-start(bf16[2,256,128]{2,1,0:T(8,128)(2,1)S(1)} %collective-permute-done.5.refs_3_), channel_id=1, source_target_pairs={{0,2},{2,0},{1,3},{3,1},{4,6},{6,4},{5,7},{7,5},{8,10},{10,8},{9,1... | collective-permute-start | bytes 393224 | tf_op jit(solution)/shard_map/ppermute | solution.py:474
  23.1 1.7 %collective-permute-done.3.refs_3_.refs_2_ = bf16[2,256,128]{2,1,0:T(8,128)(2,1)S(1)} collective-permute-done((bf16[2,256,128]{2,1,0:T(8,128)(2,1)S(1)}, bf16[2,256,128]{2,1,0:T(8,128)(2,1)S(1)}, u32[]{:S(2)}, u32[]{:S(2)}) %collective-permute-start.3) | collective-permute-done | bytes 131104 | tf_op jit(solution)/shard_map/ppermute | solution.py:470
  24.8 2.7 %collective-permute-done.10.refs_6_ = bf16[2,256,128]{2,1,0:T(8,128)(2,1)S(1)} collective-permute-done((bf16[2,256,128]{2,1,0:T(8,128)(2,1)S(1)}, bf16[2,256,128]{2,1,0:T(8,128)(2,1)S(1)}, u32[]{:S(2)}, u32[]{:S(2)}) %collective-permute-start.10) | collective-permute-done | bytes 131104 | tf_op jit(solution)/shard_map/ppermute | solution.py:474
  28.1 2.4 %pick_slots.1 = bf16[8,2,2,32,128]{4,3,2,1,0:T(8,128)(2,1)} custom-call(s32[4]{0:T(128)} %order_ref.3, s32[16]{0:T(128)} %bitcast.18, bf16[2,256,128]{2,1,0:T(8,128)(2,1)} %get-tuple-element.13.refs_4_.refs_0_, bf16[2,256,128]{2,1,0:T(8,128)(2,1)} %copy-done, bf16[2,256,128]{2,1,0:T(8,128)(2,1)} %copy-done.2, bf16[2,256,128]{2,1,0:T(8,128)(2,1)} %copy-done.1, ...), custom_call_target="tpu_custom_call" | custom-call | tf_op jit(solution)/shard_map/pick_slots/pallas_call | solution.py:407
  30.5 3.2 %collective-permute-start.12 = (bf16[8,2,2,32,128]{4,3,2,1,0:T(8,128)(2,1)}, bf16[8,2,2,32,128]{4,3,2,1,0:T(8,128)(2,1)S(1)}, u32[]{:S(2)}, u32[]{:S(2)}) collective-permute-start(bf16[8,2,2,32,128]{4,3,2,1,0:T(8,128)(2,1)} %pick_slots.1), channel_id=1, source_target_pairs={{0,1},{1,0},{2,3},{3,2},{4,5},{5,4},{6,7},{7,6},{8,9},{9,8},{10,11... | collective-permute-start | bytes 786440 | tf_op jit(solution)/shard_map/ppermute | solution.py:474
  33.7 7.5 %attend.4 = (f32[1,2048]{1,0:T(1,128)}, f32[1,2048]{1,0:T(1,128)}, f32[128,2048]{1,0:T(8,128)}) custom-call(s32[4]{0:T(128)} %order_ref.3, s32[4]{0:T(128)} %refs_1_.7, bf16[2048,128]{1,0:T(8,128)(2,1)} %bitcast.8, bf16[2,256,128]{2,1,0:T(8,128)(2,1)} %get-tuple-element.14.refs_3_, bf16[2,256,128]{2,1,0:T(8,128)(2,1)} %get-tuple-element.13.refs_4_.refs_0_), custom_call_target="tpu_custom_call" | custom-call | flops 268435456 | bytes 1048576 | tf_op jit(solution)/shard_map/attend/pallas_call | solution.py:338
  41.2 7.2 %attend.5 = (f32[1,2048]{1,0:T(1,128)}, f32[1,2048]{1,0:T(1,128)}, f32[128,2048]{1,0:T(8,128)}) custom-call(s32[4]{0:T(128)} %order_ref.3, s32[4]{0:T(128)} %refs_1_.7, bf16[2048,128]{1,0:T(8,128)(2,1)} %bitcast.9, bf16[2,256,128]{2,1,0:T(8,128)(2,1)} %copy-done.9, bf16[2,256,128]{2,1,0:T(8,128)(2,1)} %copy-done.8, bf16[2,256,128]{2,1,0:T(8,128)(2,1)} %copy-done.1, ...), custom_call_target="tpu_custom_call" | custom-call | flops 402653184 | bytes 1048576 | tf_op jit(solution)/shard_map/attend/pallas_call | solution.py:338
  48.4 4.5 %attend.6 = (f32[1,2048]{1,0:T(1,128)}, f32[1,2048]{1,0:T(1,128)}, f32[128,2048]{1,0:T(8,128)}) custom-call(s32[4]{0:T(128)} %order_ref.3, s32[4]{0:T(128)} %refs_1_.7, bf16[2048,128]{1,0:T(8,128)(2,1)} %bitcast.10, bf16[2,256,128]{2,1,0:T(8,128)(2,1)} %copy-done.10, bf16[2,256,128]{2,1,0:T(8,128)(2,1)} %copy-done, f32[1,2048]{1,0:T(1,128)} %get-tuple-element.18.refs_5_, ...), custom_call_target="tpu_custom_call" | custom-call | flops 268435456 | bytes 1048576 | tf_op jit(solution)/shard_map/attend/pallas_call | solution.py:338
  52.8 3.7 %attend.7 = bf16[2048,128]{1,0:T(8,128)(2,1)} custom-call(s32[4]{0:T(128)} %order_ref.3, s32[4]{0:T(128)} %refs_1_.7, bf16[2048,128]{1,0:T(8,128)(2,1)} %bitcast.11, bf16[2,256,128]{2,1,0:T(8,128)(2,1)} %copy-done.2, f32[1,2048]{1,0:T(1,128)} %get-tuple-element.21.refs_4_, f32[1,2048]{1,0:T(1,128)} %get-tuple-element.22.refs_5_, ...), custom_call_target="tpu_custom_call" | custom-call | flops 134217728 | bytes 1048576 | tf_op jit(solution)/shard_map/attend/pallas_call | solution.py:338
  57.3 3.1 %place_slots.1 = bf16[2048,128]{1,0:T(8,128)(2,1)} custom-call(s32[4]{0:T(128)} %order_ref.3, s32[16]{0:T(128)} %bitcast.19, bf16[2,256,128]{2,1,0:T(8,128)(2,1)} %get-tuple-element.13.refs_4_.refs_0_, bf16[2,256,128]{2,1,0:T(8,128)(2,1)} %copy-done, bf16[2,256,128]{2,1,0:T(8,128)(2,1)} %copy-done.2, bf16[2,256,128]{2,1,0:T(8,128)(2,1)} %copy-done.1, ...), custom_call_target="tpu_custom_call" | custom-call | tf_op jit(solution)/shard_map/place_slots/pallas_call | solution.py:459
  (35 shorter events, 2.6 us)
Async XLA Ops:
  0.6 1.9 %collective-permute-start = (bf16[256,2,128]{2,1,0:T(2,128)(2,1)}, bf16[256,2,128]{2,1,0:T(2,128)(2,1)S(1)}, u32[]{:S(2)}, u32[]{:S(2)}) collective-permute-start(bf16[256,2,128]{2,1,0:T(2,128)(2,1)} %param.7), channel_id=1, source_target_pairs={{0,1},{1,0},{2,3},{3,2},{4,5},{5,4},{6,7},{7,6},{8,9},{9,8},{10,11... | collective-permute-start | bytes 393224 | tf_op jit(solution)/shard_map/ppermute | solution.py:474
  1.4 1.6 %collective-permute-start.1 = (bf16[256,2,128]{2,1,0:T(2,128)(2,1)}, bf16[256,2,128]{2,1,0:T(2,128)(2,1)S(1)}, u32[]{:S(2)}, u32[]{:S(2)}) collective-permute-start(bf16[256,2,128]{2,1,0:T(2,128)(2,1)} %param.8), channel_id=1, source_target_pairs={{0,1},{1,0},{2,3},{3,2},{4,5},{5,4},{6,7},{7,6},{8,9},{9,8},{10,11... | collective-permute-start | bytes 393224 | tf_op jit(solution)/shard_map/ppermute | solution.py:474
  2.9 0.7 %copy-start.12 = (bf16[256,2,128]{2,1,0:T(2,128)(2,1)}, bf16[256,2,128]{2,1,0:T(2,128)(2,1)S(1)}, u32[]{:S(2)}) copy-start(bf16[256,2,128]{2,1,0:T(2,128)(2,1)S(1)} %collective-permute-done.1) | copy-start | bytes 393220
  5.5 5.1 %collective-permute-start.4 = (bf16[2,256,128]{2,1,0:T(8,128)(2,1)}, bf16[2,256,128]{2,1,0:T(8,128)(2,1)S(1)}, u32[]{:S(2)}, u32[]{:S(2)}) collective-permute-start(bf16[2,256,128]{2,1,0:T(8,128)(2,1)} %get-tuple-element.14.refs_3_), channel_id=1, source_target_pairs={{0,4},{4,8},{8,12},{12,0},{1,5},{5,9},{9,13},{13,1},{2,6},{6,10},{... | collective-permute-start | bytes 393224 | tf_op jit(solution)/shard_map/ppermute | solution.py:470
  6.8 8.0 %collective-permute-start.2 = (bf16[2,256,128]{2,1,0:T(8,128)(2,1)}, bf16[2,256,128]{2,1,0:T(8,128)(2,1)S(1)}, u32[]{:S(2)}, u32[]{:S(2)}) collective-permute-start(bf16[2,256,128]{2,1,0:T(8,128)(2,1)} %get-tuple-element.13.refs_4_.refs_0_), channel_id=1, source_target_pairs={{0,12},{4,0},{8,4},{12,8},{1,13},{5,1},{9,5},{13,9},{2,14},{6,2},{... | collective-permute-start | bytes 393224 | tf_op jit(solution)/shard_map/ppermute | solution.py:470
  6.9 10.8 %collective-permute-start.6 = (bf16[2,256,128]{2,1,0:T(8,128)(2,1)}, bf16[2,256,128]{2,1,0:T(8,128)(2,1)S(1)}, u32[]{:S(2)}, u32[]{:S(2)}) collective-permute-start(bf16[2,256,128]{2,1,0:T(8,128)(2,1)} %get-tuple-element.14.refs_3_), channel_id=1, source_target_pairs={{0,12},{4,0},{8,4},{12,8},{1,13},{5,1},{9,5},{13,9},{2,14},{6,2},{... | collective-permute-start | bytes 393224 | tf_op jit(solution)/shard_map/ppermute | solution.py:470
  9.0 10.1 %collective-permute-start.7 = (bf16[2,256,128]{2,1,0:T(8,128)(2,1)}, bf16[2,256,128]{2,1,0:T(8,128)(2,1)S(1)}, u32[]{:S(2)}, u32[]{:S(2)}) collective-permute-start(bf16[2,256,128]{2,1,0:T(8,128)(2,1)} %get-tuple-element.13.refs_4_.refs_0_), channel_id=1, source_target_pairs={{0,4},{4,8},{8,12},{12,0},{1,5},{5,9},{9,13},{13,1},{2,6},{6,10},{... | collective-permute-start | bytes 393224 | tf_op jit(solution)/shard_map/ppermute | solution.py:470
  10.6 19.9 %copy-start.8 = (bf16[2,256,128]{2,1,0:T(8,128)(2,1)}, bf16[2,256,128]{2,1,0:T(8,128)(2,1)S(1)}, u32[]{:S(2)}) copy-start(bf16[2,256,128]{2,1,0:T(8,128)(2,1)S(1)} %collective-permute-done.4.refs_4_) | copy-start | bytes 393220
  10.6 11.3 %collective-permute-start.5 = (bf16[2,256,128]{2,1,0:T(8,128)(2,1)S(1)}, bf16[2,256,128]{2,1,0:T(8,128)(2,1)S(1)}, u32[]{:S(2)}, u32[]{:S(2)}) collective-permute-start(bf16[2,256,128]{2,1,0:T(8,128)(2,1)S(1)} %collective-permute-done.4.refs_4_), channel_id=1, source_target_pairs={{0,4},{4,8},{8,12},{12,0},{1,5},{5,9},{9,13},{13,1},{2,6},{6,10},{... | collective-permute-start | bytes 393224 | tf_op jit(solution)/shard_map/ppermute | solution.py:470
  12.0 11.1 %collective-permute-start.8 = (bf16[2,256,128]{2,1,0:T(8,128)(2,1)}, bf16[2,256,128]{2,1,0:T(8,128)(2,1)S(1)}, u32[]{:S(2)}, u32[]{:S(2)}) collective-permute-start(bf16[2,256,128]{2,1,0:T(8,128)(2,1)} %get-tuple-element.14.refs_3_), channel_id=1, source_target_pairs={{0,2},{2,0},{1,3},{3,1},{4,6},{6,4},{5,7},{7,5},{8,10},{10,8},{9,1... | collective-permute-start | bytes 393224 | tf_op jit(solution)/shard_map/ppermute | solution.py:474
  14.8 12.7 %copy-start = (bf16[2,256,128]{2,1,0:T(8,128)(2,1)}, bf16[2,256,128]{2,1,0:T(8,128)(2,1)S(1)}, u32[]{:S(2)}) copy-start(bf16[2,256,128]{2,1,0:T(8,128)(2,1)S(1)} %collective-permute-done.2.refs_4_.refs_1_) | copy-start | bytes 393220
  14.8 10.0 %collective-permute-start.11 = (bf16[2,256,128]{2,1,0:T(8,128)(2,1)S(1)}, bf16[2,256,128]{2,1,0:T(8,128)(2,1)S(1)}, u32[]{:S(2)}, u32[]{:S(2)}) collective-permute-start(bf16[2,256,128]{2,1,0:T(8,128)(2,1)S(1)} %collective-permute-done.4.refs_4_), channel_id=1, source_target_pairs={{0,2},{2,0},{1,3},{3,1},{4,6},{6,4},{5,7},{7,5},{8,10},{10,8},{9,1... | collective-permute-start | bytes 393224 | tf_op jit(solution)/shard_map/ppermute | solution.py:474
  17.7 12.8 %copy-start.9 = (bf16[2,256,128]{2,1,0:T(8,128)(2,1)}, bf16[2,256,128]{2,1,0:T(8,128)(2,1)S(1)}, u32[]{:S(2)}) copy-start(bf16[2,256,128]{2,1,0:T(8,128)(2,1)S(1)} %collective-permute-done.6.refs_3_) | copy-start | bytes 393220
  17.7 7.1 %collective-permute-start.3 = (bf16[2,256,128]{2,1,0:T(8,128)(2,1)S(1)}, bf16[2,256,128]{2,1,0:T(8,128)(2,1)S(1)}, u32[]{:S(2)}, u32[]{:S(2)}) collective-permute-start(bf16[2,256,128]{2,1,0:T(8,128)(2,1)S(1)} %collective-permute-done.2.refs_4_.refs_1_), channel_id=1, source_target_pairs={{0,12},{4,0},{8,4},{12,8},{1,13},{5,1},{9,5},{13,9},{2,14},{6,2},{... | collective-permute-start | bytes 393224 | tf_op jit(solution)/shard_map/ppermute | solution.py:470
  19.1 8.4 %copy-start.1 = (bf16[2,256,128]{2,1,0:T(8,128)(2,1)}, bf16[2,256,128]{2,1,0:T(8,128)(2,1)S(1)}, u32[]{:S(2)}) copy-start(bf16[2,256,128]{2,1,0:T(8,128)(2,1)S(1)} %collective-permute-done.7.refs_5_.refs_3_) | copy-start | bytes 393220
  19.1 5.7 %collective-permute-start.9 = (bf16[2,256,128]{2,1,0:T(8,128)(2,1)S(1)}, bf16[2,256,128]{2,1,0:T(8,128)(2,1)S(1)}, u32[]{:S(2)}, u32[]{:S(2)}) collective-permute-start(bf16[2,256,128]{2,1,0:T(8,128)(2,1)S(1)} %collective-permute-done.6.refs_3_), channel_id=1, source_target_pairs={{0,2},{2,0},{1,3},{3,1},{4,6},{6,4},{5,7},{7,5},{8,10},{10,8},{9,1... | collective-permute-start | bytes 393224 | tf_op jit(solution)/shard_map/ppermute | solution.py:474
  21.9 8.6 %copy-start.10 = (bf16[2,256,128]{2,1,0:T(8,128)(2,1)}, bf16[2,256,128]{2,1,0:T(8,128)(2,1)S(1)}, u32[]{:S(2)}) copy-start(bf16[2,256,128]{2,1,0:T(8,128)(2,1)S(1)} %collective-permute-done.5.refs_3_) | copy-start | bytes 393220
  21.9 5.6 %collective-permute-start.10 = (bf16[2,256,128]{2,1,0:T(8,128)(2,1)S(1)}, bf16[2,256,128]{2,1,0:T(8,128)(2,1)S(1)}, u32[]{:S(2)}, u32[]{:S(2)}) collective-permute-start(bf16[2,256,128]{2,1,0:T(8,128)(2,1)S(1)} %collective-permute-done.5.refs_3_), channel_id=1, source_target_pairs={{0,2},{2,0},{1,3},{3,1},{4,6},{6,4},{5,7},{7,5},{8,10},{10,8},{9,1... | collective-permute-start | bytes 393224 | tf_op jit(solution)/shard_map/ppermute | solution.py:474
  23.1 4.4 %copy-start.3 = (bf16[2,256,128]{2,1,0:T(8,128)(2,1)}, bf16[2,256,128]{2,1,0:T(8,128)(2,1)S(1)}, u32[]{:S(2)}) copy-start(bf16[2,256,128]{2,1,0:T(8,128)(2,1)S(1)} %collective-permute-done.8.refs_4_) | copy-start | bytes 393220
  24.8 2.7 %copy-start.2 = (bf16[2,256,128]{2,1,0:T(8,128)(2,1)}, bf16[2,256,128]{2,1,0:T(8,128)(2,1)S(1)}, u32[]{:S(2)}) copy-start(bf16[2,256,128]{2,1,0:T(8,128)(2,1)S(1)} %collective-permute-done.3.refs_3_.refs_2_) | copy-start | bytes 393220
  24.8 2.7 %copy-start.5 = (bf16[2,256,128]{2,1,0:T(8,128)(2,1)}, bf16[2,256,128]{2,1,0:T(8,128)(2,1)S(1)}, u32[]{:S(2)}) copy-start(bf16[2,256,128]{2,1,0:T(8,128)(2,1)S(1)} %collective-permute-done.9.refs_5_) | copy-start | bytes 393220
  24.8 2.7 %copy-start.4 = (bf16[2,256,128]{2,1,0:T(8,128)(2,1)}, bf16[2,256,128]{2,1,0:T(8,128)(2,1)S(1)}, u32[]{:S(2)}) copy-start(bf16[2,256,128]{2,1,0:T(8,128)(2,1)S(1)} %collective-permute-done.11.refs_7_) | copy-start | bytes 393220
  30.5 26.0 %collective-permute-start.12 = (bf16[8,2,2,32,128]{4,3,2,1,0:T(8,128)(2,1)}, bf16[8,2,2,32,128]{4,3,2,1,0:T(8,128)(2,1)S(1)}, u32[]{:S(2)}, u32[]{:S(2)}) collective-permute-start(bf16[8,2,2,32,128]{4,3,2,1,0:T(8,128)(2,1)} %pick_slots.1), channel_id=1, source_target_pairs={{0,1},{1,0},{2,3},{3,2},{4,5},{5,4},{6,7},{7,6},{8,9},{9,8},{10,11... | collective-permute-start | bytes 786440 | tf_op jit(solution)/shard_map/ppermute | solution.py:474
  56.6 0.7 %copy-start.7 = (bf16[8,2,2,32,128]{4,3,2,1,0:T(8,128)(2,1)}, bf16[8,2,2,32,128]{4,3,2,1,0:T(8,128)(2,1)S(1)}, u32[]{:S(2)}) copy-start(bf16[8,2,2,32,128]{4,3,2,1,0:T(8,128)(2,1)S(1)} %collective-permute-done.12.refs_8_) | copy-start | bytes 786436
  (2 other events, 1.3 us)

commit v2 on v0

--- a/solution.py
+++ b/solution.py
@@ -1,6 +1,10 @@
+import functools
+
 import jax
 import jax.numpy as jnp
 from jax import lax
+from jax.experimental import pallas as pl
+from jax.experimental.pallas import tpu as pltpu
 from jax.sharding import PartitionSpec as P
 
 GROUP = 4
@@ -173,9 +177,382 @@
     return (attended, decode_cache)
 
 
+HALF_TOKENS = BLK // 2
+LOG2E = 1.4426950408889634
+MASKED = -1e30
+FLOOR = -1e29
+COST_FLOPS = 4 * 10**9
+Q_TILE = 1024
+STRIP = 64
+
+
+def split_kernel(key_a, key_b, value_a, value_b, cross_ref, stay_ref, wide):
+    pair = lax.axis_index("pair")
+    core = lax.axis_index("tp")
+    for kind, (own, other) in enumerate(((key_a, key_b), (value_a, value_b))):
+        wide[kind, core] = own[...].astype(jnp.float32)
+        wide[kind, 1 - core] = other[...].astype(jnp.float32)
+    for kind in range(2):
+        for block in range(4):
+            at = pl.ds(block * HALF_TOKENS, HALF_TOKENS)
+            for out, part in ((cross_ref, 1 - pair), (stay_ref, pair)):
+                first = (block % 2) * 2 * BLK + part * 2 * HALF_TOKENS + core
+                rows = wide[kind, block // 2, pl.ds(first, HALF_TOKENS, stride=2), :]
+                rows = rows.astype(jnp.bfloat16)
+                out[kind, at, :] = rows
+
+
+def split_heads(keys, keys_other, values, values_other):
+    rows, width = keys.shape
+    piece = jax.ShapeDtypeStruct((2, rows // 2, width), jnp.bfloat16)
+    return pl.pallas_call(
+        split_kernel,
+        out_shape=(piece, piece),
+        scratch_shapes=[pltpu.VMEM((2, 2, rows, width), jnp.float32)],
+        name="split_heads",
+    )(keys, keys_other, values, values_other)
+
+
+def attend_kernel(sources, first, last, span_total, heads, *refs):
+    order_ref, lengths_ref, query_ref = refs[:3]
+    refs = refs[3:]
+    pieces = []
+    for _ in sources:
+        pieces.append((refs[0], refs[1]))
+        refs = refs[2:]
+    if not first:
+        peak_in, total_in, summed_in = refs[:3]
+        refs = refs[3:]
+    if last:
+        out_ref, refs = refs[0], refs[1:]
+    else:
+        peak_out, total_out, summed_out = refs[:3]
+        refs = refs[3:]
+    score_ref, weights_ref, values_ref, top_ref, total_ref, summed_ref = refs
+    shard = lax.axis_index("ctx")
+    pair = lax.axis_index("pair")
+    rows, width = query_ref.shape
+    half_rows = rows // heads // 2
+    factor = LOG2E * width**-0.5
+    starts = [jnp.int32(0)]
+    for r in range(lengths_ref.shape[0] - 1):
+        starts.append(starts[-1] + lengths_ref[r])
+
+    def begin_of(position):
+        begin = jnp.zeros_like(position)
+        for start in starts[1:]:
+            begin = jnp.where(start <= position, start, begin)
+        return begin
+
+    spans = []
+    for shift, (cross, stay) in zip(sources, pieces):
+        lead = order_ref[lax.rem(shard + shift, span_total // 2)]
+        spans.append((lead, cross, stay, 0))
+        spans.append((span_total - 1 - lead, cross, stay, 1))
+    part_keys = pieces[0][0].shape[1] // 2
+    keys_each = 2 * part_keys
+    for number, (_, cross, stay, half) in enumerate(spans):
+        for which, piece in enumerate((cross, stay)):
+            values_ref[number, pl.ds(which * part_keys, part_keys), :] = piece[
+                1, pl.ds(half * part_keys, part_keys), :
+            ]
+    lane = lax.broadcasted_iota(jnp.int32, (1, keys_each), 1)
+    in_part = lax.rem(lane, part_keys)
+    local = (
+        in_part
+        + jnp.where(in_part >= HALF_TOKENS, BLK - HALF_TOKENS, 0)
+        + HALF_TOKENS * jnp.where(lane < part_keys, 1 - pair, pair)
+    )
+
+    tile_tokens = Q_TILE // heads
+    tiles_half = half_rows // tile_tokens
+
+    def tile(index, _):
+        at = pl.ds(pl.multiple_of(index * Q_TILE, Q_TILE), Q_TILE)
+        own_lead = order_ref[shard]
+        query_span = jnp.where(index < tiles_half, own_lead, span_total - 1 - own_lead)
+        first_pos = query_span * half_rows + lax.rem(index, tiles_half) * tile_tokens
+        begin_low = begin_of(first_pos)
+        near = []
+        for span, _, _, _ in spans:
+            near.append(
+                (span * half_rows <= first_pos + tile_tokens - 1)
+                & (span * half_rows + half_rows - 1 >= begin_low)
+            )
+        if first:
+            top_ref[...] = jnp.full(top_ref.shape, FLOOR, jnp.float32)
+        else:
+            top_ref[...] = peak_in[at, :]
+
+        for number, (span, cross, stay, half) in enumerate(spans):
+
+            @pl.when(near[number])
+            def _():
+                part = pl.ds(half * part_keys, part_keys)
+                score_ref[number] = lax.dot_general(
+                    query_ref[at, :],
+                    jnp.concatenate([cross[0, part, :], stay[0, part, :]], axis=0),
+                    (((1,), (1,)), ((), ())),
+                    preferred_element_type=jnp.float32,
+                )
+                key_pos = span * half_rows + local
+                for row in range(0, Q_TILE, STRIP):
+                    strip = pl.ds(row, STRIP)
+                    index_in = lax.broadcasted_iota(jnp.int32, (STRIP, width), 0)
+                    query_pos = first_pos + row // heads + index_in // heads
+                    query_begin = begin_of(query_pos)
+                    top = top_ref[strip, :]
+                    for column in range(0, keys_each, width):
+                        at_key = key_pos[:, column : column + width]
+                        visible = (at_key <= query_pos) & (at_key >= query_begin)
+                        score = score_ref[number, strip, column : column + width]
+                        score = jnp.where(visible, score, MASKED)
+                        score_ref[number, strip, column : column + width] = score
+                        top = jnp.maximum(top, score)
+                    top_ref[strip, :] = top
+
+        for row in range(0, Q_TILE, STRIP):
+            strip = pl.ds(row, STRIP)
+            peak = jnp.max(top_ref[strip, :], axis=1, keepdims=True)
+            peak = jnp.broadcast_to(peak, (STRIP, width))
+            top_ref[strip, :] = peak
+            rows_at = pl.ds(pl.multiple_of(index * Q_TILE + row, STRIP), STRIP)
+            if first:
+                total_ref[strip, :] = jnp.zeros((STRIP, width), jnp.float32)
+                summed_ref[strip, :] = jnp.zeros((STRIP, width), jnp.float32)
+            else:
+                fade = jnp.exp2((peak_in[rows_at, :] - peak) * factor)
+                total_ref[strip, :] = total_in[rows_at, :] * fade
+                summed_ref[strip, :] = summed_in[rows_at, :] * fade
+            if not last:
+                peak_out[rows_at, :] = peak
+        for number in range(len(spans)):
+
+            @pl.when(near[number])
+            def _():
+                for row in range(0, Q_TILE, STRIP):
+                    strip = pl.ds(row, STRIP)
+                    peak = top_ref[strip, :]
+                    total = total_ref[strip, :]
+                    for column in range(0, keys_each, width):
+                        score = score_ref[number, strip, column : column + width]
+                        weight = jnp.exp2((score - peak) * factor)
+                        total = total + weight
+                        weights_ref[strip, column : column + width] = weight.astype(jnp.bfloat16)
+                    total_ref[strip, :] = total
+                summed_ref[...] += jnp.dot(
+                    weights_ref[...], values_ref[number], preferred_element_type=jnp.float32
+                )
+
+        if last:
+            total = jnp.sum(total_ref[...], axis=1, keepdims=True)
+            out_ref[at, :] = (summed_ref[...] / total).astype(jnp.bfloat16)
+        else:
+            total_out[at, :] = total_ref[...]
+            summed_out[at, :] = summed_ref[...]
+        return 0
+
+    lax.fori_loop(0, rows // Q_TILE, tile, 0)
+
+
+def attend(order, lengths, query, pieces, sources, state, last, heads):
+    rows, width = query.shape
+    first = state is None
+    smem = pl.BlockSpec(memory_space=pltpu.SMEM)
+    vmem = pl.BlockSpec(memory_space=pltpu.VMEM)
+    state = () if first else state
+    if last:
+        out_shape = jax.ShapeDtypeStruct((rows, width), jnp.bfloat16)
+        out_specs = vmem
+    else:
+        out_shape = (jax.ShapeDtypeStruct((rows, width), jnp.float32),) * 3
+        out_specs = (vmem,) * 3
+    keys_each = pieces[0].shape[-2]
+    count = 2 * len(sources)
+    tile = pltpu.VMEM((Q_TILE, width), jnp.float32)
+    return pl.pallas_call(
+        functools.partial(attend_kernel, sources, first, last, 2 * order.shape[0], heads),
+        out_shape=out_shape,
+        in_specs=[smem, smem] + [vmem] * (1 + len(pieces) + len(state)),
+        out_specs=out_specs,
+        scratch_shapes=[
+            pltpu.VMEM((count, Q_TILE, keys_each), jnp.float32),
+            pltpu.VMEM((Q_TILE, keys_each), jnp.bfloat16),
+            pltpu.VMEM((count, keys_each, width), jnp.bfloat16),
+            tile,
+            tile,
+            tile,
+        ],
+        cost_estimate=pl.CostEstimate(
+            flops=COST_FLOPS, bytes_accessed=4 * rows * width, transcendentals=0
+        ),
+        name="attend",
+    )(order, lengths, query, *pieces, *state)
+
+
+def locate_slots(order_ref, partner_ref, found, shard, shard_count):
+    for slot in range(CAP):
+        found[0, slot] = -1
+    for index in range(shard_count):
+        lead = order_ref[index]
+        shift = lax.rem(index - shard + shard_count, shard_count)
+        found[1, lead] = shift
+        found[2, lead] = 0
+        found[1, 2 * shard_count - 1 - lead] = shift
+        found[2, 2 * shard_count - 1 - lead] = 1
+    taken = jnp.int32(0)
+    for block in range(partner_ref.shape[0]):
+        mine = partner_ref[block] == shard
+
+        @pl.when(mine)
+        def _():
+            found[0, taken] = block
+
+        taken = taken + mine.astype(jnp.int32)
+
+
+def slot_place(found, slot):
+    block = found[0, slot]
+    span = jnp.maximum(block, 0) // 2
+    place = found[2, span] * 2 + lax.rem(jnp.maximum(block, 0), 2)
+    return block >= 0, found[1, span], place * HALF_TOKENS
+
+
+def gather_pieces(pieces, count, held):
+    for index, piece in enumerate(pieces):
+        held[index // count, index % count] = piece[...]
+
+
+def pick_kernel(order_ref, partner_ref, *refs):
+    count = order_ref.shape[0]
+    out_ref, found, held = refs[2 * count :]
+    shard = lax.axis_index("ctx")
+    core = lax.axis_index("tp")
+    share = HALF_TOKENS // 2
+    gather_pieces(refs[: 2 * count], count, held)
+    locate_slots(order_ref, partner_ref, found, shard, count)
+    for slot in range(CAP):
+        live, index, start = slot_place(found, slot)
+        begin = pl.ds(pl.multiple_of(start + (1 - core) * share, share), share)
+        for which in range(2):
+            for kind in range(2):
+                out_ref[slot, kind, which] = held[which, index, kind, begin, :]
+
+
+def slot_call(kernel, out_shape, scratch, name, operands, piece_shape):
+    smem = pl.BlockSpec(memory_space=pltpu.SMEM)
+    vmem = pl.BlockSpec(memory_space=pltpu.VMEM)
+    count = operands[0].shape[0]
+    return pl.pallas_call(
+        kernel,
+        out_shape=out_shape,
+        in_specs=[smem, smem] + [vmem] * (len(operands) - 2),
+        out_specs=vmem,
+        scratch_shapes=[
+            pltpu.SMEM((3, max(CAP, 2 * count)), jnp.int32),
+            pltpu.VMEM((2, count) + piece_shape, jnp.bfloat16),
+        ]
+        + scratch,
+        name=name,
+    )(*operands)
+
+
+def pick(order, partner, stay, cross):
+    piece_shape = cross[0].shape
+    out_shape = jax.ShapeDtypeStruct((CAP, 2, 2, HALF_TOKENS // 2, piece_shape[2]), jnp.bfloat16)
+    operands = (order, partner, *stay, *cross)
+    return slot_call(pick_kernel, out_shape, [], "pick_slots", operands, piece_shape)
+
+
+def place_kernel(order_ref, partner_ref, *refs):
+    count = order_ref.shape[0]
+    given_ref, out_ref, found, held, wide = refs[2 * count :]
+    shard = lax.axis_index("ctx")
+    pair = lax.axis_index("pair")
+    core = lax.axis_index("tp")
+    share = HALF_TOKENS // 2
+    gather_pieces(refs[: 2 * count], count, held)
+    locate_slots(order_ref, partner_ref, found, shard, count)
+    for slot in range(CAP):
+        live, index, start = slot_place(found, slot)
+        begin = pl.ds(pl.multiple_of(start + core * share, share), share)
+        for which in range(2):
+            group = 2 * (pair if which == 0 else 1 - pair)
+            for kind in range(2):
+                base = (slot * 2 + kind) * share * 4 + group
+                kept = held[which, index, kind, begin, :].astype(jnp.float32)
+                given = given_ref[slot, kind, which].astype(jnp.float32)
+                wide[pl.ds(base + core, share, stride=4), :] = jnp.where(live, kept, 0.0)
+                wide[pl.ds(base + 1 - core, share, stride=4), :] = jnp.where(live, given, 0.0)
+    out_ref[...] = wide[...].astype(jnp.bfloat16)
+
+
+def place(order, partner, stay, cross, given):
+    piece_shape = cross[0].shape
+    rows = CAP * 2 * (HALF_TOKENS // 2) * 4
+    out_shape = jax.ShapeDtypeStruct((rows, piece_shape[2]), jnp.bfloat16)
+    scratch = [pltpu.VMEM((rows, piece_shape[2]), jnp.float32)]
+    operands = (order, partner, *stay, *cross, given)
+    return slot_call(place_kernel, out_shape, scratch, "place_slots", operands, piece_shape)
+
+
+def ring(array, step, count):
+    return lax.ppermute(array, "ctx", [(i, (i + step) % count) for i in range(count)])
+
+
+def swap(array, axis):
+    return lax.ppermute(array, axis, [(0, 1), (1, 0)])
+
+
+def after(value, earlier):
+    return lax.optimization_barrier((value, earlier))
+
+
+def pieces_program(queries, keys, values, span_order, lengths, kv_partner):
+    count = lax.axis_size("ctx")
+    query_rows, heads, width = queries.shape
+    partner = kv_partner[:, 0]
+    query = queries.reshape(query_rows * heads, width)
+    cross0, stay0 = split_heads(
+        keys.reshape(-1, width),
+        swap(keys, "tp").reshape(-1, width),
+        values.reshape(-1, width),
+        swap(values, "tp").reshape(-1, width),
+    )
+
+    def step(pieces, sources, state, last=False):
+        return attend(span_order, lengths, query, pieces, sources, state, last, heads)
+
+    cross3 = ring(cross0, 1, count)
+    cross1 = ring(cross0, -1, count)
+    stay1 = ring(stay0, -1, count)
+    stay3 = ring(stay0, 1, count)
+    over0 = swap(cross0, "pair")
+    cross2 = ring(cross3, 1, count)
+    over3 = swap(cross3, "pair")
+    over1 = swap(cross1, "pair")
+    stay2 = ring(stay3, 1, count)
+    stay0_late, stay3 = after(stay0, stay3)
+    state = step((cross0, stay0_late, cross1, stay1), (0, 1), None)
+    over2 = swap(cross2, "pair")
+    attended = step((cross3, stay3, cross2, stay2), (3, 2), state, True)
+    over2, attended = after(over2, attended)
+    stay = (stay0, stay1, stay2, stay3)
+    over = (over0, over1, over2, over3)
+    given = swap(pick(span_order, partner, stay, over), "tp")
+    cache = place(span_order, partner, stay, over, given)
+    return attended.reshape(queries.shape), cache.reshape(CAP, 2, HALF_TOKENS // 2, 4, width)
+
+
+def pick_program(mesh):
+    sizes = mesh.shape
+    fits = sizes["ctx"] == 4 and sizes["pair"] == 2 and sizes["tp"] == 2
+    return pieces_program if fits else shards
+
+
 def solution(mesh):
     return jax.shard_map(
-        shards,
+        pick_program(mesh),
         mesh=mesh,
         in_specs=(
             P(("groups", "ctx"), ("pair", "tp"), None),

time: 130 us -> 45.8 us (0.35)
  waiting for transfers between devices: 40.6 us -> 6.11 us
  local copies, waits for them, and re-layouts: 29.2 us -> 2.74 us
  matrix products: 19.9 us -> 0 us
  other arithmetic: 19.8 us -> 0 us
  Pallas kernels: 0 us -> 18.1 us
  starting transfers between devices: 3.56 us -> 17.8 us
  between operations: 14.2 us -> 0.72 us
  loops' own time: 1.6 us -> 0 us
    all_gather x2 -> x0, waiting for transfers between devices: 39.3 us -> none  [the longest x1 20.8 us: shards(): lax.all_gather(values, ('ctx', 'tp'), axis=0, tiled=True)]
    dot_general x4 -> x0, matrix products: 19.9 us -> none  [the longest x2 14.3 us: update(): jnp.einsum('rhn,nhd->rhd', weights.astype(jnp.bfloat16), head_values, pre...]
    pallas_call x0 -> x5, Pallas kernels: none -> 18.1 us  [the longest x2 11.5 us: attend(): pl.pallas_call(functools.partial(attend_kernel, sources, first, last, 2 *...]
    ppermute x0 -> x13, starting transfers between devices: none -> 17.8 us  [the longest x6 11.9 us: ring(): lax.ppermute(array, 'ctx', [(i, (i + step) % count) for i in range(count)])]
    gather x6 -> x0, local copies, waits for them, and re-layouts: 8.14 us -> none  [the longest x1 2.57 us: absorb(): jnp.take(piece_keys, safe, axis=0)]
    reduce_sum x11 -> x0, other arithmetic: 7.11 us -> none  [the longest x2 4.18 us: update(): new_total = total * factor + jnp.sum(weights, axis=2)]
    cond x6 -> x0, local copies, waits for them, and re-layouts: 6.4 us -> none
    ppermute x0 -> x13, waiting for transfers between devices: none -> 6.11 us  [the longest x7 3.23 us: swap(): return lax.ppermute(array, axis, [(0, 1), (1, 0)])]
  transfers between devices with their start and end apart: 3 -> 13, of which waited for: 2 -> 5; matrix products, arithmetic and copies ran while one was open for 43% -> 0% of each run, Pallas kernels for 0% -> 25%
where the time goes in v2:
time: 45.8 us; the launch traced here: 45.5 us
  Pallas kernels  18.1 us (40%)
  starting transfers between devices  17.8 us (39%)
  waiting for transfers between devices  6.11 us (13%)
  local copies, waits for them, and re-layouts  2.74 us (6%)
  between operations  0.72 us (2%)
    ppermute x6, starting transfers between devices, ring(): lax.ppermute(array, 'ctx', [(i, (i + step) % count) for i in range(count)])  11.9 us
    pallas_call x2, Pallas kernels, attend(): pl.pallas_call(functools.partial(attend_kernel, sources, first, last, 2 *...  11.5 us
    ppermute x7, starting transfers between devices, swap(): return lax.ppermute(array, axis, [(0, 1), (1, 0)])  5.87 us
    pallas_call x2, Pallas kernels, slot_call(): pl.pallas_call(kernel, out_shape=out_shape, in_specs=[smem, smem] + [vmem...  4.65 us
    ppermute x7, waiting for transfers between devices, swap(): return lax.ppermute(array, axis, [(0, 1), (1, 0)])  3.23 us
    ppermute x6, waiting for transfers between devices, ring(): lax.ppermute(array, 'ctx', [(i, (i + step) % count) for i in range(count)])  2.87 us
    unnamed x26, local copies, waits for them, and re-layouts  2.74 us
    pallas_call x1, Pallas kernels, split_heads(): pl.pallas_call(split_kernel, out_shape=(piece, piece), scratch_shapes=[pl...  1.93 us
  transfers between devices with their start and end apart: 13, of which 5 were waited for; matrix products, arithmetic and copies ran while one was open for 0% of the time, Pallas kernels for 25%

profile of v2, /device:TPU:0, one launch (start us, length us, event | category | flops | bytes accessed | tf_op | source)
XLA Modules:
  0.0 45.5 jit_solution(15576929974536577861)
XLA Ops:
  0.6 0.5 %collective-permute-start = (bf16[256,2,128]{2,1,0:T(2,128)(2,1)}, bf16[256,2,128]{2,1,0:T(2,128)(2,1)S(1)}, u32[]{:S(2)}, u32[]{:S(2)}) collective-permute-start(bf16[256,2,128]{2,1,0:T(2,128)(2,1)} %param.7), channel_id=1, source_target_pairs={{0,1},{1,0},{2,3},{3,2},{4,5},{5,4},{6,7},{7,6},{8,9},{9,8},{10,11... | collective-permute-start | bytes 393224 | tf_op jit(solution)/shard_map/ppermute | solution.py:504
  1.2 1.1 %collective-permute-done = bf16[256,2,128]{2,1,0:T(2,128)(2,1)S(1)} collective-permute-done((bf16[256,2,128]{2,1,0:T(2,128)(2,1)}, bf16[256,2,128]{2,1,0:T(2,128)(2,1)S(1)}, u32[]{:S(2)}, u32[]{:S(2)}) %collective-permute-start) | collective-permute-done | bytes 131104 | tf_op jit(solution)/shard_map/ppermute | solution.py:504
  2.3 0.4 collective-permute-done.1
  3.0 0.4 copy-done.9
  3.4 1.9 %split_heads.1 = (bf16[2,256,128]{2,1,0:T(8,128)(2,1)}, bf16[2,256,128]{2,1,0:T(8,128)(2,1)}) custom-call(bf16[512,128]{1,0:T(8,128)(2,1)} %bitcast.9, bf16[512,128]{1,0:T(8,128)(2,1)} %bitcast.11, bf16[512,128]{1,0:T(8,128)(2,1)} %bitcast.10, bf16[512,128]{1,0:T(8,128)(2,1)} %bitcast.12), custom_call_target="tpu_custom_call" | custom-call | tf_op jit(solution)/shard_map/split_heads/pallas_call | solution.py:208
  5.3 2.8 %collective-permute-start.5 = (bf16[2,256,128]{2,1,0:T(8,128)(2,1)}, bf16[2,256,128]{2,1,0:T(8,128)(2,1)S(1)}, u32[]{:S(2)}, u32[]{:S(2)}) collective-permute-start(bf16[2,256,128]{2,1,0:T(8,128)(2,1)} %get-tuple-element.14.refs_4_.refs_0_), channel_id=1, source_target_pairs={{0,4},{4,8},{8,12},{12,0},{1,5},{5,9},{9,13},{13,1},{2,6},{6,10},{... | collective-permute-start | bytes 393224 | tf_op jit(solution)/shard_map/ppermute | solution.py:500
  8.0 1.6 %collective-permute-start.2 = (bf16[2,256,128]{2,1,0:T(8,128)(2,1)}, bf16[2,256,128]{2,1,0:T(8,128)(2,1)S(1)}, u32[]{:S(2)}, u32[]{:S(2)}) collective-permute-start(bf16[2,256,128]{2,1,0:T(8,128)(2,1)} %get-tuple-element.11.refs_3_), channel_id=1, source_target_pairs={{0,4},{4,8},{8,12},{12,0},{1,5},{5,9},{9,13},{13,1},{2,6},{6,10},{... | collective-permute-start | bytes 393224 | tf_op jit(solution)/shard_map/ppermute | solution.py:500
  9.6 2.2 %collective-permute-start.8 = (bf16[2,256,128]{2,1,0:T(8,128)(2,1)}, bf16[2,256,128]{2,1,0:T(8,128)(2,1)S(1)}, u32[]{:S(2)}, u32[]{:S(2)}) collective-permute-start(bf16[2,256,128]{2,1,0:T(8,128)(2,1)} %get-tuple-element.14.refs_4_.refs_0_), channel_id=1, source_target_pairs={{0,12},{4,0},{8,4},{12,8},{1,13},{5,1},{9,5},{13,9},{2,14},{6,2},{... | collective-permute-start | bytes 393224 | tf_op jit(solution)/shard_map/ppermute | solution.py:500
  12.1 1.7 %collective-permute-start.9 = (bf16[2,256,128]{2,1,0:T(8,128)(2,1)}, bf16[2,256,128]{2,1,0:T(8,128)(2,1)S(1)}, u32[]{:S(2)}, u32[]{:S(2)}) collective-permute-start(bf16[2,256,128]{2,1,0:T(8,128)(2,1)} %get-tuple-element.11.refs_3_), channel_id=1, source_target_pairs={{0,2},{2,0},{1,3},{3,1},{4,6},{6,4},{5,7},{7,5},{8,10},{10,8},{9,1... | collective-permute-start | bytes 393224 | tf_op jit(solution)/shard_map/ppermute | solution.py:504
  13.8 0.9 %collective-permute-done.5.refs_4_.refs_3_ = bf16[2,256,128]{2,1,0:T(8,128)(2,1)S(1)} collective-permute-done((bf16[2,256,128]{2,1,0:T(8,128)(2,1)}, bf16[2,256,128]{2,1,0:T(8,128)(2,1)S(1)}, u32[]{:S(2)}, u32[]{:S(2)}) %collective-permute-start.5) | collective-permute-done | bytes 131104 | tf_op jit(solution)/shard_map/ppermute | solution.py:500
  14.7 0.7 %collective-permute-start.6 = (bf16[2,256,128]{2,1,0:T(8,128)(2,1)S(1)}, bf16[2,256,128]{2,1,0:T(8,128)(2,1)S(1)}, u32[]{:S(2)}, u32[]{:S(2)}) collective-permute-start(bf16[2,256,128]{2,1,0:T(8,128)(2,1)S(1)} %collective-permute-done.5.refs_4_.refs_3_), channel_id=1, source_target_pairs={{0,4},{4,8},{8,12},{12,0},{1,5},{5,9},{9,13},{13,1},{2,6},{6,10},{... | collective-permute-start | bytes 393224 | tf_op jit(solution)/shard_map/ppermute | solution.py:500
  15.4 2.0 %collective-permute-done.2.refs_3_ = bf16[2,256,128]{2,1,0:T(8,128)(2,1)S(1)} collective-permute-done((bf16[2,256,128]{2,1,0:T(8,128)(2,1)}, bf16[2,256,128]{2,1,0:T(8,128)(2,1)S(1)}, u32[]{:S(2)}, u32[]{:S(2)}) %collective-permute-start.2) | collective-permute-done | bytes 131104 | tf_op jit(solution)/shard_map/ppermute | solution.py:500
  17.4 4.4 %collective-permute-start.3 = (bf16[2,256,128]{2,1,0:T(8,128)(2,1)S(1)}, bf16[2,256,128]{2,1,0:T(8,128)(2,1)S(1)}, u32[]{:S(2)}, u32[]{:S(2)}) collective-permute-start(bf16[2,256,128]{2,1,0:T(8,128)(2,1)S(1)} %collective-permute-done.2.refs_3_), channel_id=1, source_target_pairs={{0,4},{4,8},{8,12},{12,0},{1,5},{5,9},{9,13},{13,1},{2,6},{6,10},{... | collective-permute-start | bytes 393224 | tf_op jit(solution)/shard_map/ppermute | solution.py:500
  21.8 1.5 %collective-permute-start.11 = (bf16[2,256,128]{2,1,0:T(8,128)(2,1)S(1)}, bf16[2,256,128]{2,1,0:T(8,128)(2,1)S(1)}, u32[]{:S(2)}, u32[]{:S(2)}) collective-permute-start(bf16[2,256,128]{2,1,0:T(8,128)(2,1)S(1)} %collective-permute-done.2.refs_3_), channel_id=1, source_target_pairs={{0,2},{2,0},{1,3},{3,1},{4,6},{6,4},{5,7},{7,5},{8,10},{10,8},{9,1... | collective-permute-start | bytes 393224 | tf_op jit(solution)/shard_map/ppermute | solution.py:504
  23.3 1.4 %collective-permute-start.10 = (bf16[2,256,128]{2,1,0:T(8,128)(2,1)S(1)}, bf16[2,256,128]{2,1,0:T(8,128)(2,1)S(1)}, u32[]{:S(2)}, u32[]{:S(2)}) collective-permute-start(bf16[2,256,128]{2,1,0:T(8,128)(2,1)S(1)} %collective-permute-done.7.refs_5_), channel_id=1, source_target_pairs={{0,2},{2,0},{1,3},{3,1},{4,6},{6,4},{5,7},{7,5},{8,10},{10,8},{9,1... | collective-permute-start | bytes 393224 | tf_op jit(solution)/shard_map/ppermute | solution.py:504
  24.7 5.9 %attend.2 = (f32[2048,128]{1,0:T(8,128)}, f32[2048,128]{1,0:T(8,128)}, f32[2048,128]{1,0:T(8,128)}) custom-call(s32[4]{0:T(128)} %order_ref.3, s32[4]{0:T(128)} %refs_1_.3, bf16[2048,128]{1,0:T(8,128)(2,1)} %bitcast.15, bf16[2,256,128]{2,1,0:T(8,128)(2,1)} %get-tuple-element.11.refs_3_, bf16[2,256,128]{2,1,0:T(8,128)(2,1)} %get-tuple-element.14.refs_4_.refs_0_, ...), custom_call_target="tpu_custom_call" | custom-call | flops 4000000000 | bytes 1048576 | tf_op jit(solution)/shard_map/attend/pallas_call | solution.py:373
  30.6 0.7 %collective-permute-start.4 = (bf16[2,256,128]{2,1,0:T(8,128)(2,1)S(1)}, bf16[2,256,128]{2,1,0:T(8,128)(2,1)S(1)}, u32[]{:S(2)}, u32[]{:S(2)}) collective-permute-start(bf16[2,256,128]{2,1,0:T(8,128)(2,1)S(1)} %collective-permute-done.3.refs_5_), channel_id=1, source_target_pairs={{0,2},{2,0},{1,3},{3,1},{4,6},{6,4},{5,7},{7,5},{8,10},{10,8},{9,1... | collective-permute-start | bytes 393224 | tf_op jit(solution)/shard_map/ppermute | solution.py:504
  31.4 0.6 %copy-done.3 = bf16[2,256,128]{2,1,0:T(8,128)(2,1)} copy-done((bf16[2,256,128]{2,1,0:T(8,128)(2,1)}, bf16[2,256,128]{2,1,0:T(8,128)(2,1)S(1)}, u32[]{:S(2)}) %copy-start.3) | copy-done | bytes 131096
  32.0 5.6 %attend.3 = bf16[2048,128]{1,0:T(8,128)(2,1)} custom-call(s32[4]{0:T(128)} %order_ref.3, s32[4]{0:T(128)} %refs_1_.3, bf16[2048,128]{1,0:T(8,128)(2,1)} %bitcast.16, bf16[2,256,128]{2,1,0:T(8,128)(2,1)} %copy-done.10, bf16[2,256,128]{2,1,0:T(8,128)(2,1)} %copy-done, bf16[2,256,128]{2,1,0:T(8,128)(2,1)} %copy-done.12, bf16[2,256,128]{2,1,0:T(8,128)(2,1)} %copy-done.3, ...), custom_call_target="tpu_custom_call" | custom-call | flops 4000000000 | bytes 1048576 | tf_op jit(solution)/shard_map/attend/pallas_call | solution.py:373
  37.7 0.6 %copy-done.6 = bf16[2,256,128]{2,1,0:T(8,128)(2,1)} copy-done((bf16[2,256,128]{2,1,0:T(8,128)(2,1)}, bf16[2,256,128]{2,1,0:T(8,128)(2,1)S(1)}, u32[]{:S(2)}) %copy-start.6) | copy-done | bytes 131096
  38.4 2.1 %pick_slots.1 = bf16[8,2,2,32,128]{4,3,2,1,0:T(8,128)(2,1)} custom-call(s32[4]{0:T(128)} %order_ref.3, s32[16]{0:T(128)} %bitcast.13, bf16[2,256,128]{2,1,0:T(8,128)(2,1)} %get-tuple-element.14.refs_4_.refs_0_, bf16[2,256,128]{2,1,0:T(8,128)(2,1)} %copy-done.1, bf16[2,256,128]{2,1,0:T(8,128)(2,1)} %copy-done.3, bf16[2,256,128]{2,1,0:T(8,128)(2,1)} %copy-done, ...), custom_call_target="tpu_custom_call" | custom-call | tf_op jit(solution)/shard_map/pick_slots/pallas_call | solution.py:446
  40.5 1.7 %collective-permute-done.12.refs_8_ = bf16[8,2,2,32,128]{4,3,2,1,0:T(8,128)(2,1)S(1)} collective-permute-done((bf16[8,2,2,32,128]{4,3,2,1,0:T(8,128)(2,1)}, bf16[8,2,2,32,128]{4,3,2,1,0:T(8,128)(2,1)S(1)}, u32[]{:S(2)}, u32[]{:S(2)}) %collective-permute-start.12) | collective-permute-done | bytes 262176 | tf_op jit(solution)/shard_map/ppermute | solution.py:504
  42.3 0.7 %copy-done.7 = bf16[8,2,2,32,128]{4,3,2,1,0:T(8,128)(2,1)} copy-done((bf16[8,2,2,32,128]{4,3,2,1,0:T(8,128)(2,1)}, bf16[8,2,2,32,128]{4,3,2,1,0:T(8,128)(2,1)S(1)}, u32[]{:S(2)}) %copy-start.7) | copy-done | bytes 262168
  43.0 2.5 %place_slots.1 = bf16[2048,128]{1,0:T(8,128)(2,1)} custom-call(s32[4]{0:T(128)} %order_ref.3, s32[16]{0:T(128)} %bitcast.14, bf16[2,256,128]{2,1,0:T(8,128)(2,1)} %get-tuple-element.14.refs_4_.refs_0_, bf16[2,256,128]{2,1,0:T(8,128)(2,1)} %copy-done.1, bf16[2,256,128]{2,1,0:T(8,128)(2,1)} %copy-done.3, bf16[2,256,128]{2,1,0:T(8,128)(2,1)} %copy-done, ...), custom_call_target="tpu_custom_call" | custom-call | tf_op jit(solution)/shard_map/place_slots/pallas_call | solution.py:446
  (33 shorter events, 0.8 us)
Async XLA Ops:
  0.6 1.7 %collective-permute-start = (bf16[256,2,128]{2,1,0:T(2,128)(2,1)}, bf16[256,2,128]{2,1,0:T(2,128)(2,1)S(1)}, u32[]{:S(2)}, u32[]{:S(2)}) collective-permute-start(bf16[256,2,128]{2,1,0:T(2,128)(2,1)} %param.7), channel_id=1, source_target_pairs={{0,1},{1,0},{2,3},{3,2},{4,5},{5,4},{6,7},{7,6},{8,9},{9,8},{10,11... | collective-permute-start | bytes 393224 | tf_op jit(solution)/shard_map/ppermute | solution.py:504
  1.1 1.6 %collective-permute-start.1 = (bf16[256,2,128]{2,1,0:T(2,128)(2,1)}, bf16[256,2,128]{2,1,0:T(2,128)(2,1)S(1)}, u32[]{:S(2)}, u32[]{:S(2)}) collective-permute-start(bf16[256,2,128]{2,1,0:T(2,128)(2,1)} %param.8), channel_id=1, source_target_pairs={{0,1},{1,0},{2,3},{3,2},{4,5},{5,4},{6,7},{7,6},{8,9},{9,8},{10,11... | collective-permute-start | bytes 393224 | tf_op jit(solution)/shard_map/ppermute | solution.py:504
  2.3 0.7 %copy-start.8 = (bf16[256,2,128]{2,1,0:T(2,128)(2,1)}, bf16[256,2,128]{2,1,0:T(2,128)(2,1)S(1)}, u32[]{:S(2)}) copy-start(bf16[256,2,128]{2,1,0:T(2,128)(2,1)S(1)} %collective-permute-done) | copy-start | bytes 393220
  2.7 0.7 %copy-start.9 = (bf16[256,2,128]{2,1,0:T(2,128)(2,1)}, bf16[256,2,128]{2,1,0:T(2,128)(2,1)S(1)}, u32[]{:S(2)}) copy-start(bf16[256,2,128]{2,1,0:T(2,128)(2,1)S(1)} %collective-permute-done.1) | copy-start | bytes 393220
  5.3 9.4 %collective-permute-start.5 = (bf16[2,256,128]{2,1,0:T(8,128)(2,1)}, bf16[2,256,128]{2,1,0:T(8,128)(2,1)S(1)}, u32[]{:S(2)}, u32[]{:S(2)}) collective-permute-start(bf16[2,256,128]{2,1,0:T(8,128)(2,1)} %get-tuple-element.14.refs_4_.refs_0_), channel_id=1, source_target_pairs={{0,4},{4,8},{8,12},{12,0},{1,5},{5,9},{9,13},{13,1},{2,6},{6,10},{... | collective-permute-start | bytes 393224 | tf_op jit(solution)/shard_map/ppermute | solution.py:500
  8.0 9.3 %collective-permute-start.2 = (bf16[2,256,128]{2,1,0:T(8,128)(2,1)}, bf16[2,256,128]{2,1,0:T(8,128)(2,1)S(1)}, u32[]{:S(2)}, u32[]{:S(2)}) collective-permute-start(bf16[2,256,128]{2,1,0:T(8,128)(2,1)} %get-tuple-element.11.refs_3_), channel_id=1, source_target_pairs={{0,4},{4,8},{8,12},{12,0},{1,5},{5,9},{9,13},{13,1},{2,6},{6,10},{... | collective-permute-start | bytes 393224 | tf_op jit(solution)/shard_map/ppermute | solution.py:500
  9.6 12.2 %collective-permute-start.8 = (bf16[2,256,128]{2,1,0:T(8,128)(2,1)}, bf16[2,256,128]{2,1,0:T(8,128)(2,1)S(1)}, u32[]{:S(2)}, u32[]{:S(2)}) collective-permute-start(bf16[2,256,128]{2,1,0:T(8,128)(2,1)} %get-tuple-element.14.refs_4_.refs_0_), channel_id=1, source_target_pairs={{0,12},{4,0},{8,4},{12,8},{1,13},{5,1},{9,5},{13,9},{2,14},{6,2},{... | collective-permute-start | bytes 393224 | tf_op jit(solution)/shard_map/ppermute | solution.py:500
  11.9 11.4 %collective-permute-start.7 = (bf16[2,256,128]{2,1,0:T(8,128)(2,1)}, bf16[2,256,128]{2,1,0:T(8,128)(2,1)S(1)}, u32[]{:S(2)}, u32[]{:S(2)}) collective-permute-start(bf16[2,256,128]{2,1,0:T(8,128)(2,1)} %get-tuple-element.11.refs_3_), channel_id=1, source_target_pairs={{0,12},{4,0},{8,4},{12,8},{1,13},{5,1},{9,5},{13,9},{2,14},{6,2},{... | collective-permute-start | bytes 393224 | tf_op jit(solution)/shard_map/ppermute | solution.py:500
  12.1 25.5 %collective-permute-start.9 = (bf16[2,256,128]{2,1,0:T(8,128)(2,1)}, bf16[2,256,128]{2,1,0:T(8,128)(2,1)S(1)}, u32[]{:S(2)}, u32[]{:S(2)}) collective-permute-start(bf16[2,256,128]{2,1,0:T(8,128)(2,1)} %get-tuple-element.11.refs_3_), channel_id=1, source_target_pairs={{0,2},{2,0},{1,3},{3,1},{4,6},{6,4},{5,7},{7,5},{8,10},{10,8},{9,1... | collective-permute-start | bytes 393224 | tf_op jit(solution)/shard_map/ppermute | solution.py:504
  14.7 15.9 %copy-start = (bf16[2,256,128]{2,1,0:T(8,128)(2,1)}, bf16[2,256,128]{2,1,0:T(8,128)(2,1)S(1)}, u32[]{:S(2)}) copy-start(bf16[2,256,128]{2,1,0:T(8,128)(2,1)S(1)} %collective-permute-done.5.refs_4_.refs_3_) | copy-start | bytes 393220
  14.7 16.7 %collective-permute-start.6 = (bf16[2,256,128]{2,1,0:T(8,128)(2,1)S(1)}, bf16[2,256,128]{2,1,0:T(8,128)(2,1)S(1)}, u32[]{:S(2)}, u32[]{:S(2)}) collective-permute-start(bf16[2,256,128]{2,1,0:T(8,128)(2,1)S(1)} %collective-permute-done.5.refs_4_.refs_3_), channel_id=1, source_target_pairs={{0,4},{4,8},{8,12},{12,0},{1,5},{5,9},{9,13},{13,1},{2,6},{6,10},{... | collective-permute-start | bytes 393224 | tf_op jit(solution)/shard_map/ppermute | solution.py:500
  17.4 13.2 %copy-start.10 = (bf16[2,256,128]{2,1,0:T(8,128)(2,1)}, bf16[2,256,128]{2,1,0:T(8,128)(2,1)S(1)}, u32[]{:S(2)}) copy-start(bf16[2,256,128]{2,1,0:T(8,128)(2,1)S(1)} %collective-permute-done.2.refs_3_) | copy-start | bytes 393220
  17.4 13.2 %collective-permute-start.3 = (bf16[2,256,128]{2,1,0:T(8,128)(2,1)S(1)}, bf16[2,256,128]{2,1,0:T(8,128)(2,1)S(1)}, u32[]{:S(2)}, u32[]{:S(2)}) collective-permute-start(bf16[2,256,128]{2,1,0:T(8,128)(2,1)S(1)} %collective-permute-done.2.refs_3_), channel_id=1, source_target_pairs={{0,4},{4,8},{8,12},{12,0},{1,5},{5,9},{9,13},{13,1},{2,6},{6,10},{... | collective-permute-start | bytes 393224 | tf_op jit(solution)/shard_map/ppermute | solution.py:500
  21.8 2.9 %copy-start.1 = (bf16[2,256,128]{2,1,0:T(8,128)(2,1)}, bf16[2,256,128]{2,1,0:T(8,128)(2,1)S(1)}, u32[]{:S(2)}) copy-start(bf16[2,256,128]{2,1,0:T(8,128)(2,1)S(1)} %collective-permute-done.8.refs_6_.refs_1_) | copy-start | bytes 393220
  21.8 15.9 %collective-permute-start.11 = (bf16[2,256,128]{2,1,0:T(8,128)(2,1)S(1)}, bf16[2,256,128]{2,1,0:T(8,128)(2,1)S(1)}, u32[]{:S(2)}, u32[]{:S(2)}) collective-permute-start(bf16[2,256,128]{2,1,0:T(8,128)(2,1)S(1)} %collective-permute-done.2.refs_3_), channel_id=1, source_target_pairs={{0,2},{2,0},{1,3},{3,1},{4,6},{6,4},{5,7},{7,5},{8,10},{10,8},{9,1... | collective-permute-start | bytes 393224 | tf_op jit(solution)/shard_map/ppermute | solution.py:504
  23.3 1.4 %copy-start.11 = (bf16[2,256,128]{2,1,0:T(8,128)(2,1)}, bf16[2,256,128]{2,1,0:T(8,128)(2,1)S(1)}, u32[]{:S(2)}) copy-start(bf16[2,256,128]{2,1,0:T(8,128)(2,1)S(1)} %collective-permute-done.7.refs_5_) | copy-start | bytes 393220
  23.3 14.4 %collective-permute-start.10 = (bf16[2,256,128]{2,1,0:T(8,128)(2,1)S(1)}, bf16[2,256,128]{2,1,0:T(8,128)(2,1)S(1)}, u32[]{:S(2)}, u32[]{:S(2)}) collective-permute-start(bf16[2,256,128]{2,1,0:T(8,128)(2,1)S(1)} %collective-permute-done.7.refs_5_), channel_id=1, source_target_pairs={{0,2},{2,0},{1,3},{3,1},{4,6},{6,4},{5,7},{7,5},{8,10},{10,8},{9,1... | collective-permute-start | bytes 393224 | tf_op jit(solution)/shard_map/ppermute | solution.py:504
  30.6 0.7 %copy-start.12 = (bf16[2,256,128]{2,1,0:T(8,128)(2,1)}, bf16[2,256,128]{2,1,0:T(8,128)(2,1)S(1)}, u32[]{:S(2)}) copy-start(bf16[2,256,128]{2,1,0:T(8,128)(2,1)S(1)} %collective-permute-done.3.refs_5_) | copy-start | bytes 393220
  30.6 7.0 %collective-permute-start.4 = (bf16[2,256,128]{2,1,0:T(8,128)(2,1)S(1)}, bf16[2,256,128]{2,1,0:T(8,128)(2,1)S(1)}, u32[]{:S(2)}, u32[]{:S(2)}) collective-permute-start(bf16[2,256,128]{2,1,0:T(8,128)(2,1)S(1)} %collective-permute-done.3.refs_5_), channel_id=1, source_target_pairs={{0,2},{2,0},{1,3},{3,1},{4,6},{6,4},{5,7},{7,5},{8,10},{10,8},{9,1... | collective-permute-start | bytes 393224 | tf_op jit(solution)/shard_map/ppermute | solution.py:504
  37.6 0.7 %copy-start.2 = (bf16[2,256,128]{2,1,0:T(8,128)(2,1)}, bf16[2,256,128]{2,1,0:T(8,128)(2,1)S(1)}, u32[]{:S(2)}) copy-start(bf16[2,256,128]{2,1,0:T(8,128)(2,1)S(1)} %collective-permute-done.9.refs_4_) | copy-start | bytes 393220
  37.6 0.7 %copy-start.4 = (bf16[2,256,128]{2,1,0:T(8,128)(2,1)}, bf16[2,256,128]{2,1,0:T(8,128)(2,1)S(1)}, u32[]{:S(2)}) copy-start(bf16[2,256,128]{2,1,0:T(8,128)(2,1)S(1)} %collective-permute-done.11.refs_7_) | copy-start | bytes 393220
  37.7 0.7 %copy-start.5 = (bf16[2,256,128]{2,1,0:T(8,128)(2,1)}, bf16[2,256,128]{2,1,0:T(8,128)(2,1)S(1)}, u32[]{:S(2)}) copy-start(bf16[2,256,128]{2,1,0:T(8,128)(2,1)S(1)} %collective-permute-done.10.refs_5_) | copy-start | bytes 393220
  40.5 1.7 %collective-permute-start.12 = (bf16[8,2,2,32,128]{4,3,2,1,0:T(8,128)(2,1)}, bf16[8,2,2,32,128]{4,3,2,1,0:T(8,128)(2,1)S(1)}, u32[]{:S(2)}, u32[]{:S(2)}) collective-permute-start(bf16[8,2,2,32,128]{4,3,2,1,0:T(8,128)(2,1)} %pick_slots.1), channel_id=1, source_target_pairs={{0,1},{1,0},{2,3},{3,2},{4,5},{5,4},{6,7},{7,6},{8,9},{9,8},{10,11... | collective-permute-start | bytes 786440 | tf_op jit(solution)/shard_map/ppermute | solution.py:504
  42.3 0.7 %copy-start.7 = (bf16[8,2,2,32,128]{4,3,2,1,0:T(8,128)(2,1)}, bf16[8,2,2,32,128]{4,3,2,1,0:T(8,128)(2,1)S(1)}, u32[]{:S(2)}) copy-start(bf16[8,2,2,32,128]{4,3,2,1,0:T(8,128)(2,1)S(1)} %collective-permute-done.12.refs_8_) | copy-start | bytes 786436
  (2 other events, 1.3 us)

commit v3 on v2

--- a/solution.py
+++ b/solution.py
@@ -209,6 +209,7 @@
         split_kernel,
         out_shape=(piece, piece),
         scratch_shapes=[pltpu.VMEM((2, 2, rows, width), jnp.float32)],
+        compiler_params=pltpu.CompilerParams(vmem_limit_bytes=12 * 2**20),
         name="split_heads",
     )(keys, keys_other, values, values_other)
 
@@ -386,6 +387,7 @@
         cost_estimate=pl.CostEstimate(
             flops=COST_FLOPS, bytes_accessed=4 * rows * width, transcendentals=0
         ),
+        compiler_params=pltpu.CompilerParams(vmem_limit_bytes=24 * 2**20),
         name="attend",
     )(order, lengths, query, *pieces, *state)
 
@@ -453,6 +455,7 @@
             pltpu.VMEM((2, count) + piece_shape, jnp.bfloat16),
         ]
         + scratch,
+        compiler_params=pltpu.CompilerParams(vmem_limit_bytes=12 * 2**20),
         name=name,
     )(*operands)
 

time: 45.8 us -> 38.6 us (0.84)
  Pallas kernels: 18.1 us -> 11.5 us
  waiting for transfers between devices: 6.11 us -> 5.47 us
    pallas_call x2, Pallas kernels: 11.5 us -> 9.04 us  [attend(): pl.pallas_call(functools.partial(attend_kernel, sources, first, last, 2 *...]
    pallas_call x2, Pallas kernels: 4.65 us -> 2.4 us  [slot_call(): pl.pallas_call(kernel, out_shape=out_shape, in_specs=[smem, smem] + [vmem...]
    pallas_call x1, Pallas kernels: 1.93 us -> 0.11 us  [split_heads(): pl.pallas_call(split_kernel, out_shape=(piece, piece), scratch_shapes=[pl...]
    unnamed x26 -> x12, local copies, waits for them, and re-layouts: 2.74 us -> 2.44 us
  transfers between devices with their start and end apart: 13 -> 13, of which waited for: 5 -> 5; matrix products, arithmetic and copies ran while one was open for 0% -> 0% of each run, Pallas kernels for 25% -> 24%
where the time goes in v3:
time: 38.6 us; the launch traced here: 38.4 us
  starting transfers between devices  18.2 us (47%)
  Pallas kernels  11.5 us (30%)
  waiting for transfers between devices  5.47 us (14%)
  local copies, waits for them, and re-layouts  2.44 us (6%)
  between operations  0.7 us (2%)
    ppermute x6, starting transfers between devices, ring(): lax.ppermute(array, 'ctx', [(i, (i + step) % count) for i in range(count)])  12.1 us
    pallas_call x2, Pallas kernels, attend(): pl.pallas_call(functools.partial(attend_kernel, sources, first, last, 2 *...  9.04 us
    ppermute x7, starting transfers between devices, swap(): return lax.ppermute(array, axis, [(0, 1), (1, 0)])  6.08 us
    ppermute x7, waiting for transfers between devices, swap(): return lax.ppermute(array, axis, [(0, 1), (1, 0)])  3.01 us
    ppermute x6, waiting for transfers between devices, ring(): lax.ppermute(array, 'ctx', [(i, (i + step) % count) for i in range(count)])  2.45 us
    unnamed x12, local copies, waits for them, and re-layouts  2.44 us
    pallas_call x2, Pallas kernels, slot_call(): pl.pallas_call(kernel, out_shape=out_shape, in_specs=[smem, smem] + [vmem...  2.4 us
  transfers between devices with their start and end apart: 13, of which 5 were waited for; matrix products, arithmetic and copies ran while one was open for 0% of the time, Pallas kernels for 24%

profile of v3, /device:TPU:0, one launch (start us, length us, event | category | flops | bytes accessed | tf_op | source)
XLA Modules:
  0.0 38.4 jit_solution(12160737248035779445)
XLA Ops:
  0.6 0.5 %collective-permute-start = (bf16[256,2,128]{2,1,0:T(2,128)(2,1)}, bf16[256,2,128]{2,1,0:T(2,128)(2,1)S(1)}, u32[]{:S(2)}, u32[]{:S(2)}) collective-permute-start(bf16[256,2,128]{2,1,0:T(2,128)(2,1)} %param.7), channel_id=1, source_target_pairs={{0,1},{1,0},{2,3},{3,2},{4,5},{5,4},{6,7},{7,6},{8,9},{9,8},{10,11... | collective-permute-start | bytes 393224 | tf_op jit(solution)/shard_map/ppermute | solution.py:507
  1.2 1.1 %collective-permute-done = bf16[256,2,128]{2,1,0:T(2,128)(2,1)S(1)} collective-permute-done((bf16[256,2,128]{2,1,0:T(2,128)(2,1)}, bf16[256,2,128]{2,1,0:T(2,128)(2,1)S(1)}, u32[]{:S(2)}, u32[]{:S(2)}) %collective-permute-start) | collective-permute-done | bytes 131104 | tf_op jit(solution)/shard_map/ppermute | solution.py:507
  2.3 0.4 collective-permute-done.1
  2.7 0.9 %copy-done = bf16[256,2,128]{2,1,0:T(2,128)(2,1)S(1)} copy-done((bf16[256,2,128]{2,1,0:T(2,128)(2,1)S(1)}, bf16[256,2,128]{2,1,0:T(2,128)(2,1)}, u32[]{:S(2)}) %copy-start) | copy-done | bytes 131096
  3.6 0.9 %copy-done.1 = bf16[256,2,128]{2,1,0:T(2,128)(2,1)S(1)} copy-done((bf16[256,2,128]{2,1,0:T(2,128)(2,1)S(1)}, bf16[256,2,128]{2,1,0:T(2,128)(2,1)}, u32[]{:S(2)}) %copy-start.1) | copy-done | bytes 131096
  4.5 0.1 split_heads.1
  4.6 2.8 %collective-permute-start.5 = (bf16[2,256,128]{2,1,0:T(8,128)(2,1)S(1)}, bf16[2,256,128]{2,1,0:T(8,128)(2,1)S(1)}, u32[]{:S(2)}, u32[]{:S(2)}) collective-permute-start(bf16[2,256,128]{2,1,0:T(8,128)(2,1)S(1)} %get-tuple-element.14.refs_4_.refs_0_), channel_id=1, source_target_pairs={{0,4},{4,8},{8,12},{12,0},{1,5},{5,9},{9,13},{13,1},{2,6},{6,10},{... | collective-permute-start | bytes 393224 | tf_op jit(solution)/shard_map/ppermute | solution.py:503
  7.4 1.6 %collective-permute-start.2 = (bf16[2,256,128]{2,1,0:T(8,128)(2,1)S(1)}, bf16[2,256,128]{2,1,0:T(8,128)(2,1)S(1)}, u32[]{:S(2)}, u32[]{:S(2)}) collective-permute-start(bf16[2,256,128]{2,1,0:T(8,128)(2,1)S(1)} %get-tuple-element.11.refs_3_), channel_id=1, source_target_pairs={{0,4},{4,8},{8,12},{12,0},{1,5},{5,9},{9,13},{13,1},{2,6},{6,10},{... | collective-permute-start | bytes 393224 | tf_op jit(solution)/shard_map/ppermute | solution.py:503
  9.0 2.2 %collective-permute-start.8 = (bf16[2,256,128]{2,1,0:T(8,128)(2,1)S(1)}, bf16[2,256,128]{2,1,0:T(8,128)(2,1)S(1)}, u32[]{:S(2)}, u32[]{:S(2)}) collective-permute-start(bf16[2,256,128]{2,1,0:T(8,128)(2,1)S(1)} %get-tuple-element.14.refs_4_.refs_0_), channel_id=1, source_target_pairs={{0,12},{4,0},{8,4},{12,8},{1,13},{5,1},{9,5},{13,9},{2,14},{6,2},{... | collective-permute-start | bytes 393224 | tf_op jit(solution)/shard_map/ppermute | solution.py:503
  11.3 0.3 collective-permute-start.7
  11.6 1.6 %collective-permute-start.9 = (bf16[2,256,128]{2,1,0:T(8,128)(2,1)S(1)}, bf16[2,256,128]{2,1,0:T(8,128)(2,1)S(1)}, u32[]{:S(2)}, u32[]{:S(2)}) collective-permute-start(bf16[2,256,128]{2,1,0:T(8,128)(2,1)S(1)} %get-tuple-element.11.refs_3_), channel_id=1, source_target_pairs={{0,2},{2,0},{1,3},{3,1},{4,6},{6,4},{5,7},{7,5},{8,10},{10,8},{9,1... | collective-permute-start | bytes 393224 | tf_op jit(solution)/shard_map/ppermute | solution.py:507
  13.2 0.7 %collective-permute-done.5.refs_4_.refs_3_ = bf16[2,256,128]{2,1,0:T(8,128)(2,1)S(1)} collective-permute-done((bf16[2,256,128]{2,1,0:T(8,128)(2,1)S(1)}, bf16[2,256,128]{2,1,0:T(8,128)(2,1)S(1)}, u32[]{:S(2)}, u32[]{:S(2)}) %collective-permute-start.5) | collective-permute-done | bytes 131104 | tf_op jit(solution)/shard_map/ppermute | solution.py:503
  13.9 0.9 %collective-permute-start.6 = (bf16[2,256,128]{2,1,0:T(8,128)(2,1)S(1)}, bf16[2,256,128]{2,1,0:T(8,128)(2,1)S(1)}, u32[]{:S(2)}, u32[]{:S(2)}) collective-permute-start(bf16[2,256,128]{2,1,0:T(8,128)(2,1)S(1)} %collective-permute-done.5.refs_4_.refs_3_), channel_id=1, source_target_pairs={{0,4},{4,8},{8,12},{12,0},{1,5},{5,9},{9,13},{13,1},{2,6},{6,10},{... | collective-permute-start | bytes 393224 | tf_op jit(solution)/shard_map/ppermute | solution.py:503
  14.8 1.8 %collective-permute-done.2.refs_3_ = bf16[2,256,128]{2,1,0:T(8,128)(2,1)S(1)} collective-permute-done((bf16[2,256,128]{2,1,0:T(8,128)(2,1)S(1)}, bf16[2,256,128]{2,1,0:T(8,128)(2,1)S(1)}, u32[]{:S(2)}, u32[]{:S(2)}) %collective-permute-start.2) | collective-permute-done | bytes 131104 | tf_op jit(solution)/shard_map/ppermute | solution.py:503
  16.6 4.3 %collective-permute-start.3 = (bf16[2,256,128]{2,1,0:T(8,128)(2,1)S(1)}, bf16[2,256,128]{2,1,0:T(8,128)(2,1)S(1)}, u32[]{:S(2)}, u32[]{:S(2)}) collective-permute-start(bf16[2,256,128]{2,1,0:T(8,128)(2,1)S(1)} %collective-permute-done.2.refs_3_), channel_id=1, source_target_pairs={{0,4},{4,8},{8,12},{12,0},{1,5},{5,9},{9,13},{13,1},{2,6},{6,10},{... | collective-permute-start | bytes 393224 | tf_op jit(solution)/shard_map/ppermute | solution.py:503
  20.9 1.5 %collective-permute-start.11 = (bf16[2,256,128]{2,1,0:T(8,128)(2,1)S(1)}, bf16[2,256,128]{2,1,0:T(8,128)(2,1)S(1)}, u32[]{:S(2)}, u32[]{:S(2)}) collective-permute-start(bf16[2,256,128]{2,1,0:T(8,128)(2,1)S(1)} %collective-permute-done.2.refs_3_), channel_id=1, source_target_pairs={{0,2},{2,0},{1,3},{3,1},{4,6},{6,4},{5,7},{7,5},{8,10},{10,8},{9,1... | collective-permute-start | bytes 393224 | tf_op jit(solution)/shard_map/ppermute | solution.py:507
  22.3 1.5 %collective-permute-start.10 = (bf16[2,256,128]{2,1,0:T(8,128)(2,1)S(1)}, bf16[2,256,128]{2,1,0:T(8,128)(2,1)S(1)}, u32[]{:S(2)}, u32[]{:S(2)}) collective-permute-start(bf16[2,256,128]{2,1,0:T(8,128)(2,1)S(1)} %collective-permute-done.7.refs_5_), channel_id=1, source_target_pairs={{0,2},{2,0},{1,3},{3,1},{4,6},{6,4},{5,7},{7,5},{8,10},{10,8},{9,1... | collective-permute-start | bytes 393224 | tf_op jit(solution)/shard_map/ppermute | solution.py:507
  23.9 4.4 %attend.2 = (f32[2048,128]{1,0:T(8,128)S(1)}, f32[2048,128]{1,0:T(8,128)S(1)}, f32[2048,128]{1,0:T(8,128)S(1)}) custom-call(s32[4]{0:T(128)S(1)} %copy-done.2, s32[4]{0:T(128)S(1)} %copy-done.5, bf16[2048,128]{1,0:T(8,128)(2,1)S(1)} %bitcast.14, bf16[2,256,128]{2,1,0:T(8,128)(2,1)S(1)} %get-tuple-element.11.refs_3_, ...), custom_call_target="tpu_custom_call" | custom-call | flops 4000000000 | bytes 1048576 | tf_op jit(solution)/shard_map/attend/pallas_call | solution.py:374
  28.2 0.8 %collective-permute-start.4 = (bf16[2,256,128]{2,1,0:T(8,128)(2,1)S(1)}, bf16[2,256,128]{2,1,0:T(8,128)(2,1)S(1)}, u32[]{:S(2)}, u32[]{:S(2)}) collective-permute-start(bf16[2,256,128]{2,1,0:T(8,128)(2,1)S(1)} %collective-permute-done.3.refs_5_), channel_id=1, source_target_pairs={{0,2},{2,0},{1,3},{3,1},{4,6},{6,4},{5,7},{7,5},{8,10},{10,8},{9,1... | collective-permute-start | bytes 393224 | tf_op jit(solution)/shard_map/ppermute | solution.py:507
  29.0 4.7 %attend.3 = bf16[2048,128]{1,0:T(8,128)(2,1)} custom-call(s32[4]{0:T(128)S(1)} %copy-done.2, s32[4]{0:T(128)S(1)} %copy-done.5, bf16[2048,128]{1,0:T(8,128)(2,1)S(1)} %bitcast.15, bf16[2,256,128]{2,1,0:T(8,128)(2,1)S(1)} %collective-permute-done.2.refs_3_, bf16[2,256,128]{2,1,0:T(8,128)(2,1)S(1)} %collective-permute-done.5.refs_4_.refs_3_, ...), custom_call_target="tpu_custom_call" | custom-call | flops 4000000000 | bytes 1048576 | tf_op jit(solution)/shard_map/attend/pallas_call | solution.py:374
  33.7 0.6 %copy-done.3 = s32[16,1]{0,1:T(1,128)S(1)} copy-done((s32[16,1]{0,1:T(1,128)S(1)}, s32[16,1]{0,1:T(1,128)}, u32[]{:S(2)}) %copy-start.3) | copy-done | bytes 88
  34.4 0.7 %pick_slots.1 = bf16[8,2,2,32,128]{4,3,2,1,0:T(8,128)(2,1)S(1)} custom-call(s32[4]{0:T(128)S(1)} %copy-done.2, s32[16]{0:T(128)S(1)} %bitcast.12, bf16[2,256,128]{2,1,0:T(8,128)(2,1)S(1)} %get-tuple-element.14.refs_4_.refs_0_, bf16[2,256,128]{2,1,0:T(8,128)(2,1)S(1)} %collective-permute-done.8.refs_6_.refs_1_, ...), custom_call_target="tpu_custom_call" | custom-call | tf_op jit(solution)/shard_map/pick_slots/pallas_call | solution.py:448
  35.1 1.5 %collective-permute-done.12.refs_8_ = bf16[8,2,2,32,128]{4,3,2,1,0:T(8,128)(2,1)S(1)} collective-permute-done((bf16[8,2,2,32,128]{4,3,2,1,0:T(8,128)(2,1)S(1)}, bf16[8,2,2,32,128]{4,3,2,1,0:T(8,128)(2,1)S(1)}, u32[]{:S(2)}, u32[]{:S(2)}) %collective-permute-start.12) | collective-permute-done | bytes 262176 | tf_op jit(solution)/shard_map/ppermute | solution.py:507
  36.7 1.7 %place_slots.1 = bf16[2048,128]{1,0:T(8,128)(2,1)} custom-call(s32[4]{0:T(128)S(1)} %copy-done.2, s32[16]{0:T(128)S(1)} %bitcast.13, bf16[2,256,128]{2,1,0:T(8,128)(2,1)S(1)} %get-tuple-element.14.refs_4_.refs_0_, bf16[2,256,128]{2,1,0:T(8,128)(2,1)S(1)} %collective-permute-done.8.refs_6_.refs_1_, ...), custom_call_target="tpu_custom_call" | custom-call | tf_op jit(solution)/shard_map/place_slots/pallas_call | solution.py:448
  (19 shorter events, 0.2 us)
Async XLA Ops:
  0.6 1.7 %collective-permute-start = (bf16[256,2,128]{2,1,0:T(2,128)(2,1)}, bf16[256,2,128]{2,1,0:T(2,128)(2,1)S(1)}, u32[]{:S(2)}, u32[]{:S(2)}) collective-permute-start(bf16[256,2,128]{2,1,0:T(2,128)(2,1)} %param.7), channel_id=1, source_target_pairs={{0,1},{1,0},{2,3},{3,2},{4,5},{5,4},{6,7},{7,6},{8,9},{9,8},{10,11... | collective-permute-start | bytes 393224 | tf_op jit(solution)/shard_map/ppermute | solution.py:507
  1.1 1.6 %collective-permute-start.1 = (bf16[256,2,128]{2,1,0:T(2,128)(2,1)}, bf16[256,2,128]{2,1,0:T(2,128)(2,1)S(1)}, u32[]{:S(2)}, u32[]{:S(2)}) collective-permute-start(bf16[256,2,128]{2,1,0:T(2,128)(2,1)} %param.8), channel_id=1, source_target_pairs={{0,1},{1,0},{2,3},{3,2},{4,5},{5,4},{6,7},{7,6},{8,9},{9,8},{10,11... | collective-permute-start | bytes 393224 | tf_op jit(solution)/shard_map/ppermute | solution.py:507
  2.7 0.9 %copy-start = (bf16[256,2,128]{2,1,0:T(2,128)(2,1)S(1)}, bf16[256,2,128]{2,1,0:T(2,128)(2,1)}, u32[]{:S(2)}) copy-start(bf16[256,2,128]{2,1,0:T(2,128)(2,1)} %param.7) | copy-start | bytes 393220
  3.6 0.9 %copy-start.1 = (bf16[256,2,128]{2,1,0:T(2,128)(2,1)S(1)}, bf16[256,2,128]{2,1,0:T(2,128)(2,1)}, u32[]{:S(2)}) copy-start(bf16[256,2,128]{2,1,0:T(2,128)(2,1)} %param.8) | copy-start | bytes 393220
  4.5 19.3 %copy-start.4 = (bf16[512,4,128]{2,1,0:T(4,128)(2,1)S(1)}, bf16[512,4,128]{2,1,0:T(4,128)(2,1)}, u32[]{:S(2)}) copy-start(bf16[512,4,128]{2,1,0:T(4,128)(2,1)} %param.6) | copy-start | bytes 1572868
  4.6 9.2 %collective-permute-start.5 = (bf16[2,256,128]{2,1,0:T(8,128)(2,1)S(1)}, bf16[2,256,128]{2,1,0:T(8,128)(2,1)S(1)}, u32[]{:S(2)}, u32[]{:S(2)}) collective-permute-start(bf16[2,256,128]{2,1,0:T(8,128)(2,1)S(1)} %get-tuple-element.14.refs_4_.refs_0_), channel_id=1, source_target_pairs={{0,4},{4,8},{8,12},{12,0},{1,5},{5,9},{9,13},{13,1},{2,6},{6,10},{... | collective-permute-start | bytes 393224 | tf_op jit(solution)/shard_map/ppermute | solution.py:503
  7.4 16.4 %copy-start.2 = (s32[4]{0:T(128)S(1)}, s32[4]{0:T(128)}, u32[]{:S(2)}) copy-start(s32[4]{0:T(128)} %order_ref.3) | copy-start | bytes 52
  7.4 16.4 %copy-start.5 = (s32[4]{0:T(128)S(1)}, s32[4]{0:T(128)}, u32[]{:S(2)}) copy-start(s32[4]{0:T(128)} %refs_1_.3) | copy-start | bytes 52
  7.4 9.1 %collective-permute-start.2 = (bf16[2,256,128]{2,1,0:T(8,128)(2,1)S(1)}, bf16[2,256,128]{2,1,0:T(8,128)(2,1)S(1)}, u32[]{:S(2)}, u32[]{:S(2)}) collective-permute-start(bf16[2,256,128]{2,1,0:T(8,128)(2,1)S(1)} %get-tuple-element.11.refs_3_), channel_id=1, source_target_pairs={{0,4},{4,8},{8,12},{12,0},{1,5},{5,9},{9,13},{13,1},{2,6},{6,10},{... | collective-permute-start | bytes 393224 | tf_op jit(solution)/shard_map/ppermute | solution.py:503
  9.0 11.8 %collective-permute-start.8 = (bf16[2,256,128]{2,1,0:T(8,128)(2,1)S(1)}, bf16[2,256,128]{2,1,0:T(8,128)(2,1)S(1)}, u32[]{:S(2)}, u32[]{:S(2)}) collective-permute-start(bf16[2,256,128]{2,1,0:T(8,128)(2,1)S(1)} %get-tuple-element.14.refs_4_.refs_0_), channel_id=1, source_target_pairs={{0,12},{4,0},{8,4},{12,8},{1,13},{5,1},{9,5},{13,9},{2,14},{6,2},{... | collective-permute-start | bytes 393224 | tf_op jit(solution)/shard_map/ppermute | solution.py:503
  11.3 11.1 %collective-permute-start.7 = (bf16[2,256,128]{2,1,0:T(8,128)(2,1)S(1)}, bf16[2,256,128]{2,1,0:T(8,128)(2,1)S(1)}, u32[]{:S(2)}, u32[]{:S(2)}) collective-permute-start(bf16[2,256,128]{2,1,0:T(8,128)(2,1)S(1)} %get-tuple-element.11.refs_3_), channel_id=1, source_target_pairs={{0,12},{4,0},{8,4},{12,8},{1,13},{5,1},{9,5},{13,9},{2,14},{6,2},{... | collective-permute-start | bytes 393224 | tf_op jit(solution)/shard_map/ppermute | solution.py:503
  11.6 22.1 %collective-permute-start.9 = (bf16[2,256,128]{2,1,0:T(8,128)(2,1)S(1)}, bf16[2,256,128]{2,1,0:T(8,128)(2,1)S(1)}, u32[]{:S(2)}, u32[]{:S(2)}) collective-permute-start(bf16[2,256,128]{2,1,0:T(8,128)(2,1)S(1)} %get-tuple-element.11.refs_3_), channel_id=1, source_target_pairs={{0,2},{2,0},{1,3},{3,1},{4,6},{6,4},{5,7},{7,5},{8,10},{10,8},{9,1... | collective-permute-start | bytes 393224 | tf_op jit(solution)/shard_map/ppermute | solution.py:507
  13.9 15.2 %collective-permute-start.6 = (bf16[2,256,128]{2,1,0:T(8,128)(2,1)S(1)}, bf16[2,256,128]{2,1,0:T(8,128)(2,1)S(1)}, u32[]{:S(2)}, u32[]{:S(2)}) collective-permute-start(bf16[2,256,128]{2,1,0:T(8,128)(2,1)S(1)} %collective-permute-done.5.refs_4_.refs_3_), channel_id=1, source_target_pairs={{0,4},{4,8},{8,12},{12,0},{1,5},{5,9},{9,13},{13,1},{2,6},{6,10},{... | collective-permute-start | bytes 393224 | tf_op jit(solution)/shard_map/ppermute | solution.py:503
  16.6 11.7 %collective-permute-start.3 = (bf16[2,256,128]{2,1,0:T(8,128)(2,1)S(1)}, bf16[2,256,128]{2,1,0:T(8,128)(2,1)S(1)}, u32[]{:S(2)}, u32[]{:S(2)}) collective-permute-start(bf16[2,256,128]{2,1,0:T(8,128)(2,1)S(1)} %collective-permute-done.2.refs_3_), channel_id=1, source_target_pairs={{0,4},{4,8},{8,12},{12,0},{1,5},{5,9},{9,13},{13,1},{2,6},{6,10},{... | collective-permute-start | bytes 393224 | tf_op jit(solution)/shard_map/ppermute | solution.py:503
  20.9 12.9 %collective-permute-start.11 = (bf16[2,256,128]{2,1,0:T(8,128)(2,1)S(1)}, bf16[2,256,128]{2,1,0:T(8,128)(2,1)S(1)}, u32[]{:S(2)}, u32[]{:S(2)}) collective-permute-start(bf16[2,256,128]{2,1,0:T(8,128)(2,1)S(1)} %collective-permute-done.2.refs_3_), channel_id=1, source_target_pairs={{0,2},{2,0},{1,3},{3,1},{4,6},{6,4},{5,7},{7,5},{8,10},{10,8},{9,1... | collective-permute-start | bytes 393224 | tf_op jit(solution)/shard_map/ppermute | solution.py:507
  22.3 11.4 %collective-permute-start.10 = (bf16[2,256,128]{2,1,0:T(8,128)(2,1)S(1)}, bf16[2,256,128]{2,1,0:T(8,128)(2,1)S(1)}, u32[]{:S(2)}, u32[]{:S(2)}) collective-permute-start(bf16[2,256,128]{2,1,0:T(8,128)(2,1)S(1)} %collective-permute-done.7.refs_5_), channel_id=1, source_target_pairs={{0,2},{2,0},{1,3},{3,1},{4,6},{6,4},{5,7},{7,5},{8,10},{10,8},{9,1... | collective-permute-start | bytes 393224 | tf_op jit(solution)/shard_map/ppermute | solution.py:507
  28.2 5.5 %collective-permute-start.4 = (bf16[2,256,128]{2,1,0:T(8,128)(2,1)S(1)}, bf16[2,256,128]{2,1,0:T(8,128)(2,1)S(1)}, u32[]{:S(2)}, u32[]{:S(2)}) collective-permute-start(bf16[2,256,128]{2,1,0:T(8,128)(2,1)S(1)} %collective-permute-done.3.refs_5_), channel_id=1, source_target_pairs={{0,2},{2,0},{1,3},{3,1},{4,6},{6,4},{5,7},{7,5},{8,10},{10,8},{9,1... | collective-permute-start | bytes 393224 | tf_op jit(solution)/shard_map/ppermute | solution.py:507
  33.7 0.7 %copy-start.3 = (s32[16,1]{0,1:T(1,128)S(1)}, s32[16,1]{0,1:T(1,128)}, u32[]{:S(2)}) copy-start(s32[16,1]{0,1:T(1,128)} %param.11) | copy-start | bytes 196
  35.1 1.6 %collective-permute-start.12 = (bf16[8,2,2,32,128]{4,3,2,1,0:T(8,128)(2,1)S(1)}, bf16[8,2,2,32,128]{4,3,2,1,0:T(8,128)(2,1)S(1)}, u32[]{:S(2)}, u32[]{:S(2)}) collective-permute-start(bf16[8,2,2,32,128]{4,3,2,1,0:T(8,128)(2,1)S(1)} %pick_slots.1), channel_id=1, source_target_pairs={{0,1},{1,0},{2,3},{3,2},{4,5},{5,4},{6,7},{7,6},{8,9},{9,8},{10,11... | collective-permute-start | bytes 786440 | tf_op jit(solution)/shard_map/ppermute | solution.py:507

commit v4 on v3

--- a/solution.py
+++ b/solution.py
@@ -186,32 +186,45 @@
 STRIP = 64
 
 
-def split_kernel(key_a, key_b, value_a, value_b, cross_ref, stay_ref, wide):
+def find_kernel(order_ref, partner_ref, found_ref):
+    locate_slots(order_ref, partner_ref, found_ref, lax.axis_index("ctx"), order_ref.shape[0])
+
+
+def find(order, partner):
+    smem = pl.BlockSpec(memory_space=pltpu.SMEM)
+    return pl.pallas_call(
+        find_kernel,
+        out_shape=jax.ShapeDtypeStruct((3, max(CAP, 2 * order.shape[0])), jnp.int32),
+        in_specs=[smem, smem],
+        out_specs=smem,
+        compiler_params=pltpu.CompilerParams(vmem_limit_bytes=8 * 2**20),
+        name="find_slots",
+    )(order, partner)
+
+
+def split_kernel(cross, own_ref, key_other, value_other, out_ref, wide):
     pair = lax.axis_index("pair")
     core = lax.axis_index("tp")
-    for kind, (own, other) in enumerate(((key_a, key_b), (value_a, value_b))):
-        wide[kind, core] = own[...].astype(jnp.float32)
+    part = 1 - pair if cross else pair
+    for kind, other in enumerate((key_other, value_other)):
+        wide[kind, core] = own_ref[kind]
         wide[kind, 1 - core] = other[...].astype(jnp.float32)
     for kind in range(2):
         for block in range(4):
-            at = pl.ds(block * HALF_TOKENS, HALF_TOKENS)
-            for out, part in ((cross_ref, 1 - pair), (stay_ref, pair)):
-                first = (block % 2) * 2 * BLK + part * 2 * HALF_TOKENS + core
-                rows = wide[kind, block // 2, pl.ds(first, HALF_TOKENS, stride=2), :]
-                rows = rows.astype(jnp.bfloat16)
-                out[kind, at, :] = rows
-
-
-def split_heads(keys, keys_other, values, values_other):
-    rows, width = keys.shape
-    piece = jax.ShapeDtypeStruct((2, rows // 2, width), jnp.bfloat16)
+            first = (block % 2) * 2 * BLK + part * 2 * HALF_TOKENS + core
+            rows = wide[kind, block // 2, pl.ds(first, HALF_TOKENS, stride=2), :]
+            out_ref[kind, pl.ds(block * HALF_TOKENS, HALF_TOKENS), :] = rows.astype(jnp.bfloat16)
+
+
+def split_heads(own, keys_other, values_other, cross):
+    _, rows, width = own.shape
     return pl.pallas_call(
-        split_kernel,
-        out_shape=(piece, piece),
+        functools.partial(split_kernel, cross),
+        out_shape=jax.ShapeDtypeStruct((2, rows // 2, width), jnp.bfloat16),
         scratch_shapes=[pltpu.VMEM((2, 2, rows, width), jnp.float32)],
         compiler_params=pltpu.CompilerParams(vmem_limit_bytes=12 * 2**20),
         name="split_heads",
-    )(keys, keys_other, values, values_other)
+    )(own, keys_other, values_other)
 
 
 def attend_kernel(sources, first, last, span_total, heads, *refs):
@@ -425,14 +438,12 @@
         held[index // count, index % count] = piece[...]
 
 
-def pick_kernel(order_ref, partner_ref, *refs):
-    count = order_ref.shape[0]
-    out_ref, found, held = refs[2 * count :]
-    shard = lax.axis_index("ctx")
+def pick_kernel(found, *refs):
+    out_ref, held = refs[-2:]
+    count = held.shape[1]
     core = lax.axis_index("tp")
     share = HALF_TOKENS // 2
     gather_pieces(refs[: 2 * count], count, held)
-    locate_slots(order_ref, partner_ref, found, shard, count)
     for slot in range(CAP):
         live, index, start = slot_place(found, slot)
         begin = pl.ds(pl.multiple_of(start + (1 - core) * share, share), share)
@@ -441,41 +452,34 @@
                 out_ref[slot, kind, which] = held[which, index, kind, begin, :]
 
 
-def slot_call(kernel, out_shape, scratch, name, operands, piece_shape):
+def slot_call(kernel, out_shape, scratch, name, count, operands, piece_shape):
     smem = pl.BlockSpec(memory_space=pltpu.SMEM)
     vmem = pl.BlockSpec(memory_space=pltpu.VMEM)
-    count = operands[0].shape[0]
     return pl.pallas_call(
         kernel,
         out_shape=out_shape,
-        in_specs=[smem, smem] + [vmem] * (len(operands) - 2),
+        in_specs=[smem] + [vmem] * (len(operands) - 1),
         out_specs=vmem,
-        scratch_shapes=[
-            pltpu.SMEM((3, max(CAP, 2 * count)), jnp.int32),
-            pltpu.VMEM((2, count) + piece_shape, jnp.bfloat16),
-        ]
-        + scratch,
+        scratch_shapes=[pltpu.VMEM((2, count) + piece_shape, jnp.bfloat16)] + scratch,
         compiler_params=pltpu.CompilerParams(vmem_limit_bytes=12 * 2**20),
         name=name,
     )(*operands)
 
 
-def pick(order, partner, stay, cross):
+def pick(found, stay, cross):
     piece_shape = cross[0].shape
     out_shape = jax.ShapeDtypeStruct((CAP, 2, 2, HALF_TOKENS // 2, piece_shape[2]), jnp.bfloat16)
-    operands = (order, partner, *stay, *cross)
-    return slot_call(pick_kernel, out_shape, [], "pick_slots", operands, piece_shape)
-
-
-def place_kernel(order_ref, partner_ref, *refs):
-    count = order_ref.shape[0]
-    given_ref, out_ref, found, held, wide = refs[2 * count :]
-    shard = lax.axis_index("ctx")
+    operands = (found, *stay, *cross)
+    return slot_call(pick_kernel, out_shape, [], "pick_slots", len(stay), operands, piece_shape)
+
+
+def place_kernel(found, *refs):
+    given_ref, out_ref, held, wide = refs[-4:]
+    count = held.shape[1]
     pair = lax.axis_index("pair")
     core = lax.axis_index("tp")
     share = HALF_TOKENS // 2
     gather_pieces(refs[: 2 * count], count, held)
-    locate_slots(order_ref, partner_ref, found, shard, count)
     for slot in range(CAP):
         live, index, start = slot_place(found, slot)
         begin = pl.ds(pl.multiple_of(start + core * share, share), share)
@@ -490,13 +494,13 @@
     out_ref[...] = wide[...].astype(jnp.bfloat16)
 
 
-def place(order, partner, stay, cross, given):
+def place(found, stay, cross, given):
     piece_shape = cross[0].shape
     rows = CAP * 2 * (HALF_TOKENS // 2) * 4
     out_shape = jax.ShapeDtypeStruct((rows, piece_shape[2]), jnp.bfloat16)
     scratch = [pltpu.VMEM((rows, piece_shape[2]), jnp.float32)]
-    operands = (order, partner, *stay, *cross, given)
-    return slot_call(place_kernel, out_shape, scratch, "place_slots", operands, piece_shape)
+    operands = (found, *stay, *cross, given)
+    return slot_call(place_kernel, out_shape, scratch, "place_slots", len(stay), operands, piece_shape)
 
 
 def ring(array, step, count):
@@ -516,34 +520,39 @@
     query_rows, heads, width = queries.shape
     partner = kv_partner[:, 0]
     query = queries.reshape(query_rows * heads, width)
-    cross0, stay0 = split_heads(
-        keys.reshape(-1, width),
-        swap(keys, "tp").reshape(-1, width),
-        values.reshape(-1, width),
-        swap(values, "tp").reshape(-1, width),
-    )
+    keys_flat = keys.reshape(-1, width)
+    values_flat = values.reshape(-1, width)
+    keys_other = swap(keys, "tp").reshape(-1, width)
+    values_other = swap(values, "tp").reshape(-1, width)
+    own = jnp.stack([keys_flat, values_flat]).astype(jnp.float32)
+    cross0 = split_heads(own, keys_other, values_other, True)
+    keys_other, _ = after(keys_other, cross0)
+    stay0 = split_heads(own, keys_other, values_other, False)
+    partner, _ = after(partner, stay0)
+    found = find(span_order, partner)
 
     def step(pieces, sources, state, last=False):
         return attend(span_order, lengths, query, pieces, sources, state, last, heads)
 
     cross3 = ring(cross0, 1, count)
     cross1 = ring(cross0, -1, count)
+    stay3 = ring(stay0, 1, count)
     stay1 = ring(stay0, -1, count)
-    stay3 = ring(stay0, 1, count)
     over0 = swap(cross0, "pair")
+    state = step((cross0, stay0), (0,), None)
     cross2 = ring(cross3, 1, count)
     over3 = swap(cross3, "pair")
     over1 = swap(cross1, "pair")
     stay2 = ring(stay3, 1, count)
-    stay0_late, stay3 = after(stay0, stay3)
-    state = step((cross0, stay0_late, cross1, stay1), (0, 1), None)
+    state = step((cross3, stay3, cross1, stay1), (3, 1), state)
     over2 = swap(cross2, "pair")
-    attended = step((cross3, stay3, cross2, stay2), (3, 2), state, True)
-    over2, attended = after(over2, attended)
     stay = (stay0, stay1, stay2, stay3)
     over = (over0, over1, over2, over3)
-    given = swap(pick(span_order, partner, stay, over), "tp")
-    cache = place(span_order, partner, stay, over, given)
+    picked = pick(found, stay, over)
+    given = swap(picked, "tp")
+    cross2, _ = after(cross2, picked)
+    attended = step((cross2, stay2), (2,), state, True)
+    cache = place(found, stay, over, given)
     return attended.reshape(queries.shape), cache.reshape(CAP, 2, HALF_TOKENS // 2, 4, width)
 
 

time: 38.6 us -> 35.8 us (0.927)
  starting transfers between devices: 18.2 us -> 15.5 us
  Pallas kernels: 11.5 us -> 14 us
  waiting for transfers between devices: 5.47 us -> 3.63 us
  local copies, waits for them, and re-layouts: 2.44 us -> 0.67 us
  other arithmetic: 0 us -> 1 us
    ppermute x6, starting transfers between devices: 12.1 us -> 9.26 us  [ring(): lax.ppermute(array, 'ctx', [(i, (i + step) % count) for i in range(count)])]
    unnamed x12 -> x8, local copies, waits for them, and re-layouts: 2.44 us -> 0.67 us
    pallas_call x2 -> x3, Pallas kernels: 9.04 us -> 10.3 us  [attend(): pl.pallas_call(functools.partial(attend_kernel, sources, first, last, 2 *...]
    pallas_call x3 -> x5, Pallas kernels: 2.51 us -> 3.73 us  [the longest x2 2.31 us: slot_call(): pl.pallas_call(kernel, out_shape=out_shape, in_specs=[smem] + [vmem] * (l...]
    ppermute x7, waiting for transfers between devices: 3.01 us -> 1.98 us  [swap(): return lax.ppermute(array, axis, [(0, 1), (1, 0)])]
    convert_element_type x0 -> x1, other arithmetic: none -> 1 us  [pieces_program(): own = jnp.stack([keys_flat, values_flat]).astype(jnp.float32)]
    ppermute x6, waiting for transfers between devices: 2.45 us -> 1.65 us  [ring(): lax.ppermute(array, 'ctx', [(i, (i + step) % count) for i in range(count)])]
  transfers between devices with their start and end apart: 13 -> 13, of which waited for: 5 -> 5; matrix products, arithmetic and copies ran while one was open for 0% -> 3% of each run, Pallas kernels for 24% -> 33%
where the time goes in v4:
time: 35.8 us; the launch traced here: 35.6 us
  starting transfers between devices  15.5 us (43%)
  Pallas kernels  14 us (39%)
  waiting for transfers between devices  3.63 us (10%)
  other arithmetic  1 us (3%)
  between operations  0.76 us (2%)
  local copies, waits for them, and re-layouts  0.67 us (2%)
    pallas_call x3, Pallas kernels, attend(): pl.pallas_call(functools.partial(attend_kernel, sources, first, last, 2 *...  10.3 us
    ppermute x6, starting transfers between devices, ring(): lax.ppermute(array, 'ctx', [(i, (i + step) % count) for i in range(count)])  9.26 us
    ppermute x7, starting transfers between devices, swap(): return lax.ppermute(array, axis, [(0, 1), (1, 0)])  6.24 us
    pallas_call x2, Pallas kernels, slot_call(): pl.pallas_call(kernel, out_shape=out_shape, in_specs=[smem] + [vmem] * (l...  2.31 us
    ppermute x7, waiting for transfers between devices, swap(): return lax.ppermute(array, axis, [(0, 1), (1, 0)])  1.98 us
    ppermute x6, waiting for transfers between devices, ring(): lax.ppermute(array, 'ctx', [(i, (i + step) % count) for i in range(count)])  1.65 us
    pallas_call x1, Pallas kernels, find(): pl.pallas_call(find_kernel, out_shape=jax.ShapeDtypeStruct((3, max(CAP, 2...  1.22 us
    convert_element_type x1, other arithmetic, pieces_program(): own = jnp.stack([keys_flat, values_flat]).astype(jnp.float32)  1 us
  transfers between devices with their start and end apart: 13, of which 5 were waited for; matrix products, arithmetic and copies ran while one was open for 3% of the time, Pallas kernels for 33%

profile of v4, /device:TPU:0, one launch (start us, length us, event | category | flops | bytes accessed | tf_op | source)
XLA Modules:
  0.0 35.6 jit_solution(1583758196902098715)
XLA Ops:
  0.6 0.5 %collective-permute-start = (bf16[256,2,128]{2,1,0:T(2,128)(2,1)}, bf16[256,2,128]{2,1,0:T(2,128)(2,1)S(1)}, u32[]{:S(2)}, u32[]{:S(2)}) collective-permute-start(bf16[256,2,128]{2,1,0:T(2,128)(2,1)} %param.7), channel_id=1, source_target_pairs={{0,1},{1,0},{2,3},{3,2},{4,5},{5,4},{6,7},{7,6},{8,9},{9,8},{10,11... | collective-permute-start | bytes 393224 | tf_op jit(solution)/shard_map/ppermute | solution.py:511
  1.2 1.0 %maximum_convert_fusion.own_ref = f32[2,512,128]{2,1,0:T(8,128)S(1)} fusion(bf16[1,512,128]{2,1,0:T(8,128)(2,1)} %bitcast.18, bf16[1,512,128]{2,1,0:T(8,128)(2,1)} %bitcast.17), kind=kLoop, calls=%fused_computation | loop fusion | flops 262144 | bytes 786432 | tf_op jit(solution)/shard_map/convert_element_type | solution.py:527
  2.2 0.1 collective-permute-done
  2.3 0.4 %collective-permute-done.1 = bf16[256,2,128]{2,1,0:T(2,128)(2,1)S(1)} collective-permute-done((bf16[256,2,128]{2,1,0:T(2,128)(2,1)}, bf16[256,2,128]{2,1,0:T(2,128)(2,1)S(1)}, u32[]{:S(2)}, u32[]{:S(2)}) %collective-permute-start.1) | collective-permute-done | bytes 131104 | tf_op jit(solution)/shard_map/ppermute | solution.py:511
  2.8 2.8 %collective-permute-start.2 = (bf16[2,256,128]{2,1,0:T(8,128)(2,1)S(1)}, bf16[2,256,128]{2,1,0:T(8,128)(2,1)S(1)}, u32[]{:S(2)}, u32[]{:S(2)}) collective-permute-start(bf16[2,256,128]{2,1,0:T(8,128)(2,1)S(1)} %split_heads.2.refs_3_), channel_id=1, source_target_pairs={{0,4},{4,8},{8,12},{12,0},{1,5},{5,9},{9,13},{13,1},{2,6},{6,10},{... | collective-permute-start | bytes 393224 | tf_op jit(solution)/shard_map/ppermute | solution.py:507
  5.8 1.6 %collective-permute-start.5 = (bf16[2,256,128]{2,1,0:T(8,128)(2,1)S(1)}, bf16[2,256,128]{2,1,0:T(8,128)(2,1)S(1)}, u32[]{:S(2)}, u32[]{:S(2)}) collective-permute-start(bf16[2,256,128]{2,1,0:T(8,128)(2,1)S(1)} %split_heads.3.refs_0_.refs_4_), channel_id=1, source_target_pairs={{0,4},{4,8},{8,12},{12,0},{1,5},{5,9},{9,13},{13,1},{2,6},{6,10},{... | collective-permute-start | bytes 393224 | tf_op jit(solution)/shard_map/ppermute | solution.py:507
  7.4 2.2 %collective-permute-start.4 = (bf16[2,256,128]{2,1,0:T(8,128)(2,1)S(1)}, bf16[2,256,128]{2,1,0:T(8,128)(2,1)S(1)}, u32[]{:S(2)}, u32[]{:S(2)}) collective-permute-start(bf16[2,256,128]{2,1,0:T(8,128)(2,1)S(1)} %split_heads.3.refs_0_.refs_4_), channel_id=1, source_target_pairs={{0,12},{4,0},{8,4},{12,8},{1,13},{5,1},{9,5},{13,9},{2,14},{6,2},{... | collective-permute-start | bytes 393224 | tf_op jit(solution)/shard_map/ppermute | solution.py:507
  9.6 0.3 collective-permute-start.8
  9.9 1.6 %collective-permute-start.7 = (bf16[2,256,128]{2,1,0:T(8,128)(2,1)S(1)}, bf16[2,256,128]{2,1,0:T(8,128)(2,1)S(1)}, u32[]{:S(2)}, u32[]{:S(2)}) collective-permute-start(bf16[2,256,128]{2,1,0:T(8,128)(2,1)S(1)} %split_heads.2.refs_3_), channel_id=1, source_target_pairs={{0,2},{2,0},{1,3},{3,1},{4,6},{6,4},{5,7},{7,5},{8,10},{10,8},{9,1... | collective-permute-start | bytes 393224 | tf_op jit(solution)/shard_map/ppermute | solution.py:511
  11.6 0.5 %collective-permute-done.2.refs_3_ = bf16[2,256,128]{2,1,0:T(8,128)(2,1)S(1)} collective-permute-done((bf16[2,256,128]{2,1,0:T(8,128)(2,1)S(1)}, bf16[2,256,128]{2,1,0:T(8,128)(2,1)S(1)}, u32[]{:S(2)}, u32[]{:S(2)}) %collective-permute-start.2) | collective-permute-done | bytes 131104 | tf_op jit(solution)/shard_map/ppermute | solution.py:507
  12.1 1.1 %collective-permute-start.3 = (bf16[2,256,128]{2,1,0:T(8,128)(2,1)S(1)}, bf16[2,256,128]{2,1,0:T(8,128)(2,1)S(1)}, u32[]{:S(2)}, u32[]{:S(2)}) collective-permute-start(bf16[2,256,128]{2,1,0:T(8,128)(2,1)S(1)} %collective-permute-done.2.refs_3_), channel_id=1, source_target_pairs={{0,4},{4,8},{8,12},{12,0},{1,5},{5,9},{9,13},{13,1},{2,6},{6,10},{... | collective-permute-start | bytes 393224 | tf_op jit(solution)/shard_map/ppermute | solution.py:507
  13.2 3.6 %attend.3 = (f32[2048,128]{1,0:T(8,128)S(1)}, f32[2048,128]{1,0:T(8,128)S(1)}, f32[2048,128]{1,0:T(8,128)S(1)}) custom-call(s32[4]{0:T(128)S(1)} %copy-done.1, s32[4]{0:T(128)S(1)} %copy-done.3, bf16[2048,128]{1,0:T(8,128)(2,1)S(1)} %bitcast.13, bf16[2,256,128]{2,1,0:T(8,128)(2,1)S(1)} %split_heads.2.refs_3_, bf16[2,256,128]{2,1,0:T(8,128)(2,1)S(1)} %split_heads.3.refs_0_.refs_4_), custom_call_target="tpu_custom_call" | custom-call | flops 4000000000 | bytes 1048576 | tf_op jit(solution)/shard_map/attend/pallas_call | solution.py:387
  16.8 0.6 %copy-done = s32[16,1]{0,1:T(1,128)S(1)} copy-done((s32[16,1]{0,1:T(1,128)S(1)}, s32[16,1]{0,1:T(1,128)}, u32[]{:S(2)}) %copy-start) | copy-done | bytes 88
  17.4 1.2 %find_slots.1.found = s32[3,8]{1,0:T(4,128)S(1)} custom-call(s32[4]{0:T(128)S(1)} %copy-done.1, s32[16]{0:T(128)S(1)} %bitcast.12), custom_call_target="tpu_custom_call" | custom-call | tf_op jit(solution)/shard_map/find_slots/pallas_call | solution.py:195
  18.7 0.7 %collective-permute-start.11 = (bf16[2,256,128]{2,1,0:T(8,128)(2,1)S(1)}, bf16[2,256,128]{2,1,0:T(8,128)(2,1)S(1)}, u32[]{:S(2)}, u32[]{:S(2)}) collective-permute-start(bf16[2,256,128]{2,1,0:T(8,128)(2,1)S(1)} %collective-permute-done.2.refs_3_), channel_id=1, source_target_pairs={{0,2},{2,0},{1,3},{3,1},{4,6},{6,4},{5,7},{7,5},{8,10},{10,8},{9,1... | collective-permute-start | bytes 393224 | tf_op jit(solution)/shard_map/ppermute | solution.py:511
  19.4 1.2 %collective-permute-start.6 = (bf16[2,256,128]{2,1,0:T(8,128)(2,1)S(1)}, bf16[2,256,128]{2,1,0:T(8,128)(2,1)S(1)}, u32[]{:S(2)}, u32[]{:S(2)}) collective-permute-start(bf16[2,256,128]{2,1,0:T(8,128)(2,1)S(1)} %collective-permute-done.5.refs_3_.refs_4_), channel_id=1, source_target_pairs={{0,4},{4,8},{8,12},{12,0},{1,5},{5,9},{9,13},{13,1},{2,6},{6,10},{... | collective-permute-start | bytes 393224 | tf_op jit(solution)/shard_map/ppermute | solution.py:507
  20.6 1.5 %collective-permute-start.9 = (bf16[2,256,128]{2,1,0:T(8,128)(2,1)S(1)}, bf16[2,256,128]{2,1,0:T(8,128)(2,1)S(1)}, u32[]{:S(2)}, u32[]{:S(2)}) collective-permute-start(bf16[2,256,128]{2,1,0:T(8,128)(2,1)S(1)} %collective-permute-done.8.refs_5_), channel_id=1, source_target_pairs={{0,2},{2,0},{1,3},{3,1},{4,6},{6,4},{5,7},{7,5},{8,10},{10,8},{9,1... | collective-permute-start | bytes 393224 | tf_op jit(solution)/shard_map/ppermute | solution.py:511
  22.0 1.2 %collective-permute-done.3.refs_3_ = bf16[2,256,128]{2,1,0:T(8,128)(2,1)S(1)} collective-permute-done((bf16[2,256,128]{2,1,0:T(8,128)(2,1)S(1)}, bf16[2,256,128]{2,1,0:T(8,128)(2,1)S(1)}, u32[]{:S(2)}, u32[]{:S(2)}) %collective-permute-start.3) | collective-permute-done | bytes 131104 | tf_op jit(solution)/shard_map/ppermute | solution.py:507
  23.2 1.7 %collective-permute-start.10 = (bf16[2,256,128]{2,1,0:T(8,128)(2,1)S(1)}, bf16[2,256,128]{2,1,0:T(8,128)(2,1)S(1)}, u32[]{:S(2)}, u32[]{:S(2)}) collective-permute-start(bf16[2,256,128]{2,1,0:T(8,128)(2,1)S(1)} %collective-permute-done.3.refs_3_), channel_id=1, source_target_pairs={{0,2},{2,0},{1,3},{3,1},{4,6},{6,4},{5,7},{7,5},{8,10},{10,8},{9,1... | collective-permute-start | bytes 393224 | tf_op jit(solution)/shard_map/ppermute | solution.py:511
  24.9 2.8 %attend.4 = (f32[2048,128]{1,0:T(8,128)S(1)}, f32[2048,128]{1,0:T(8,128)S(1)}, f32[2048,128]{1,0:T(8,128)S(1)}) custom-call(s32[4]{0:T(128)S(1)} %copy-done.1, s32[4]{0:T(128)S(1)} %copy-done.3, bf16[2048,128]{1,0:T(8,128)(2,1)S(1)} %bitcast.14, bf16[2,256,128]{2,1,0:T(8,128)(2,1)S(1)} %collective-permute-done.2.refs_3_, ...), custom_call_target="tpu_custom_call" | custom-call | flops 4000000000 | bytes 1048576 | tf_op jit(solution)/shard_map/attend/pallas_call | solution.py:387
  27.8 1.5 %collective-permute-done.10.refs_6_ = bf16[2,256,128]{2,1,0:T(8,128)(2,1)S(1)} collective-permute-done((bf16[2,256,128]{2,1,0:T(8,128)(2,1)S(1)}, bf16[2,256,128]{2,1,0:T(8,128)(2,1)S(1)}, u32[]{:S(2)}, u32[]{:S(2)}) %collective-permute-start.10) | collective-permute-done | bytes 131104 | tf_op jit(solution)/shard_map/ppermute | solution.py:511
  29.3 0.7 %pick_slots.1 = bf16[8,2,2,32,128]{4,3,2,1,0:T(8,128)(2,1)S(1)} custom-call(s32[3,8]{1,0:T(4,128)S(1)} %find_slots.1.found, bf16[2,256,128]{2,1,0:T(8,128)(2,1)S(1)} %split_heads.3.refs_0_.refs_4_, bf16[2,256,128]{2,1,0:T(8,128)(2,1)S(1)} %collective-permute-done.4.refs_1_.refs_6_, bf16[2,256,128]{2,1,0:T(8,128)(2,1)S(1)} %collective-permute-done.6.refs_2_.refs_4_, ...), custom_call_target="tpu_custom_call" | custom-call | tf_op jit(solution)/shard_map/pick_slots/pallas_call | solution.py:458
  30.1 3.9 %attend.5 = bf16[2048,128]{1,0:T(8,128)(2,1)} custom-call(s32[4]{0:T(128)S(1)} %copy-done.1, s32[4]{0:T(128)S(1)} %copy-done.3, bf16[2048,128]{1,0:T(8,128)(2,1)S(1)} %bitcast.15, bf16[2,256,128]{2,1,0:T(8,128)(2,1)S(1)} %collective-permute-done.3.refs_3_, bf16[2,256,128]{2,1,0:T(8,128)(2,1)S(1)} %collective-permute-done.6.refs_2_.refs_4_, ...), custom_call_target="tpu_custom_call" | custom-call | flops 4000000000 | bytes 1048576 | tf_op jit(solution)/shard_map/attend/pallas_call | solution.py:387
  33.9 1.6 %place_slots.1 = bf16[2048,128]{1,0:T(8,128)(2,1)} custom-call(s32[3,8]{1,0:T(4,128)S(1)} %find_slots.1.found, bf16[2,256,128]{2,1,0:T(8,128)(2,1)S(1)} %split_heads.3.refs_0_.refs_4_, bf16[2,256,128]{2,1,0:T(8,128)(2,1)S(1)} %collective-permute-done.4.refs_1_.refs_6_, bf16[2,256,128]{2,1,0:T(8,128)(2,1)S(1)} %collective-permute-done.6.refs_2_.refs_4_, ...), custom_call_target="tpu_custom_call" | custom-call | tf_op jit(solution)/shard_map/place_slots/pallas_call | solution.py:458
  (19 shorter events, 0.4 us)
Async XLA Ops:
  0.6 1.7 %collective-permute-start = (bf16[256,2,128]{2,1,0:T(2,128)(2,1)}, bf16[256,2,128]{2,1,0:T(2,128)(2,1)S(1)}, u32[]{:S(2)}, u32[]{:S(2)}) collective-permute-start(bf16[256,2,128]{2,1,0:T(2,128)(2,1)} %param.7), channel_id=1, source_target_pairs={{0,1},{1,0},{2,3},{3,2},{4,5},{5,4},{6,7},{7,6},{8,9},{9,8},{10,11... | collective-permute-start | bytes 393224 | tf_op jit(solution)/shard_map/ppermute | solution.py:511
  1.1 1.6 %collective-permute-start.1 = (bf16[256,2,128]{2,1,0:T(2,128)(2,1)}, bf16[256,2,128]{2,1,0:T(2,128)(2,1)S(1)}, u32[]{:S(2)}, u32[]{:S(2)}) collective-permute-start(bf16[256,2,128]{2,1,0:T(2,128)(2,1)} %param.8), channel_id=1, source_target_pairs={{0,1},{1,0},{2,3},{3,2},{4,5},{5,4},{6,7},{7,6},{8,9},{9,8},{10,11... | collective-permute-start | bytes 393224 | tf_op jit(solution)/shard_map/ppermute | solution.py:511
  2.8 10.3 %copy-start.2 = (bf16[512,4,128]{2,1,0:T(4,128)(2,1)S(1)}, bf16[512,4,128]{2,1,0:T(4,128)(2,1)}, u32[]{:S(2)}) copy-start(bf16[512,4,128]{2,1,0:T(4,128)(2,1)} %param.6) | copy-start | bytes 1572868
  2.8 9.2 %collective-permute-start.2 = (bf16[2,256,128]{2,1,0:T(8,128)(2,1)S(1)}, bf16[2,256,128]{2,1,0:T(8,128)(2,1)S(1)}, u32[]{:S(2)}, u32[]{:S(2)}) collective-permute-start(bf16[2,256,128]{2,1,0:T(8,128)(2,1)S(1)} %split_heads.2.refs_3_), channel_id=1, source_target_pairs={{0,4},{4,8},{8,12},{12,0},{1,5},{5,9},{9,13},{13,1},{2,6},{6,10},{... | collective-permute-start | bytes 393224 | tf_op jit(solution)/shard_map/ppermute | solution.py:507
  5.7 7.4 %copy-start.1 = (s32[4]{0:T(128)S(1)}, s32[4]{0:T(128)}, u32[]{:S(2)}) copy-start(s32[4]{0:T(128)} %refs_0_.5) | copy-start | bytes 52
  5.7 7.4 %copy-start.3 = (s32[4]{0:T(128)S(1)}, s32[4]{0:T(128)}, u32[]{:S(2)}) copy-start(s32[4]{0:T(128)} %refs_1_.5) | copy-start | bytes 52
  5.8 12.9 %collective-permute-start.5 = (bf16[2,256,128]{2,1,0:T(8,128)(2,1)S(1)}, bf16[2,256,128]{2,1,0:T(8,128)(2,1)S(1)}, u32[]{:S(2)}, u32[]{:S(2)}) collective-permute-start(bf16[2,256,128]{2,1,0:T(8,128)(2,1)S(1)} %split_heads.3.refs_0_.refs_4_), channel_id=1, source_target_pairs={{0,4},{4,8},{8,12},{12,0},{1,5},{5,9},{9,13},{13,1},{2,6},{6,10},{... | collective-permute-start | bytes 393224 | tf_op jit(solution)/shard_map/ppermute | solution.py:507
  7.4 12.0 %collective-permute-start.4 = (bf16[2,256,128]{2,1,0:T(8,128)(2,1)S(1)}, bf16[2,256,128]{2,1,0:T(8,128)(2,1)S(1)}, u32[]{:S(2)}, u32[]{:S(2)}) collective-permute-start(bf16[2,256,128]{2,1,0:T(8,128)(2,1)S(1)} %split_heads.3.refs_0_.refs_4_), channel_id=1, source_target_pairs={{0,12},{4,0},{8,4},{12,8},{1,13},{5,1},{9,5},{13,9},{2,14},{6,2},{... | collective-permute-start | bytes 393224 | tf_op jit(solution)/shard_map/ppermute | solution.py:507
  9.6 11.0 %collective-permute-start.8 = (bf16[2,256,128]{2,1,0:T(8,128)(2,1)S(1)}, bf16[2,256,128]{2,1,0:T(8,128)(2,1)S(1)}, u32[]{:S(2)}, u32[]{:S(2)}) collective-permute-start(bf16[2,256,128]{2,1,0:T(8,128)(2,1)S(1)} %split_heads.2.refs_3_), channel_id=1, source_target_pairs={{0,12},{4,0},{8,4},{12,8},{1,13},{5,1},{9,5},{13,9},{2,14},{6,2},{... | collective-permute-start | bytes 393224 | tf_op jit(solution)/shard_map/ppermute | solution.py:507
  9.9 17.8 %collective-permute-start.7 = (bf16[2,256,128]{2,1,0:T(8,128)(2,1)S(1)}, bf16[2,256,128]{2,1,0:T(8,128)(2,1)S(1)}, u32[]{:S(2)}, u32[]{:S(2)}) collective-permute-start(bf16[2,256,128]{2,1,0:T(8,128)(2,1)S(1)} %split_heads.2.refs_3_), channel_id=1, source_target_pairs={{0,2},{2,0},{1,3},{3,1},{4,6},{6,4},{5,7},{7,5},{8,10},{10,8},{9,1... | collective-permute-start | bytes 393224 | tf_op jit(solution)/shard_map/ppermute | solution.py:511
  12.1 11.1 %collective-permute-start.3 = (bf16[2,256,128]{2,1,0:T(8,128)(2,1)S(1)}, bf16[2,256,128]{2,1,0:T(8,128)(2,1)S(1)}, u32[]{:S(2)}, u32[]{:S(2)}) collective-permute-start(bf16[2,256,128]{2,1,0:T(8,128)(2,1)S(1)} %collective-permute-done.2.refs_3_), channel_id=1, source_target_pairs={{0,4},{4,8},{8,12},{12,0},{1,5},{5,9},{9,13},{13,1},{2,6},{6,10},{... | collective-permute-start | bytes 393224 | tf_op jit(solution)/shard_map/ppermute | solution.py:507
  16.8 0.7 %copy-start = (s32[16,1]{0,1:T(1,128)S(1)}, s32[16,1]{0,1:T(1,128)}, u32[]{:S(2)}) copy-start(s32[16,1]{0,1:T(1,128)} %param.11) | copy-start | bytes 196
  18.7 9.1 %collective-permute-start.11 = (bf16[2,256,128]{2,1,0:T(8,128)(2,1)S(1)}, bf16[2,256,128]{2,1,0:T(8,128)(2,1)S(1)}, u32[]{:S(2)}, u32[]{:S(2)}) collective-permute-start(bf16[2,256,128]{2,1,0:T(8,128)(2,1)S(1)} %collective-permute-done.2.refs_3_), channel_id=1, source_target_pairs={{0,2},{2,0},{1,3},{3,1},{4,6},{6,4},{5,7},{7,5},{8,10},{10,8},{9,1... | collective-permute-start | bytes 393224 | tf_op jit(solution)/shard_map/ppermute | solution.py:511
  19.4 8.4 %collective-permute-start.6 = (bf16[2,256,128]{2,1,0:T(8,128)(2,1)S(1)}, bf16[2,256,128]{2,1,0:T(8,128)(2,1)S(1)}, u32[]{:S(2)}, u32[]{:S(2)}) collective-permute-start(bf16[2,256,128]{2,1,0:T(8,128)(2,1)S(1)} %collective-permute-done.5.refs_3_.refs_4_), channel_id=1, source_target_pairs={{0,4},{4,8},{8,12},{12,0},{1,5},{5,9},{9,13},{13,1},{2,6},{6,10},{... | collective-permute-start | bytes 393224 | tf_op jit(solution)/shard_map/ppermute | solution.py:507
  20.6 7.2 %collective-permute-start.9 = (bf16[2,256,128]{2,1,0:T(8,128)(2,1)S(1)}, bf16[2,256,128]{2,1,0:T(8,128)(2,1)S(1)}, u32[]{:S(2)}, u32[]{:S(2)}) collective-permute-start(bf16[2,256,128]{2,1,0:T(8,128)(2,1)S(1)} %collective-permute-done.8.refs_5_), channel_id=1, source_target_pairs={{0,2},{2,0},{1,3},{3,1},{4,6},{6,4},{5,7},{7,5},{8,10},{10,8},{9,1... | collective-permute-start | bytes 393224 | tf_op jit(solution)/shard_map/ppermute | solution.py:511
  23.2 6.1 %collective-permute-start.10 = (bf16[2,256,128]{2,1,0:T(8,128)(2,1)S(1)}, bf16[2,256,128]{2,1,0:T(8,128)(2,1)S(1)}, u32[]{:S(2)}, u32[]{:S(2)}) collective-permute-start(bf16[2,256,128]{2,1,0:T(8,128)(2,1)S(1)} %collective-permute-done.3.refs_3_), channel_id=1, source_target_pairs={{0,2},{2,0},{1,3},{3,1},{4,6},{6,4},{5,7},{7,5},{8,10},{10,8},{9,1... | collective-permute-start | bytes 393224 | tf_op jit(solution)/shard_map/ppermute | solution.py:511
  30.0 4.0 %collective-permute-start.12 = (bf16[8,2,2,32,128]{4,3,2,1,0:T(8,128)(2,1)S(1)}, bf16[8,2,2,32,128]{4,3,2,1,0:T(8,128)(2,1)S(1)}, u32[]{:S(2)}, u32[]{:S(2)}) collective-permute-start(bf16[8,2,2,32,128]{4,3,2,1,0:T(8,128)(2,1)S(1)} %pick_slots.1), channel_id=1, source_target_pairs={{0,1},{1,0},{2,3},{3,2},{4,5},{5,4},{6,7},{7,6},{8,9},{9,8},{10,11... | collective-permute-start | bytes 786440 | tf_op jit(solution)/shard_map/ppermute | solution.py:511

commit v5 on v4

--- a/solution.py
+++ b/solution.py
@@ -183,23 +183,7 @@
 FLOOR = -1e29
 COST_FLOPS = 4 * 10**9
 Q_TILE = 1024
-STRIP = 64
-
-
-def find_kernel(order_ref, partner_ref, found_ref):
-    locate_slots(order_ref, partner_ref, found_ref, lax.axis_index("ctx"), order_ref.shape[0])
-
-
-def find(order, partner):
-    smem = pl.BlockSpec(memory_space=pltpu.SMEM)
-    return pl.pallas_call(
-        find_kernel,
-        out_shape=jax.ShapeDtypeStruct((3, max(CAP, 2 * order.shape[0])), jnp.int32),
-        in_specs=[smem, smem],
-        out_specs=smem,
-        compiler_params=pltpu.CompilerParams(vmem_limit_bytes=8 * 2**20),
-        name="find_slots",
-    )(order, partner)
+STRIP = 512
 
 
 def split_kernel(cross, own_ref, key_other, value_other, out_ref, wide):
@@ -228,8 +212,8 @@
 
 
 def attend_kernel(sources, first, last, span_total, heads, *refs):
-    order_ref, lengths_ref, query_ref = refs[:3]
-    refs = refs[3:]
+    order_ref, lengths_ref, _, query_ref = refs[:4]
+    refs = refs[4:]
     pieces = []
     for _ in sources:
         pieces.append((refs[0], refs[1]))
@@ -242,7 +226,7 @@
     else:
         peak_out, total_out, summed_out = refs[:3]
         refs = refs[3:]
-    score_ref, weights_ref, values_ref, top_ref, total_ref, summed_ref = refs
+    values_ref, top_ref, total_ref, summed_ref = refs
     shard = lax.axis_index("ctx")
     pair = lax.axis_index("pair")
     rows, width = query_ref.shape
@@ -295,69 +279,62 @@
             )
         if first:
             top_ref[...] = jnp.full(top_ref.shape, FLOOR, jnp.float32)
+            total_ref[...] = jnp.zeros(total_ref.shape, jnp.float32)
+            summed_ref[...] = jnp.zeros(summed_ref.shape, jnp.float32)
         else:
             top_ref[...] = peak_in[at, :]
+            total_ref[...] = total_in[at, :]
+            summed_ref[...] = summed_in[at, :]
 
         for number, (span, cross, stay, half) in enumerate(spans):
 
             @pl.when(near[number])
             def _():
                 part = pl.ds(half * part_keys, part_keys)
-                score_ref[number] = lax.dot_general(
-                    query_ref[at, :],
-                    jnp.concatenate([cross[0, part, :], stay[0, part, :]], axis=0),
-                    (((1,), (1,)), ((), ())),
-                    preferred_element_type=jnp.float32,
-                )
+                keys = jnp.concatenate([cross[0, part, :], stay[0, part, :]], axis=0)
                 key_pos = span * half_rows + local
+                index_in = lax.broadcasted_iota(jnp.int32, (STRIP, width), 0) // heads
                 for row in range(0, Q_TILE, STRIP):
                     strip = pl.ds(row, STRIP)
-                    index_in = lax.broadcasted_iota(jnp.int32, (STRIP, width), 0)
-                    query_pos = first_pos + row // heads + index_in // heads
+                    rows_at = pl.ds(pl.multiple_of(index * Q_TILE + row, STRIP), STRIP)
+                    score = lax.dot_general(
+                        query_ref[rows_at, :],
+                        keys,
+                        (((1,), (1,)), ((), ())),
+                        preferred_element_type=jnp.float32,
+                    )
+                    query_pos = first_pos + row // heads + index_in
                     query_begin = begin_of(query_pos)
-                    top = top_ref[strip, :]
+                    old = top_ref[strip, :]
+                    top = old
+                    masked = []
                     for column in range(0, keys_each, width):
                         at_key = key_pos[:, column : column + width]
                         visible = (at_key <= query_pos) & (at_key >= query_begin)
-                        score = score_ref[number, strip, column : column + width]
-                        score = jnp.where(visible, score, MASKED)
-                        score_ref[number, strip, column : column + width] = score
-                        top = jnp.maximum(top, score)
-                    top_ref[strip, :] = top
-
-        for row in range(0, Q_TILE, STRIP):
-            strip = pl.ds(row, STRIP)
-            peak = jnp.max(top_ref[strip, :], axis=1, keepdims=True)
-            peak = jnp.broadcast_to(peak, (STRIP, width))
-            top_ref[strip, :] = peak
-            rows_at = pl.ds(pl.multiple_of(index * Q_TILE + row, STRIP), STRIP)
-            if first:
-                total_ref[strip, :] = jnp.zeros((STRIP, width), jnp.float32)
-                summed_ref[strip, :] = jnp.zeros((STRIP, width), jnp.float32)
-            else:
-                fade = jnp.exp2((peak_in[rows_at, :] - peak) * factor)
-                total_ref[strip, :] = total_in[rows_at, :] * fade
-                summed_ref[strip, :] = summed_in[rows_at, :] * fade
-            if not last:
-                peak_out[rows_at, :] = peak
-        for number in range(len(spans)):
-
-            @pl.when(near[number])
-            def _():
-                for row in range(0, Q_TILE, STRIP):
-                    strip = pl.ds(row, STRIP)
-                    peak = top_ref[strip, :]
-                    total = total_ref[strip, :]
-                    for column in range(0, keys_each, width):
-                        score = score_ref[number, strip, column : column + width]
-                        weight = jnp.exp2((score - peak) * factor)
+                        masked.append(
+                            jnp.where(visible, score[:, column : column + width], MASKED)
+                        )
+                        top = jnp.maximum(top, masked[-1])
+                    peak = jnp.broadcast_to(
+                        jnp.max(top, axis=1, keepdims=True), (STRIP, width)
+                    )
+                    top_ref[strip, :] = peak
+                    fade = jnp.exp2((old - peak) * factor)
+                    total = total_ref[strip, :] * fade
+                    weights = []
+                    for part_score in masked:
+                        weight = jnp.exp2((part_score - peak) * factor)
                         total = total + weight
-                        weights_ref[strip, column : column + width] = weight.astype(jnp.bfloat16)
+                        weights.append(weight.astype(jnp.bfloat16))
                     total_ref[strip, :] = total
-                summed_ref[...] += jnp.dot(
-                    weights_ref[...], values_ref[number], preferred_element_type=jnp.float32
-                )
-
+                    summed_ref[strip, :] = summed_ref[strip, :] * fade + jnp.dot(
+                        jnp.concatenate(weights, axis=1),
+                        values_ref[number],
+                        preferred_element_type=jnp.float32,
+                    )
+
+        if not last:
+            peak_out[at, :] = top_ref[...]
         if last:
             total = jnp.sum(total_ref[...], axis=1, keepdims=True)
             out_ref[at, :] = (summed_ref[...] / total).astype(jnp.bfloat16)
@@ -369,7 +346,7 @@
     lax.fori_loop(0, rows // Q_TILE, tile, 0)
 
 
-def attend(order, lengths, query, pieces, sources, state, last, heads):
+def attend(order, lengths, partner, query, pieces, sources, state, last, heads):
     rows, width = query.shape
     first = state is None
     smem = pl.BlockSpec(memory_space=pltpu.SMEM)
@@ -387,11 +364,9 @@
     return pl.pallas_call(
         functools.partial(attend_kernel, sources, first, last, 2 * order.shape[0], heads),
         out_shape=out_shape,
-        in_specs=[smem, smem] + [vmem] * (1 + len(pieces) + len(state)),
+        in_specs=[smem] * 3 + [vmem] * (1 + len(pieces) + len(state)),
         out_specs=out_specs,
         scratch_shapes=[
-            pltpu.VMEM((count, Q_TILE, keys_each), jnp.float32),
-            pltpu.VMEM((Q_TILE, keys_each), jnp.bfloat16),
             pltpu.VMEM((count, keys_each, width), jnp.bfloat16),
             tile,
             tile,
@@ -402,7 +377,7 @@
         ),
         compiler_params=pltpu.CompilerParams(vmem_limit_bytes=24 * 2**20),
         name="attend",
-    )(order, lengths, query, *pieces, *state)
+    )(order, lengths, partner, query, *pieces, *state)
 
 
 def locate_slots(order_ref, partner_ref, found, shard, shard_count):
@@ -438,69 +413,66 @@
         held[index // count, index % count] = piece[...]
 
 
-def pick_kernel(found, *refs):
-    out_ref, held = refs[-2:]
+def pick_kernel(order_ref, partner_ref, *refs):
+    given_ref, kept_ref, held, found = refs[-4:]
     count = held.shape[1]
     core = lax.axis_index("tp")
     share = HALF_TOKENS // 2
     gather_pieces(refs[: 2 * count], count, held)
+    locate_slots(order_ref, partner_ref, found, lax.axis_index("ctx"), count)
     for slot in range(CAP):
         live, index, start = slot_place(found, slot)
-        begin = pl.ds(pl.multiple_of(start + (1 - core) * share, share), share)
-        for which in range(2):
-            for kind in range(2):
-                out_ref[slot, kind, which] = held[which, index, kind, begin, :]
-
-
-def slot_call(kernel, out_shape, scratch, name, count, operands, piece_shape):
+        for out_ref, half in ((given_ref, 1 - core), (kept_ref, core)):
+            begin = pl.ds(pl.multiple_of(start + half * share, share), share)
+            for which in range(2):
+                for kind in range(2):
+                    rows = held[which, index, kind, begin, :]
+                    out_ref[slot, kind, which] = jnp.where(live, rows, jnp.zeros_like(rows))
+
+
+def pick(order, partner, stay, cross):
     smem = pl.BlockSpec(memory_space=pltpu.SMEM)
     vmem = pl.BlockSpec(memory_space=pltpu.VMEM)
+    count = len(stay)
+    piece_shape = cross[0].shape
+    rows = jax.ShapeDtypeStruct((CAP, 2, 2, HALF_TOKENS // 2, piece_shape[2]), jnp.bfloat16)
     return pl.pallas_call(
-        kernel,
-        out_shape=out_shape,
-        in_specs=[smem] + [vmem] * (len(operands) - 1),
-        out_specs=vmem,
-        scratch_shapes=[pltpu.VMEM((2, count) + piece_shape, jnp.bfloat16)] + scratch,
+        pick_kernel,
+        out_shape=(rows, rows),
+        in_specs=[smem, smem] + [vmem] * (2 * count),
+        out_specs=(vmem, vmem),
+        scratch_shapes=[
+            pltpu.VMEM((2, count) + piece_shape, jnp.bfloat16),
+            pltpu.SMEM((3, max(CAP, 2 * count)), jnp.int32),
+        ],
         compiler_params=pltpu.CompilerParams(vmem_limit_bytes=12 * 2**20),
-        name=name,
-    )(*operands)
-
-
-def pick(found, stay, cross):
-    piece_shape = cross[0].shape
-    out_shape = jax.ShapeDtypeStruct((CAP, 2, 2, HALF_TOKENS // 2, piece_shape[2]), jnp.bfloat16)
-    operands = (found, *stay, *cross)
-    return slot_call(pick_kernel, out_shape, [], "pick_slots", len(stay), operands, piece_shape)
-
-
-def place_kernel(found, *refs):
-    given_ref, out_ref, held, wide = refs[-4:]
-    count = held.shape[1]
+        name="pick_slots",
+    )(order, partner, *stay, *cross)
+
+
+def place_kernel(kept_ref, given_ref, out_ref, wide):
     pair = lax.axis_index("pair")
     core = lax.axis_index("tp")
-    share = HALF_TOKENS // 2
-    gather_pieces(refs[: 2 * count], count, held)
+    share = kept_ref.shape[3]
     for slot in range(CAP):
-        live, index, start = slot_place(found, slot)
-        begin = pl.ds(pl.multiple_of(start + core * share, share), share)
-        for which in range(2):
-            group = 2 * (pair if which == 0 else 1 - pair)
-            for kind in range(2):
-                base = (slot * 2 + kind) * share * 4 + group
-                kept = held[which, index, kind, begin, :].astype(jnp.float32)
-                given = given_ref[slot, kind, which].astype(jnp.float32)
-                wide[pl.ds(base + core, share, stride=4), :] = jnp.where(live, kept, 0.0)
-                wide[pl.ds(base + 1 - core, share, stride=4), :] = jnp.where(live, given, 0.0)
+        for kind in range(2):
+            for which in range(2):
+                base = (slot * 2 + kind) * share * 4 + 2 * (pair if which == 0 else 1 - pair)
+                for ref, head in ((kept_ref, core), (given_ref, 1 - core)):
+                    rows = ref[slot, kind, which].astype(jnp.float32)
+                    wide[pl.ds(base + head, share, stride=4), :] = rows
     out_ref[...] = wide[...].astype(jnp.bfloat16)
 
 
-def place(found, stay, cross, given):
-    piece_shape = cross[0].shape
-    rows = CAP * 2 * (HALF_TOKENS // 2) * 4
-    out_shape = jax.ShapeDtypeStruct((rows, piece_shape[2]), jnp.bfloat16)
-    scratch = [pltpu.VMEM((rows, piece_shape[2]), jnp.float32)]
-    operands = (found, *stay, *cross, given)
-    return slot_call(place_kernel, out_shape, scratch, "place_slots", len(stay), operands, piece_shape)
+def place(kept, given):
+    rows, width = CAP * 2 * kept.shape[3] * 4, kept.shape[4]
+    return pl.pallas_call(
+        place_kernel,
+        out_shape=jax.ShapeDtypeStruct((rows, width), jnp.bfloat16),
+        scratch_shapes=[pltpu.VMEM((rows, width), jnp.float32)],
+        compiler_params=pltpu.CompilerParams(vmem_limit_bytes=12 * 2**20),
+        name="place_slots",
+    )(kept, given)
 
 
 def ring(array, step, count):
@@ -528,11 +500,9 @@
     cross0 = split_heads(own, keys_other, values_other, True)
     keys_other, _ = after(keys_other, cross0)
     stay0 = split_heads(own, keys_other, values_other, False)
-    partner, _ = after(partner, stay0)
-    found = find(span_order, partner)
 
     def step(pieces, sources, state, last=False):
-        return attend(span_order, lengths, query, pieces, sources, state, last, heads)
+        return attend(span_order, lengths, partner, query, pieces, sources, state, last, heads)
 
     cross3 = ring(cross0, 1, count)
     cross1 = ring(cross0, -1, count)
@@ -548,11 +518,11 @@
     over2 = swap(cross2, "pair")
     stay = (stay0, stay1, stay2, stay3)
     over = (over0, over1, over2, over3)
-    picked = pick(found, stay, over)
+    picked, kept = pick(span_order, partner, stay, over)
     given = swap(picked, "tp")
     cross2, _ = after(cross2, picked)
     attended = step((cross2, stay2), (2,), state, True)
-    cache = place(found, stay, over, given)
+    cache = place(kept, given)
     return attended.reshape(queries.shape), cache.reshape(CAP, 2, HALF_TOKENS // 2, 4, width)
 
 

time: 35.8 us -> 33.4 us (0.933)
  Pallas kernels: 14 us -> 8.41 us
  starting transfers between devices: 15.5 us -> 17.5 us
  waiting for transfers between devices: 3.63 us -> 4.8 us
    pallas_call x3, Pallas kernels: 10.3 us -> 6.4 us  [attend(): pl.pallas_call(functools.partial(attend_kernel, sources, first, last, 2 *...]
    ppermute x6, starting transfers between devices: 9.26 us -> 11.2 us  [ring(): lax.ppermute(array, 'ctx', [(i, (i + step) % count) for i in range(count)])]
    pallas_call x3 -> x2, Pallas kernels: 3.54 us -> 1.82 us  [the longest x1 1.03 us: place(): pl.pallas_call(place_kernel, out_shape=jax.ShapeDtypeStruct((rows, width)...]
    ppermute x6, waiting for transfers between devices: 1.65 us -> 2.74 us  [ring(): lax.ppermute(array, 'ctx', [(i, (i + step) % count) for i in range(count)])]
  transfers between devices with their start and end apart: 13 -> 13, of which waited for: 5 -> 7; matrix products, arithmetic and copies ran while one was open for 3% -> 3% of each run, Pallas kernels for 33% -> 20%
where the time goes in v5:
time: 33.4 us; the launch traced here: 33.1 us
  starting transfers between devices  17.5 us (52%)
  Pallas kernels  8.41 us (25%)
  waiting for transfers between devices  4.8 us (14%)
  other arithmetic  1 us (3%)
  between operations  0.71 us (2%)
  local copies, waits for them, and re-layouts  0.69 us (2%)
    ppermute x6, starting transfers between devices, ring(): lax.ppermute(array, 'ctx', [(i, (i + step) % count) for i in range(count)])  11.2 us
    pallas_call x3, Pallas kernels, attend(): pl.pallas_call(functools.partial(attend_kernel, sources, first, last, 2 *...  6.4 us
    ppermute x7, starting transfers between devices, swap(): return lax.ppermute(array, axis, [(0, 1), (1, 0)])  6.31 us
    ppermute x6, waiting for transfers between devices, ring(): lax.ppermute(array, 'ctx', [(i, (i + step) % count) for i in range(count)])  2.74 us
    ppermute x7, waiting for transfers between devices, swap(): return lax.ppermute(array, axis, [(0, 1), (1, 0)])  2.06 us
    pallas_call x1, Pallas kernels, place(): pl.pallas_call(place_kernel, out_shape=jax.ShapeDtypeStruct((rows, width)...  1.03 us
    convert_element_type x1, other arithmetic, pieces_program(): own = jnp.stack([keys_flat, values_flat]).astype(jnp.float32)  1 us
    pallas_call x1, Pallas kernels, pick(): pl.pallas_call(pick_kernel, out_shape=(rows, rows), in_specs=[smem, smem]...  0.8 us
  transfers between devices with their start and end apart: 13, of which 7 were waited for; matrix products, arithmetic and copies ran while one was open for 3% of the time, Pallas kernels for 20%

profile of v5, /device:TPU:0, one launch (start us, length us, event | category | flops | bytes accessed | tf_op | source)
XLA Modules:
  0.0 33.1 jit_solution(13331361287310873167)
XLA Ops:
  0.6 0.5 %collective-permute-start = (bf16[256,2,128]{2,1,0:T(2,128)(2,1)}, bf16[256,2,128]{2,1,0:T(2,128)(2,1)S(1)}, u32[]{:S(2)}, u32[]{:S(2)}) collective-permute-start(bf16[256,2,128]{2,1,0:T(2,128)(2,1)} %param.7), channel_id=1, source_target_pairs={{0,1},{1,0},{2,3},{3,2},{4,5},{5,4},{6,7},{7,6},{8,9},{9,8},{10,11... | collective-permute-start | bytes 393224 | tf_op jit(solution)/shard_map/ppermute | solution.py:483
  1.2 1.0 %maximum_convert_fusion.own_ref = f32[2,512,128]{2,1,0:T(8,128)S(1)} fusion(bf16[1,512,128]{2,1,0:T(8,128)(2,1)} %bitcast.21, bf16[1,512,128]{2,1,0:T(8,128)(2,1)} %bitcast.20), kind=kLoop, calls=%fused_computation | loop fusion | flops 262144 | bytes 786432 | tf_op jit(solution)/shard_map/convert_element_type | solution.py:499
  2.3 0.4 %collective-permute-done.1 = bf16[256,2,128]{2,1,0:T(2,128)(2,1)S(1)} collective-permute-done((bf16[256,2,128]{2,1,0:T(2,128)(2,1)}, bf16[256,2,128]{2,1,0:T(2,128)(2,1)S(1)}, u32[]{:S(2)}, u32[]{:S(2)}) %collective-permute-start.1) | collective-permute-done | bytes 131104 | tf_op jit(solution)/shard_map/ppermute | solution.py:483
  2.8 2.8 %collective-permute-start.2 = (bf16[2,256,128]{2,1,0:T(8,128)(2,1)S(1)}, bf16[2,256,128]{2,1,0:T(8,128)(2,1)S(1)}, u32[]{:S(2)}, u32[]{:S(2)}) collective-permute-start(bf16[2,256,128]{2,1,0:T(8,128)(2,1)S(1)} %split_heads.2.refs_4_), channel_id=1, source_target_pairs={{0,4},{4,8},{8,12},{12,0},{1,5},{5,9},{9,13},{13,1},{2,6},{6,10},{... | collective-permute-start | bytes 393224 | tf_op jit(solution)/shard_map/ppermute | solution.py:479
  5.7 1.6 %collective-permute-start.5 = (bf16[2,256,128]{2,1,0:T(8,128)(2,1)S(1)}, bf16[2,256,128]{2,1,0:T(8,128)(2,1)S(1)}, u32[]{:S(2)}, u32[]{:S(2)}) collective-permute-start(bf16[2,256,128]{2,1,0:T(8,128)(2,1)S(1)} %split_heads.3.refs_0_.refs_5_), channel_id=1, source_target_pairs={{0,4},{4,8},{8,12},{12,0},{1,5},{5,9},{9,13},{13,1},{2,6},{6,10},{... | collective-permute-start | bytes 393224 | tf_op jit(solution)/shard_map/ppermute | solution.py:479
  7.4 2.2 %collective-permute-start.4 = (bf16[2,256,128]{2,1,0:T(8,128)(2,1)S(1)}, bf16[2,256,128]{2,1,0:T(8,128)(2,1)S(1)}, u32[]{:S(2)}, u32[]{:S(2)}) collective-permute-start(bf16[2,256,128]{2,1,0:T(8,128)(2,1)S(1)} %split_heads.3.refs_0_.refs_5_), channel_id=1, source_target_pairs={{0,12},{4,0},{8,4},{12,8},{1,13},{5,1},{9,5},{13,9},{2,14},{6,2},{... | collective-permute-start | bytes 393224 | tf_op jit(solution)/shard_map/ppermute | solution.py:479
  9.6 0.3 collective-permute-start.8
  9.9 1.6 %collective-permute-start.7 = (bf16[2,256,128]{2,1,0:T(8,128)(2,1)S(1)}, bf16[2,256,128]{2,1,0:T(8,128)(2,1)S(1)}, u32[]{:S(2)}, u32[]{:S(2)}) collective-permute-start(bf16[2,256,128]{2,1,0:T(8,128)(2,1)S(1)} %split_heads.2.refs_4_), channel_id=1, source_target_pairs={{0,2},{2,0},{1,3},{3,1},{4,6},{6,4},{5,7},{7,5},{8,10},{10,8},{9,1... | collective-permute-start | bytes 393224 | tf_op jit(solution)/shard_map/ppermute | solution.py:483
  11.5 0.5 %collective-permute-done.2.refs_4_ = bf16[2,256,128]{2,1,0:T(8,128)(2,1)S(1)} collective-permute-done((bf16[2,256,128]{2,1,0:T(8,128)(2,1)S(1)}, bf16[2,256,128]{2,1,0:T(8,128)(2,1)S(1)}, u32[]{:S(2)}, u32[]{:S(2)}) %collective-permute-start.2) | collective-permute-done | bytes 131104 | tf_op jit(solution)/shard_map/ppermute | solution.py:479
  12.1 1.1 %collective-permute-start.3 = (bf16[2,256,128]{2,1,0:T(8,128)(2,1)S(1)}, bf16[2,256,128]{2,1,0:T(8,128)(2,1)S(1)}, u32[]{:S(2)}, u32[]{:S(2)}) collective-permute-start(bf16[2,256,128]{2,1,0:T(8,128)(2,1)S(1)} %collective-permute-done.2.refs_4_), channel_id=1, source_target_pairs={{0,4},{4,8},{8,12},{12,0},{1,5},{5,9},{9,13},{13,1},{2,6},{6,10},{... | collective-permute-start | bytes 393224 | tf_op jit(solution)/shard_map/ppermute | solution.py:479
  13.1 0.6 %copy-done = s32[4]{0:T(128)S(1)} copy-done((s32[4]{0:T(128)S(1)}, s32[4]{0:T(128)}, u32[]{:S(2)}) %copy-start) | copy-done | bytes 40
  13.8 2.6 %attend.3 = (f32[2048,128]{1,0:T(8,128)S(1)}, f32[2048,128]{1,0:T(8,128)S(1)}, f32[2048,128]{1,0:T(8,128)S(1)}) custom-call(s32[4]{0:T(128)S(1)} %copy-done, s32[4]{0:T(128)S(1)} %copy-done.3, s32[16]{0:T(128)S(1)} %bitcast.12, bf16[2048,128]{1,0:T(8,128)(2,1)S(1)} %bitcast.16, bf16[2,256,128]{2,1,0:T(8,128)(2,1)S(1)} %split_heads.2.refs_4_, ...), custom_call_target="tpu_custom_call" | custom-call | flops 4000000000 | bytes 1048576 | tf_op jit(solution)/shard_map/attend/pallas_call | solution.py:364
  16.4 0.7 %collective-permute-start.11 = (bf16[2,256,128]{2,1,0:T(8,128)(2,1)S(1)}, bf16[2,256,128]{2,1,0:T(8,128)(2,1)S(1)}, u32[]{:S(2)}, u32[]{:S(2)}) collective-permute-start(bf16[2,256,128]{2,1,0:T(8,128)(2,1)S(1)} %collective-permute-done.2.refs_4_), channel_id=1, source_target_pairs={{0,2},{2,0},{1,3},{3,1},{4,6},{6,4},{5,7},{7,5},{8,10},{10,8},{9,1... | collective-permute-start | bytes 393224 | tf_op jit(solution)/shard_map/ppermute | solution.py:483
  17.2 0.2 collective-permute-done.4.refs_1_.refs_7_
  17.4 3.2 %collective-permute-start.6 = (bf16[2,256,128]{2,1,0:T(8,128)(2,1)S(1)}, bf16[2,256,128]{2,1,0:T(8,128)(2,1)S(1)}, u32[]{:S(2)}, u32[]{:S(2)}) collective-permute-start(bf16[2,256,128]{2,1,0:T(8,128)(2,1)S(1)} %collective-permute-done.5.refs_3_.refs_5_), channel_id=1, source_target_pairs={{0,4},{4,8},{8,12},{12,0},{1,5},{5,9},{9,13},{13,1},{2,6},{6,10},{... | collective-permute-start | bytes 393224 | tf_op jit(solution)/shard_map/ppermute | solution.py:479
  20.5 1.5 %collective-permute-start.9 = (bf16[2,256,128]{2,1,0:T(8,128)(2,1)S(1)}, bf16[2,256,128]{2,1,0:T(8,128)(2,1)S(1)}, u32[]{:S(2)}, u32[]{:S(2)}) collective-permute-start(bf16[2,256,128]{2,1,0:T(8,128)(2,1)S(1)} %collective-permute-done.8.refs_6_), channel_id=1, source_target_pairs={{0,2},{2,0},{1,3},{3,1},{4,6},{6,4},{5,7},{7,5},{8,10},{10,8},{9,1... | collective-permute-start | bytes 393224 | tf_op jit(solution)/shard_map/ppermute | solution.py:483
  22.0 1.2 %collective-permute-done.3.refs_4_ = bf16[2,256,128]{2,1,0:T(8,128)(2,1)S(1)} collective-permute-done((bf16[2,256,128]{2,1,0:T(8,128)(2,1)S(1)}, bf16[2,256,128]{2,1,0:T(8,128)(2,1)S(1)}, u32[]{:S(2)}, u32[]{:S(2)}) %collective-permute-start.3) | collective-permute-done | bytes 131104 | tf_op jit(solution)/shard_map/ppermute | solution.py:479
  23.2 1.7 %collective-permute-start.10 = (bf16[2,256,128]{2,1,0:T(8,128)(2,1)S(1)}, bf16[2,256,128]{2,1,0:T(8,128)(2,1)S(1)}, u32[]{:S(2)}, u32[]{:S(2)}) collective-permute-start(bf16[2,256,128]{2,1,0:T(8,128)(2,1)S(1)} %collective-permute-done.3.refs_4_), channel_id=1, source_target_pairs={{0,2},{2,0},{1,3},{3,1},{4,6},{6,4},{5,7},{7,5},{8,10},{10,8},{9,1... | collective-permute-start | bytes 393224 | tf_op jit(solution)/shard_map/ppermute | solution.py:483
  24.9 1.0 %attend.4 = (f32[2048,128]{1,0:T(8,128)S(1)}, f32[2048,128]{1,0:T(8,128)S(1)}, f32[2048,128]{1,0:T(8,128)S(1)}) custom-call(s32[4]{0:T(128)S(1)} %copy-done, s32[4]{0:T(128)S(1)} %copy-done.3, s32[16]{0:T(128)S(1)} %bitcast.13, bf16[2048,128]{1,0:T(8,128)(2,1)S(1)} %bitcast.17, bf16[2,256,128]{2,1,0:T(8,128)(2,1)S(1)} %collective-permute-done.2.refs_4_, ...), custom_call_target="tpu_custom_call" | custom-call | flops 4000000000 | bytes 1048576 | tf_op jit(solution)/shard_map/attend/pallas_call | solution.py:364
  26.0 0.9 %collective-permute-done.6.refs_2_.refs_5_ = bf16[2,256,128]{2,1,0:T(8,128)(2,1)S(1)} collective-permute-done((bf16[2,256,128]{2,1,0:T(8,128)(2,1)S(1)}, bf16[2,256,128]{2,1,0:T(8,128)(2,1)S(1)}, u32[]{:S(2)}, u32[]{:S(2)}) %collective-permute-start.6) | collective-permute-done | bytes 131104 | tf_op jit(solution)/shard_map/ppermute | solution.py:479
  26.8 1.6 %collective-permute-done.10.refs_6_ = bf16[2,256,128]{2,1,0:T(8,128)(2,1)S(1)} collective-permute-done((bf16[2,256,128]{2,1,0:T(8,128)(2,1)S(1)}, bf16[2,256,128]{2,1,0:T(8,128)(2,1)S(1)}, u32[]{:S(2)}, u32[]{:S(2)}) %collective-permute-start.10) | collective-permute-done | bytes 131104 | tf_op jit(solution)/shard_map/ppermute | solution.py:483
  28.4 0.8 %pick_slots.1 = (bf16[8,2,2,32,128]{4,3,2,1,0:T(8,128)(2,1)S(1)}, bf16[8,2,2,32,128]{4,3,2,1,0:T(8,128)(2,1)S(1)}) custom-call(s32[4]{0:T(128)S(1)} %copy-done, s32[16]{0:T(128)S(1)} %bitcast.14, bf16[2,256,128]{2,1,0:T(8,128)(2,1)S(1)} %split_heads.3.refs_0_.refs_5_, bf16[2,256,128]{2,1,0:T(8,128)(2,1)S(1)} %collective-permute-done.4.refs_1_.refs_7_, ...), custom_call_target="tpu_custom_call" | custom-call | tf_op jit(solution)/shard_map/pick_slots/pallas_call | solution.py:439
  29.3 2.8 %attend.5 = bf16[2048,128]{1,0:T(8,128)(2,1)} custom-call(s32[4]{0:T(128)S(1)} %copy-done, s32[4]{0:T(128)S(1)} %copy-done.3, s32[16]{0:T(128)S(1)} %bitcast.15, bf16[2048,128]{1,0:T(8,128)(2,1)S(1)} %bitcast.18, bf16[2,256,128]{2,1,0:T(8,128)(2,1)S(1)} %collective-permute-done.3.refs_4_, bf16[2,256,128]{2,1,0:T(8,128)(2,1)S(1)} %collective-permute-done.6.refs_2_.refs_5_, ...), custom_call_target="tpu_custom_call" | custom-call | flops 4000000000 | bytes 1048576 | tf_op jit(solution)/shard_map/attend/pallas_call | solution.py:364
  32.1 1.0 %place_slots.1 = bf16[2048,128]{1,0:T(8,128)(2,1)} custom-call(bf16[8,2,2,32,128]{4,3,2,1,0:T(8,128)(2,1)S(1)} %get-tuple-element.21.kept_ref, bf16[8,2,2,32,128]{4,3,2,1,0:T(8,128)(2,1)S(1)} %collective-permute-done.12.given_ref), custom_call_target="tpu_custom_call" | custom-call | tf_op jit(solution)/shard_map/place_slots/pallas_call | solution.py:469
  (18 shorter events, 0.5 us)
Async XLA Ops:
  0.6 1.7 %collective-permute-start = (bf16[256,2,128]{2,1,0:T(2,128)(2,1)}, bf16[256,2,128]{2,1,0:T(2,128)(2,1)S(1)}, u32[]{:S(2)}, u32[]{:S(2)}) collective-permute-start(bf16[256,2,128]{2,1,0:T(2,128)(2,1)} %param.7), channel_id=1, source_target_pairs={{0,1},{1,0},{2,3},{3,2},{4,5},{5,4},{6,7},{7,6},{8,9},{9,8},{10,11... | collective-permute-start | bytes 393224 | tf_op jit(solution)/shard_map/ppermute | solution.py:483
  1.1 1.6 %collective-permute-start.1 = (bf16[256,2,128]{2,1,0:T(2,128)(2,1)}, bf16[256,2,128]{2,1,0:T(2,128)(2,1)S(1)}, u32[]{:S(2)}, u32[]{:S(2)}) collective-permute-start(bf16[256,2,128]{2,1,0:T(2,128)(2,1)} %param.8), channel_id=1, source_target_pairs={{0,1},{1,0},{2,3},{3,2},{4,5},{5,4},{6,7},{7,6},{8,9},{9,8},{10,11... | collective-permute-start | bytes 393224 | tf_op jit(solution)/shard_map/ppermute | solution.py:483
  2.8 10.3 %copy-start.2 = (bf16[512,4,128]{2,1,0:T(4,128)(2,1)S(1)}, bf16[512,4,128]{2,1,0:T(4,128)(2,1)}, u32[]{:S(2)}) copy-start(bf16[512,4,128]{2,1,0:T(4,128)(2,1)} %param.6) | copy-start | bytes 1572868
  2.8 9.2 %collective-permute-start.2 = (bf16[2,256,128]{2,1,0:T(8,128)(2,1)S(1)}, bf16[2,256,128]{2,1,0:T(8,128)(2,1)S(1)}, u32[]{:S(2)}, u32[]{:S(2)}) collective-permute-start(bf16[2,256,128]{2,1,0:T(8,128)(2,1)S(1)} %split_heads.2.refs_4_), channel_id=1, source_target_pairs={{0,4},{4,8},{8,12},{12,0},{1,5},{5,9},{9,13},{13,1},{2,6},{6,10},{... | collective-permute-start | bytes 393224 | tf_op jit(solution)/shard_map/ppermute | solution.py:479
  5.7 10.7 %collective-permute-start.5 = (bf16[2,256,128]{2,1,0:T(8,128)(2,1)S(1)}, bf16[2,256,128]{2,1,0:T(8,128)(2,1)S(1)}, u32[]{:S(2)}, u32[]{:S(2)}) collective-permute-start(bf16[2,256,128]{2,1,0:T(8,128)(2,1)S(1)} %split_heads.3.refs_0_.refs_5_), channel_id=1, source_target_pairs={{0,4},{4,8},{8,12},{12,0},{1,5},{5,9},{9,13},{13,1},{2,6},{6,10},{... | collective-permute-start | bytes 393224 | tf_op jit(solution)/shard_map/ppermute | solution.py:479
  7.4 10.0 %collective-permute-start.4 = (bf16[2,256,128]{2,1,0:T(8,128)(2,1)S(1)}, bf16[2,256,128]{2,1,0:T(8,128)(2,1)S(1)}, u32[]{:S(2)}, u32[]{:S(2)}) collective-permute-start(bf16[2,256,128]{2,1,0:T(8,128)(2,1)S(1)} %split_heads.3.refs_0_.refs_5_), channel_id=1, source_target_pairs={{0,12},{4,0},{8,4},{12,8},{1,13},{5,1},{9,5},{13,9},{2,14},{6,2},{... | collective-permute-start | bytes 393224 | tf_op jit(solution)/shard_map/ppermute | solution.py:479
  9.6 10.9 %collective-permute-start.8 = (bf16[2,256,128]{2,1,0:T(8,128)(2,1)S(1)}, bf16[2,256,128]{2,1,0:T(8,128)(2,1)S(1)}, u32[]{:S(2)}, u32[]{:S(2)}) collective-permute-start(bf16[2,256,128]{2,1,0:T(8,128)(2,1)S(1)} %split_heads.2.refs_4_), channel_id=1, source_target_pairs={{0,12},{4,0},{8,4},{12,8},{1,13},{5,1},{9,5},{13,9},{2,14},{6,2},{... | collective-permute-start | bytes 393224 | tf_op jit(solution)/shard_map/ppermute | solution.py:479
  9.9 16.0 %collective-permute-start.7 = (bf16[2,256,128]{2,1,0:T(8,128)(2,1)S(1)}, bf16[2,256,128]{2,1,0:T(8,128)(2,1)S(1)}, u32[]{:S(2)}, u32[]{:S(2)}) collective-permute-start(bf16[2,256,128]{2,1,0:T(8,128)(2,1)S(1)} %split_heads.2.refs_4_), channel_id=1, source_target_pairs={{0,2},{2,0},{1,3},{3,1},{4,6},{6,4},{5,7},{7,5},{8,10},{10,8},{9,1... | collective-permute-start | bytes 393224 | tf_op jit(solution)/shard_map/ppermute | solution.py:483
  12.1 11.1 %collective-permute-start.3 = (bf16[2,256,128]{2,1,0:T(8,128)(2,1)S(1)}, bf16[2,256,128]{2,1,0:T(8,128)(2,1)S(1)}, u32[]{:S(2)}, u32[]{:S(2)}) collective-permute-start(bf16[2,256,128]{2,1,0:T(8,128)(2,1)S(1)} %collective-permute-done.2.refs_4_), channel_id=1, source_target_pairs={{0,4},{4,8},{8,12},{12,0},{1,5},{5,9},{9,13},{13,1},{2,6},{6,10},{... | collective-permute-start | bytes 393224 | tf_op jit(solution)/shard_map/ppermute | solution.py:479
  13.1 0.7 %copy-start = (s32[4]{0:T(128)S(1)}, s32[4]{0:T(128)}, u32[]{:S(2)}) copy-start(s32[4]{0:T(128)} %refs_0_.5) | copy-start | bytes 52
  13.1 0.7 %copy-start.1 = (s32[16,1]{0,1:T(1,128)S(1)}, s32[16,1]{0,1:T(1,128)}, u32[]{:S(2)}) copy-start(s32[16,1]{0,1:T(1,128)} %param.11) | copy-start | bytes 196
  13.1 0.7 %copy-start.3 = (s32[4]{0:T(128)S(1)}, s32[4]{0:T(128)}, u32[]{:S(2)}) copy-start(s32[4]{0:T(128)} %refs_1_.5) | copy-start | bytes 52
  16.4 10.4 %collective-permute-start.11 = (bf16[2,256,128]{2,1,0:T(8,128)(2,1)S(1)}, bf16[2,256,128]{2,1,0:T(8,128)(2,1)S(1)}, u32[]{:S(2)}, u32[]{:S(2)}) collective-permute-start(bf16[2,256,128]{2,1,0:T(8,128)(2,1)S(1)} %collective-permute-done.2.refs_4_), channel_id=1, source_target_pairs={{0,2},{2,0},{1,3},{3,1},{4,6},{6,4},{5,7},{7,5},{8,10},{10,8},{9,1... | collective-permute-start | bytes 393224 | tf_op jit(solution)/shard_map/ppermute | solution.py:483
  17.4 9.5 %collective-permute-start.6 = (bf16[2,256,128]{2,1,0:T(8,128)(2,1)S(1)}, bf16[2,256,128]{2,1,0:T(8,128)(2,1)S(1)}, u32[]{:S(2)}, u32[]{:S(2)}) collective-permute-start(bf16[2,256,128]{2,1,0:T(8,128)(2,1)S(1)} %collective-permute-done.5.refs_3_.refs_5_), channel_id=1, source_target_pairs={{0,4},{4,8},{8,12},{12,0},{1,5},{5,9},{9,13},{13,1},{2,6},{6,10},{... | collective-permute-start | bytes 393224 | tf_op jit(solution)/shard_map/ppermute | solution.py:479
  20.5 6.3 %collective-permute-start.9 = (bf16[2,256,128]{2,1,0:T(8,128)(2,1)S(1)}, bf16[2,256,128]{2,1,0:T(8,128)(2,1)S(1)}, u32[]{:S(2)}, u32[]{:S(2)}) collective-permute-start(bf16[2,256,128]{2,1,0:T(8,128)(2,1)S(1)} %collective-permute-done.8.refs_6_), channel_id=1, source_target_pairs={{0,2},{2,0},{1,3},{3,1},{4,6},{6,4},{5,7},{7,5},{8,10},{10,8},{9,1... | collective-permute-start | bytes 393224 | tf_op jit(solution)/shard_map/ppermute | solution.py:483
  23.2 5.2 %collective-permute-start.10 = (bf16[2,256,128]{2,1,0:T(8,128)(2,1)S(1)}, bf16[2,256,128]{2,1,0:T(8,128)(2,1)S(1)}, u32[]{:S(2)}, u32[]{:S(2)}) collective-permute-start(bf16[2,256,128]{2,1,0:T(8,128)(2,1)S(1)} %collective-permute-done.3.refs_4_), channel_id=1, source_target_pairs={{0,2},{2,0},{1,3},{3,1},{4,6},{6,4},{5,7},{7,5},{8,10},{10,8},{9,1... | collective-permute-start | bytes 393224 | tf_op jit(solution)/shard_map/ppermute | solution.py:483
  29.2 2.9 %collective-permute-start.12 = (bf16[8,2,2,32,128]{4,3,2,1,0:T(8,128)(2,1)S(1)}, bf16[8,2,2,32,128]{4,3,2,1,0:T(8,128)(2,1)S(1)}, u32[]{:S(2)}, u32[]{:S(2)}) collective-permute-start(bf16[8,2,2,32,128]{4,3,2,1,0:T(8,128)(2,1)S(1)} %get-tuple-element.13), channel_id=1, source_target_pairs={{0,1},{1,0},{2,3},{3,2},{4,5},{5,4},{6,7},{7,6},{8,9},{9,8},{10,11... | collective-permute-start | bytes 786440 | tf_op jit(solution)/shard_map/ppermute | solution.py:483

commit v6 on v5

--- a/solution.py
+++ b/solution.py
@@ -184,6 +184,7 @@
 COST_FLOPS = 4 * 10**9
 Q_TILE = 1024
 STRIP = 512
+PLACE_GROUPS = 4
 
 
 def split_kernel(cross, own_ref, key_other, value_other, out_ref, wide):
@@ -215,9 +216,9 @@
     order_ref, lengths_ref, _, query_ref = refs[:4]
     refs = refs[4:]
     pieces = []
-    for _ in sources:
-        pieces.append((refs[0], refs[1]))
-        refs = refs[2:]
+    for _, kinds in sources:
+        pieces.append(refs[: len(kinds)])
+        refs = refs[len(kinds) :]
     if not first:
         peak_in, total_in, summed_in = refs[:3]
         refs = refs[3:]
@@ -226,7 +227,14 @@
     else:
         peak_out, total_out, summed_out = refs[:3]
         refs = refs[3:]
-    values_ref, top_ref, total_ref, summed_ref = refs
+    values_ref, top_ref, total_ref, summed_ref = refs[:4]
+    if last:
+        result_ref, sems = refs[4:]
+
+    def send_strip(number):
+        at = pl.ds(pl.multiple_of(number * STRIP, STRIP), STRIP)
+        return pltpu.make_async_copy(result_ref.at[at, :], out_ref.at[at, :], sems.at[number])
+
     shard = lax.axis_index("ctx")
     pair = lax.axis_index("pair")
     rows, width = query_ref.shape
@@ -243,24 +251,20 @@
         return begin
 
     spans = []
-    for shift, (cross, stay) in zip(sources, pieces):
+    part_keys = pieces[0][0].shape[1] // 2
+    in_part = lax.broadcasted_iota(jnp.int32, (1, part_keys), 1)
+    in_part = in_part + jnp.where(in_part >= HALF_TOKENS, BLK - HALF_TOKENS, 0)
+    local_of = {True: in_part + HALF_TOKENS * (1 - pair), False: in_part + HALF_TOKENS * pair}
+    for number, ((shift, kinds), held) in enumerate(zip(sources, pieces)):
         lead = order_ref[lax.rem(shard + shift, span_total // 2)]
-        spans.append((lead, cross, stay, 0))
-        spans.append((span_total - 1 - lead, cross, stay, 1))
-    part_keys = pieces[0][0].shape[1] // 2
-    keys_each = 2 * part_keys
-    for number, (_, cross, stay, half) in enumerate(spans):
-        for which, piece in enumerate((cross, stay)):
-            values_ref[number, pl.ds(which * part_keys, part_keys), :] = piece[
-                1, pl.ds(half * part_keys, part_keys), :
-            ]
-    lane = lax.broadcasted_iota(jnp.int32, (1, keys_each), 1)
-    in_part = lax.rem(lane, part_keys)
-    local = (
-        in_part
-        + jnp.where(in_part >= HALF_TOKENS, BLK - HALF_TOKENS, 0)
-        + HALF_TOKENS * jnp.where(lane < part_keys, 1 - pair, pair)
-    )
+        parts = []
+        for half, span in enumerate((lead, span_total - 1 - lead)):
+            part = pl.ds(half * part_keys, part_keys)
+            for piece, kind in zip(held, kinds):
+                parts.append((piece, part, span * half_rows + local_of[kind]))
+                row = (len(parts) - 1) * part_keys
+                values_ref[number, pl.ds(row, part_keys), :] = piece[1, part, :]
+        spans.append((lead, span_total - 1 - lead, parts))
 
     tile_tokens = Q_TILE // heads
     tiles_half = half_rows // tile_tokens
@@ -272,27 +276,52 @@
         first_pos = query_span * half_rows + lax.rem(index, tiles_half) * tile_tokens
         begin_low = begin_of(first_pos)
         near = []
-        for span, _, _, _ in spans:
-            near.append(
+        for leading, trailing, parts in spans:
+            lead_near, trail_near = (
                 (span * half_rows <= first_pos + tile_tokens - 1)
                 & (span * half_rows + half_rows - 1 >= begin_low)
+                for span in (leading, trailing)
             )
-        if first:
-            top_ref[...] = jnp.full(top_ref.shape, FLOOR, jnp.float32)
-            total_ref[...] = jnp.zeros(total_ref.shape, jnp.float32)
-            summed_ref[...] = jnp.zeros(summed_ref.shape, jnp.float32)
-        else:
-            top_ref[...] = peak_in[at, :]
-            total_ref[...] = total_in[at, :]
-            summed_ref[...] = summed_in[at, :]
-
-        for number, (span, cross, stay, half) in enumerate(spans):
-
-            @pl.when(near[number])
+            middle = len(parts) // 2
+            near.append((lead_near & trail_near, 0, 2 * middle))
+            near.append((lead_near & jnp.logical_not(trail_near), 0, middle))
+            near.append((trail_near & jnp.logical_not(lead_near), middle, 2 * middle))
+            near.append((jnp.logical_not(lead_near | trail_near), 0, 0))
+
+        def state_of(number, strip, rows_at):
+            if number > 0:
+                return top_ref[strip, :], total_ref[strip, :], summed_ref[strip, :]
+            if not first:
+                return peak_in[rows_at, :], total_in[rows_at, :], summed_in[rows_at, :]
+            empty = jnp.zeros((STRIP, width), jnp.float32)
+            return empty + FLOOR, empty, empty
+
+        def put_state(number, strip, rows_at, state):
+            if number < len(spans) - 1:
+                top_ref[strip, :], total_ref[strip, :], summed_ref[strip, :] = state
+            elif last:
+                whole = jnp.sum(state[1], axis=1, keepdims=True)
+                result_ref[rows_at, :] = (state[2] / whole).astype(jnp.bfloat16)
+            else:
+                peak_out[rows_at, :], total_out[rows_at, :], summed_out[rows_at, :] = state
+
+        for branch, (seen, start, end) in enumerate(near):
+            number = branch // 4
+            parts = spans[number][2][start:end]
+            values_at = pl.ds(start * part_keys, (end - start) * part_keys)
+
+            @pl.when(seen)
             def _():
-                part = pl.ds(half * part_keys, part_keys)
-                keys = jnp.concatenate([cross[0, part, :], stay[0, part, :]], axis=0)
-                key_pos = span * half_rows + local
+                if not parts:
+                    if 0 < number < len(spans) - 1:
+                        return
+                    for row in range(0, Q_TILE, STRIP):
+                        strip = pl.ds(row, STRIP)
+                        rows_at = pl.ds(pl.multiple_of(index * Q_TILE + row, STRIP), STRIP)
+                        put_state(number, strip, rows_at, state_of(number, strip, rows_at))
+                    return
+                keys = jnp.concatenate([piece[0, part, :] for piece, part, _ in parts], axis=0)
+                key_pos = [positions for _, _, positions in parts]
                 index_in = lax.broadcasted_iota(jnp.int32, (STRIP, width), 0) // heads
                 for row in range(0, Q_TILE, STRIP):
                     strip = pl.ds(row, STRIP)
@@ -305,11 +334,11 @@
                     )
                     query_pos = first_pos + row // heads + index_in
                     query_begin = begin_of(query_pos)
-                    old = top_ref[strip, :]
+                    old, total, summed = state_of(number, strip, rows_at)
                     top = old
                     masked = []
-                    for column in range(0, keys_each, width):
-                        at_key = key_pos[:, column : column + width]
+                    for which, at_key in enumerate(key_pos):
+                        column = which * width
                         visible = (at_key <= query_pos) & (at_key >= query_begin)
                         masked.append(
                             jnp.where(visible, score[:, column : column + width], MASKED)
@@ -318,32 +347,29 @@
                     peak = jnp.broadcast_to(
                         jnp.max(top, axis=1, keepdims=True), (STRIP, width)
                     )
-                    top_ref[strip, :] = peak
                     fade = jnp.exp2((old - peak) * factor)
-                    total = total_ref[strip, :] * fade
+                    total = total * fade
                     weights = []
                     for part_score in masked:
                         weight = jnp.exp2((part_score - peak) * factor)
                         total = total + weight
                         weights.append(weight.astype(jnp.bfloat16))
-                    total_ref[strip, :] = total
-                    summed_ref[strip, :] = summed_ref[strip, :] * fade + jnp.dot(
+                    summed = summed * fade + jnp.dot(
                         jnp.concatenate(weights, axis=1),
-                        values_ref[number],
+                        values_ref[number, values_at, :],
                         preferred_element_type=jnp.float32,
                     )
-
-        if not last:
-            peak_out[at, :] = top_ref[...]
+                    put_state(number, strip, rows_at, (peak, total, summed))
+
         if last:
-            total = jnp.sum(total_ref[...], axis=1, keepdims=True)
-            out_ref[at, :] = (summed_ref[...] / total).astype(jnp.bfloat16)
-        else:
-            total_out[at, :] = total_ref[...]
-            summed_out[at, :] = summed_ref[...]
+            for number in range(Q_TILE // STRIP):
+                send_strip(index * (Q_TILE // STRIP) + number).start()
         return 0
 
     lax.fori_loop(0, rows // Q_TILE, tile, 0)
+    if last:
+        for number in range(rows // STRIP):
+            send_strip(number).wait()
 
 
 def attend(order, lengths, partner, query, pieces, sources, state, last, heads):
@@ -354,12 +380,17 @@
     state = () if first else state
     if last:
         out_shape = jax.ShapeDtypeStruct((rows, width), jnp.bfloat16)
-        out_specs = vmem
+        out_specs = pl.BlockSpec(memory_space=pltpu.HBM)
+        sending = [
+            pltpu.VMEM((rows, width), jnp.bfloat16),
+            pltpu.SemaphoreType.DMA((rows // STRIP,)),
+        ]
     else:
+        sending = []
         out_shape = (jax.ShapeDtypeStruct((rows, width), jnp.float32),) * 3
         out_specs = (vmem,) * 3
     keys_each = pieces[0].shape[-2]
-    count = 2 * len(sources)
+    count = len(sources)
     tile = pltpu.VMEM((Q_TILE, width), jnp.float32)
     return pl.pallas_call(
         functools.partial(attend_kernel, sources, first, last, 2 * order.shape[0], heads),
@@ -367,11 +398,12 @@
         in_specs=[smem] * 3 + [vmem] * (1 + len(pieces) + len(state)),
         out_specs=out_specs,
         scratch_shapes=[
-            pltpu.VMEM((count, keys_each, width), jnp.bfloat16),
+            pltpu.VMEM((count, 2 * keys_each, width), jnp.bfloat16),
             tile,
             tile,
             tile,
-        ],
+        ]
+        + sending,
         cost_estimate=pl.CostEstimate(
             flops=COST_FLOPS, bytes_accessed=4 * rows * width, transcendentals=0
         ),
@@ -450,18 +482,27 @@
     )(order, partner, *stay, *cross)
 
 
-def place_kernel(kept_ref, given_ref, out_ref, wide):
+def place_kernel(kept_ref, given_ref, out_ref, wide, result, sems):
     pair = lax.axis_index("pair")
     core = lax.axis_index("tp")
     share = kept_ref.shape[3]
-    for slot in range(CAP):
-        for kind in range(2):
-            for which in range(2):
-                base = (slot * 2 + kind) * share * 4 + 2 * (pair if which == 0 else 1 - pair)
-                for ref, head in ((kept_ref, core), (given_ref, 1 - core)):
-                    rows = ref[slot, kind, which].astype(jnp.float32)
-                    wide[pl.ds(base + head, share, stride=4), :] = rows
-    out_ref[...] = wide[...].astype(jnp.bfloat16)
+    group_rows = wide.shape[0] // PLACE_GROUPS
+    slots = CAP // PLACE_GROUPS
+    copies = []
+    for number in range(PLACE_GROUPS):
+        for slot in range(number * slots, (number + 1) * slots):
+            for kind in range(2):
+                for which in range(2):
+                    base = (slot * 2 + kind) * share * 4 + 2 * (pair if which == 0 else 1 - pair)
+                    for ref, head in ((kept_ref, core), (given_ref, 1 - core)):
+                        rows = ref[slot, kind, which].astype(jnp.float32)
+                        wide[pl.ds(base + head, share, stride=4), :] = rows
+        at = pl.ds(number * group_rows, group_rows)
+        result[at, :] = wide[at, :].astype(jnp.bfloat16)
+        copies.append(pltpu.make_async_copy(result.at[at, :], out_ref.at[at, :], sems.at[number]))
+        copies[-1].start()
+    for copy in copies:
+        copy.wait()
 
 
 def place(kept, given):
@@ -469,7 +510,12 @@
     return pl.pallas_call(
         place_kernel,
         out_shape=jax.ShapeDtypeStruct((rows, width), jnp.bfloat16),
-        scratch_shapes=[pltpu.VMEM((rows, width), jnp.float32)],
+        out_specs=pl.BlockSpec(memory_space=pltpu.HBM),
+        scratch_shapes=[
+            pltpu.VMEM((rows, width), jnp.float32),
+            pltpu.VMEM((rows, width), jnp.bfloat16),
+            pltpu.SemaphoreType.DMA((PLACE_GROUPS,)),
+        ],
         compiler_params=pltpu.CompilerParams(vmem_limit_bytes=12 * 2**20),
         name="place_slots",
     )(kept, given)
@@ -504,24 +550,25 @@
     def step(pieces, sources, state, last=False):
         return attend(span_order, lengths, partner, query, pieces, sources, state, last, heads)
 
+    both = (True, False)
     cross3 = ring(cross0, 1, count)
     cross1 = ring(cross0, -1, count)
     stay3 = ring(stay0, 1, count)
     stay1 = ring(stay0, -1, count)
     over0 = swap(cross0, "pair")
-    state = step((cross0, stay0), (0,), None)
+    state = step((cross0, stay0), ((0, both),), None)
     cross2 = ring(cross3, 1, count)
     over3 = swap(cross3, "pair")
     over1 = swap(cross1, "pair")
     stay2 = ring(stay3, 1, count)
-    state = step((cross3, stay3, cross1, stay1), (3, 1), state)
+    state = step((cross3, stay3, cross1, stay1), ((3, both), (1, both)), state)
     over2 = swap(cross2, "pair")
     stay = (stay0, stay1, stay2, stay3)
     over = (over0, over1, over2, over3)
     picked, kept = pick(span_order, partner, stay, over)
     given = swap(picked, "tp")
     cross2, _ = after(cross2, picked)
-    attended = step((cross2, stay2), (2,), state, True)
+    attended = step((cross2, stay2), ((2, both),), state, True)
     cache = place(kept, given)
     return attended.reshape(queries.shape), cache.reshape(CAP, 2, HALF_TOKENS // 2, 4, width)
 

time: 33.4 us -> 32.9 us (0.985); the launches traced: 33.1 us -> 32.2 us
  waiting for transfers between devices: 4.8 us -> 3.69 us
    ppermute x7, waiting for transfers between devices: 2.06 us -> 1.43 us  [swap(): return lax.ppermute(array, axis, [(0, 1), (1, 0)])]
    ppermute x6, waiting for transfers between devices: 2.74 us -> 2.26 us  [ring(): lax.ppermute(array, 'ctx', [(i, (i + step) % count) for i in range(count)])]
  transfers between devices with their start and end apart: 13 -> 13, of which waited for: 7 -> 6; matrix products, arithmetic and copies ran while one was open for 3% -> 3% of each run, Pallas kernels for 20% -> 20%
where the time goes in v6:
time: 32.9 us; the launch traced here: 32.2 us
  starting transfers between devices  17.5 us (53%)
  Pallas kernels  8.38 us (25%)
  waiting for transfers between devices  3.69 us (11%)
  other arithmetic  1 us (3%)
  between operations  0.91 us (3%)
  local copies, waits for them, and re-layouts  0.69 us (2%)
    ppermute x6, starting transfers between devices, ring(): lax.ppermute(array, 'ctx', [(i, (i + step) % count) for i in range(count)])  11.2 us
    pallas_call x3, Pallas kernels, attend(): pl.pallas_call(functools.partial(attend_kernel, sources, first, last, 2 *...  6.47 us
    ppermute x7, starting transfers between devices, swap(): return lax.ppermute(array, axis, [(0, 1), (1, 0)])  6.3 us
    ppermute x6, waiting for transfers between devices, ring(): lax.ppermute(array, 'ctx', [(i, (i + step) % count) for i in range(count)])  2.26 us
    ppermute x7, waiting for transfers between devices, swap(): return lax.ppermute(array, axis, [(0, 1), (1, 0)])  1.43 us
    convert_element_type x1, other arithmetic, pieces_program(): own = jnp.stack([keys_flat, values_flat]).astype(jnp.float32)  1 us
    pallas_call x1, Pallas kernels, place(): pl.pallas_call(place_kernel, out_shape=jax.ShapeDtypeStruct((rows, width)...  0.93 us
    pallas_call x1, Pallas kernels, pick(): pl.pallas_call(pick_kernel, out_shape=(rows, rows), in_specs=[smem, smem]...  0.8 us
  transfers between devices with their start and end apart: 13, of which 6 were waited for; matrix products, arithmetic and copies ran while one was open for 3% of the time, Pallas kernels for 20%

profile of v6, /device:TPU:0, one launch (start us, length us, event | category | flops | bytes accessed | tf_op | source)
XLA Modules:
  0.0 32.2 jit_solution(7515124253843805670)
XLA Ops:
  0.6 0.5 %collective-permute-start = (bf16[256,2,128]{2,1,0:T(2,128)(2,1)}, bf16[256,2,128]{2,1,0:T(2,128)(2,1)S(1)}, u32[]{:S(2)}, u32[]{:S(2)}) collective-permute-start(bf16[256,2,128]{2,1,0:T(2,128)(2,1)} %param.7), channel_id=1, source_target_pairs={{0,1},{1,0},{2,3},{3,2},{4,5},{5,4},{6,7},{7,6},{8,9},{9,8},{10,11... | collective-permute-start | bytes 393224 | tf_op jit(solution)/shard_map/ppermute | solution.py:529
  1.2 1.0 %maximum_convert_fusion.own_ref = f32[2,512,128]{2,1,0:T(8,128)S(1)} fusion(bf16[1,512,128]{2,1,0:T(8,128)(2,1)} %bitcast.21, bf16[1,512,128]{2,1,0:T(8,128)(2,1)} %bitcast.20), kind=kLoop, calls=%fused_computation | loop fusion | flops 262144 | bytes 786432 | tf_op jit(solution)/shard_map/convert_element_type | solution.py:545
  2.2 0.1 collective-permute-done
  2.3 0.4 %collective-permute-done.1 = bf16[256,2,128]{2,1,0:T(2,128)(2,1)S(1)} collective-permute-done((bf16[256,2,128]{2,1,0:T(2,128)(2,1)}, bf16[256,2,128]{2,1,0:T(2,128)(2,1)S(1)}, u32[]{:S(2)}, u32[]{:S(2)}) %collective-permute-start.1) | collective-permute-done | bytes 131104 | tf_op jit(solution)/shard_map/ppermute | solution.py:529
  2.8 2.8 %collective-permute-start.2 = (bf16[2,256,128]{2,1,0:T(8,128)(2,1)S(1)}, bf16[2,256,128]{2,1,0:T(8,128)(2,1)S(1)}, u32[]{:S(2)}, u32[]{:S(2)}) collective-permute-start(bf16[2,256,128]{2,1,0:T(8,128)(2,1)S(1)} %split_heads.2.refs_4_), channel_id=1, source_target_pairs={{0,4},{4,8},{8,12},{12,0},{1,5},{5,9},{9,13},{13,1},{2,6},{6,10},{... | collective-permute-start | bytes 393224 | tf_op jit(solution)/shard_map/ppermute | solution.py:525
  5.7 1.6 %collective-permute-start.5 = (bf16[2,256,128]{2,1,0:T(8,128)(2,1)S(1)}, bf16[2,256,128]{2,1,0:T(8,128)(2,1)S(1)}, u32[]{:S(2)}, u32[]{:S(2)}) collective-permute-start(bf16[2,256,128]{2,1,0:T(8,128)(2,1)S(1)} %split_heads.3.refs_0_.refs_5_), channel_id=1, source_target_pairs={{0,4},{4,8},{8,12},{12,0},{1,5},{5,9},{9,13},{13,1},{2,6},{6,10},{... | collective-permute-start | bytes 393224 | tf_op jit(solution)/shard_map/ppermute | solution.py:525
  7.4 2.2 %collective-permute-start.4 = (bf16[2,256,128]{2,1,0:T(8,128)(2,1)S(1)}, bf16[2,256,128]{2,1,0:T(8,128)(2,1)S(1)}, u32[]{:S(2)}, u32[]{:S(2)}) collective-permute-start(bf16[2,256,128]{2,1,0:T(8,128)(2,1)S(1)} %split_heads.3.refs_0_.refs_5_), channel_id=1, source_target_pairs={{0,12},{4,0},{8,4},{12,8},{1,13},{5,1},{9,5},{13,9},{2,14},{6,2},{... | collective-permute-start | bytes 393224 | tf_op jit(solution)/shard_map/ppermute | solution.py:525
  9.6 0.3 collective-permute-start.8
  9.9 1.6 %collective-permute-start.7 = (bf16[2,256,128]{2,1,0:T(8,128)(2,1)S(1)}, bf16[2,256,128]{2,1,0:T(8,128)(2,1)S(1)}, u32[]{:S(2)}, u32[]{:S(2)}) collective-permute-start(bf16[2,256,128]{2,1,0:T(8,128)(2,1)S(1)} %split_heads.2.refs_4_), channel_id=1, source_target_pairs={{0,2},{2,0},{1,3},{3,1},{4,6},{6,4},{5,7},{7,5},{8,10},{10,8},{9,1... | collective-permute-start | bytes 393224 | tf_op jit(solution)/shard_map/ppermute | solution.py:529
  11.5 0.5 %collective-permute-done.2.refs_4_ = bf16[2,256,128]{2,1,0:T(8,128)(2,1)S(1)} collective-permute-done((bf16[2,256,128]{2,1,0:T(8,128)(2,1)S(1)}, bf16[2,256,128]{2,1,0:T(8,128)(2,1)S(1)}, u32[]{:S(2)}, u32[]{:S(2)}) %collective-permute-start.2) | collective-permute-done | bytes 131104 | tf_op jit(solution)/shard_map/ppermute | solution.py:525
  12.1 1.1 %collective-permute-start.3 = (bf16[2,256,128]{2,1,0:T(8,128)(2,1)S(1)}, bf16[2,256,128]{2,1,0:T(8,128)(2,1)S(1)}, u32[]{:S(2)}, u32[]{:S(2)}) collective-permute-start(bf16[2,256,128]{2,1,0:T(8,128)(2,1)S(1)} %collective-permute-done.2.refs_4_), channel_id=1, source_target_pairs={{0,4},{4,8},{8,12},{12,0},{1,5},{5,9},{9,13},{13,1},{2,6},{6,10},{... | collective-permute-start | bytes 393224 | tf_op jit(solution)/shard_map/ppermute | solution.py:525
  13.1 0.6 %copy-done = s32[4]{0:T(128)S(1)} copy-done((s32[4]{0:T(128)S(1)}, s32[4]{0:T(128)}, u32[]{:S(2)}) %copy-start) | copy-done | bytes 40
  13.8 2.2 %attend.3 = (f32[2048,128]{1,0:T(8,128)S(1)}, f32[2048,128]{1,0:T(8,128)S(1)}, f32[2048,128]{1,0:T(8,128)S(1)}) custom-call(s32[4]{0:T(128)S(1)} %copy-done, s32[4]{0:T(128)S(1)} %copy-done.3, s32[16]{0:T(128)S(1)} %bitcast.12, bf16[2048,128]{1,0:T(8,128)(2,1)S(1)} %bitcast.16, bf16[2,256,128]{2,1,0:T(8,128)(2,1)S(1)} %split_heads.2.refs_4_, ...), custom_call_target="tpu_custom_call" | custom-call | flops 4000000000 | bytes 1048576 | tf_op jit(solution)/shard_map/attend/pallas_call | solution.py:395
  16.0 0.7 %collective-permute-start.11 = (bf16[2,256,128]{2,1,0:T(8,128)(2,1)S(1)}, bf16[2,256,128]{2,1,0:T(8,128)(2,1)S(1)}, u32[]{:S(2)}, u32[]{:S(2)}) collective-permute-start(bf16[2,256,128]{2,1,0:T(8,128)(2,1)S(1)} %collective-permute-done.2.refs_4_), channel_id=1, source_target_pairs={{0,2},{2,0},{1,3},{3,1},{4,6},{6,4},{5,7},{7,5},{8,10},{10,8},{9,1... | collective-permute-start | bytes 393224 | tf_op jit(solution)/shard_map/ppermute | solution.py:529
  16.8 0.6 %collective-permute-done.4.refs_1_.refs_7_ = bf16[2,256,128]{2,1,0:T(8,128)(2,1)S(1)} collective-permute-done((bf16[2,256,128]{2,1,0:T(8,128)(2,1)S(1)}, bf16[2,256,128]{2,1,0:T(8,128)(2,1)S(1)}, u32[]{:S(2)}, u32[]{:S(2)}) %collective-permute-start.4) | collective-permute-done | bytes 131104 | tf_op jit(solution)/shard_map/ppermute | solution.py:525
  17.4 3.2 %collective-permute-start.6 = (bf16[2,256,128]{2,1,0:T(8,128)(2,1)S(1)}, bf16[2,256,128]{2,1,0:T(8,128)(2,1)S(1)}, u32[]{:S(2)}, u32[]{:S(2)}) collective-permute-start(bf16[2,256,128]{2,1,0:T(8,128)(2,1)S(1)} %collective-permute-done.5.refs_3_.refs_5_), channel_id=1, source_target_pairs={{0,4},{4,8},{8,12},{12,0},{1,5},{5,9},{9,13},{13,1},{2,6},{6,10},{... | collective-permute-start | bytes 393224 | tf_op jit(solution)/shard_map/ppermute | solution.py:525
  20.5 1.5 %collective-permute-start.9 = (bf16[2,256,128]{2,1,0:T(8,128)(2,1)S(1)}, bf16[2,256,128]{2,1,0:T(8,128)(2,1)S(1)}, u32[]{:S(2)}, u32[]{:S(2)}) collective-permute-start(bf16[2,256,128]{2,1,0:T(8,128)(2,1)S(1)} %collective-permute-done.8.refs_6_), channel_id=1, source_target_pairs={{0,2},{2,0},{1,3},{3,1},{4,6},{6,4},{5,7},{7,5},{8,10},{10,8},{9,1... | collective-permute-start | bytes 393224 | tf_op jit(solution)/shard_map/ppermute | solution.py:529
  22.0 1.2 %collective-permute-done.3.refs_4_ = bf16[2,256,128]{2,1,0:T(8,128)(2,1)S(1)} collective-permute-done((bf16[2,256,128]{2,1,0:T(8,128)(2,1)S(1)}, bf16[2,256,128]{2,1,0:T(8,128)(2,1)S(1)}, u32[]{:S(2)}, u32[]{:S(2)}) %collective-permute-start.3) | collective-permute-done | bytes 131104 | tf_op jit(solution)/shard_map/ppermute | solution.py:525
  23.2 1.7 %collective-permute-start.10 = (bf16[2,256,128]{2,1,0:T(8,128)(2,1)S(1)}, bf16[2,256,128]{2,1,0:T(8,128)(2,1)S(1)}, u32[]{:S(2)}, u32[]{:S(2)}) collective-permute-start(bf16[2,256,128]{2,1,0:T(8,128)(2,1)S(1)} %collective-permute-done.3.refs_4_), channel_id=1, source_target_pairs={{0,2},{2,0},{1,3},{3,1},{4,6},{6,4},{5,7},{7,5},{8,10},{10,8},{9,1... | collective-permute-start | bytes 393224 | tf_op jit(solution)/shard_map/ppermute | solution.py:529
  24.9 2.5 %attend.4 = (f32[2048,128]{1,0:T(8,128)S(1)}, f32[2048,128]{1,0:T(8,128)S(1)}, f32[2048,128]{1,0:T(8,128)S(1)}) custom-call(s32[4]{0:T(128)S(1)} %copy-done, s32[4]{0:T(128)S(1)} %copy-done.3, s32[16]{0:T(128)S(1)} %bitcast.13, bf16[2048,128]{1,0:T(8,128)(2,1)S(1)} %bitcast.17, bf16[2,256,128]{2,1,0:T(8,128)(2,1)S(1)} %collective-permute-done.2.refs_4_, ...), custom_call_target="tpu_custom_call" | custom-call | flops 4000000000 | bytes 1048576 | tf_op jit(solution)/shard_map/attend/pallas_call | solution.py:395
  27.5 0.9 %collective-permute-done.10.refs_6_ = bf16[2,256,128]{2,1,0:T(8,128)(2,1)S(1)} collective-permute-done((bf16[2,256,128]{2,1,0:T(8,128)(2,1)S(1)}, bf16[2,256,128]{2,1,0:T(8,128)(2,1)S(1)}, u32[]{:S(2)}, u32[]{:S(2)}) %collective-permute-start.10) | collective-permute-done | bytes 131104 | tf_op jit(solution)/shard_map/ppermute | solution.py:529
  28.4 0.8 %pick_slots.1 = (bf16[8,2,2,32,128]{4,3,2,1,0:T(8,128)(2,1)S(1)}, bf16[8,2,2,32,128]{4,3,2,1,0:T(8,128)(2,1)S(1)}) custom-call(s32[4]{0:T(128)S(1)} %copy-done, s32[16]{0:T(128)S(1)} %bitcast.14, bf16[2,256,128]{2,1,0:T(8,128)(2,1)S(1)} %split_heads.3.refs_0_.refs_5_, bf16[2,256,128]{2,1,0:T(8,128)(2,1)S(1)} %collective-permute-done.4.refs_1_.refs_7_, ...), custom_call_target="tpu_custom_call" | custom-call | tf_op jit(solution)/shard_map/pick_slots/pallas_call | solution.py:471
  29.3 1.8 %attend.5 = bf16[2048,128]{1,0:T(8,128)(2,1)} custom-call(s32[4]{0:T(128)S(1)} %copy-done, s32[4]{0:T(128)S(1)} %copy-done.3, s32[16]{0:T(128)S(1)} %bitcast.15, bf16[2048,128]{1,0:T(8,128)(2,1)S(1)} %bitcast.18, bf16[2,256,128]{2,1,0:T(8,128)(2,1)S(1)} %collective-permute-done.3.refs_4_, bf16[2,256,128]{2,1,0:T(8,128)(2,1)S(1)} %collective-permute-done.6.refs_2_.refs_5_, ...), custom_call_target="tpu_custom_call" | custom-call | flops 4000000000 | bytes 1048576 | tf_op jit(solution)/shard_map/attend/pallas_call | solution.py:395
  31.1 0.9 %place_slots.1 = bf16[2048,128]{1,0:T(8,128)(2,1)} custom-call(bf16[8,2,2,32,128]{4,3,2,1,0:T(8,128)(2,1)S(1)} %get-tuple-element.21.kept_ref, bf16[8,2,2,32,128]{4,3,2,1,0:T(8,128)(2,1)S(1)} %collective-permute-done.12.given_ref), custom_call_target="tpu_custom_call" | custom-call | tf_op jit(solution)/shard_map/place_slots/pallas_call | solution.py:510
  (18 shorter events, 0.4 us)
Async XLA Ops:
  0.6 1.7 %collective-permute-start = (bf16[256,2,128]{2,1,0:T(2,128)(2,1)}, bf16[256,2,128]{2,1,0:T(2,128)(2,1)S(1)}, u32[]{:S(2)}, u32[]{:S(2)}) collective-permute-start(bf16[256,2,128]{2,1,0:T(2,128)(2,1)} %param.7), channel_id=1, source_target_pairs={{0,1},{1,0},{2,3},{3,2},{4,5},{5,4},{6,7},{7,6},{8,9},{9,8},{10,11... | collective-permute-start | bytes 393224 | tf_op jit(solution)/shard_map/ppermute | solution.py:529
  1.1 1.6 %collective-permute-start.1 = (bf16[256,2,128]{2,1,0:T(2,128)(2,1)}, bf16[256,2,128]{2,1,0:T(2,128)(2,1)S(1)}, u32[]{:S(2)}, u32[]{:S(2)}) collective-permute-start(bf16[256,2,128]{2,1,0:T(2,128)(2,1)} %param.8), channel_id=1, source_target_pairs={{0,1},{1,0},{2,3},{3,2},{4,5},{5,4},{6,7},{7,6},{8,9},{9,8},{10,11... | collective-permute-start | bytes 393224 | tf_op jit(solution)/shard_map/ppermute | solution.py:529
  2.8 10.3 %copy-start.2 = (bf16[512,4,128]{2,1,0:T(4,128)(2,1)S(1)}, bf16[512,4,128]{2,1,0:T(4,128)(2,1)}, u32[]{:S(2)}) copy-start(bf16[512,4,128]{2,1,0:T(4,128)(2,1)} %param.6) | copy-start | bytes 1572868
  2.8 9.2 %collective-permute-start.2 = (bf16[2,256,128]{2,1,0:T(8,128)(2,1)S(1)}, bf16[2,256,128]{2,1,0:T(8,128)(2,1)S(1)}, u32[]{:S(2)}, u32[]{:S(2)}) collective-permute-start(bf16[2,256,128]{2,1,0:T(8,128)(2,1)S(1)} %split_heads.2.refs_4_), channel_id=1, source_target_pairs={{0,4},{4,8},{8,12},{12,0},{1,5},{5,9},{9,13},{13,1},{2,6},{6,10},{... | collective-permute-start | bytes 393224 | tf_op jit(solution)/shard_map/ppermute | solution.py:525
  5.7 10.3 %collective-permute-start.5 = (bf16[2,256,128]{2,1,0:T(8,128)(2,1)S(1)}, bf16[2,256,128]{2,1,0:T(8,128)(2,1)S(1)}, u32[]{:S(2)}, u32[]{:S(2)}) collective-permute-start(bf16[2,256,128]{2,1,0:T(8,128)(2,1)S(1)} %split_heads.3.refs_0_.refs_5_), channel_id=1, source_target_pairs={{0,4},{4,8},{8,12},{12,0},{1,5},{5,9},{9,13},{13,1},{2,6},{6,10},{... | collective-permute-start | bytes 393224 | tf_op jit(solution)/shard_map/ppermute | solution.py:525
  7.4 10.0 %collective-permute-start.4 = (bf16[2,256,128]{2,1,0:T(8,128)(2,1)S(1)}, bf16[2,256,128]{2,1,0:T(8,128)(2,1)S(1)}, u32[]{:S(2)}, u32[]{:S(2)}) collective-permute-start(bf16[2,256,128]{2,1,0:T(8,128)(2,1)S(1)} %split_heads.3.refs_0_.refs_5_), channel_id=1, source_target_pairs={{0,12},{4,0},{8,4},{12,8},{1,13},{5,1},{9,5},{13,9},{2,14},{6,2},{... | collective-permute-start | bytes 393224 | tf_op jit(solution)/shard_map/ppermute | solution.py:525
  9.6 10.9 %collective-permute-start.8 = (bf16[2,256,128]{2,1,0:T(8,128)(2,1)S(1)}, bf16[2,256,128]{2,1,0:T(8,128)(2,1)S(1)}, u32[]{:S(2)}, u32[]{:S(2)}) collective-permute-start(bf16[2,256,128]{2,1,0:T(8,128)(2,1)S(1)} %split_heads.2.refs_4_), channel_id=1, source_target_pairs={{0,12},{4,0},{8,4},{12,8},{1,13},{5,1},{9,5},{13,9},{2,14},{6,2},{... | collective-permute-start | bytes 393224 | tf_op jit(solution)/shard_map/ppermute | solution.py:525
  9.9 17.5 %collective-permute-start.7 = (bf16[2,256,128]{2,1,0:T(8,128)(2,1)S(1)}, bf16[2,256,128]{2,1,0:T(8,128)(2,1)S(1)}, u32[]{:S(2)}, u32[]{:S(2)}) collective-permute-start(bf16[2,256,128]{2,1,0:T(8,128)(2,1)S(1)} %split_heads.2.refs_4_), channel_id=1, source_target_pairs={{0,2},{2,0},{1,3},{3,1},{4,6},{6,4},{5,7},{7,5},{8,10},{10,8},{9,1... | collective-permute-start | bytes 393224 | tf_op jit(solution)/shard_map/ppermute | solution.py:529
  12.1 11.1 %collective-permute-start.3 = (bf16[2,256,128]{2,1,0:T(8,128)(2,1)S(1)}, bf16[2,256,128]{2,1,0:T(8,128)(2,1)S(1)}, u32[]{:S(2)}, u32[]{:S(2)}) collective-permute-start(bf16[2,256,128]{2,1,0:T(8,128)(2,1)S(1)} %collective-permute-done.2.refs_4_), channel_id=1, source_target_pairs={{0,4},{4,8},{8,12},{12,0},{1,5},{5,9},{9,13},{13,1},{2,6},{6,10},{... | collective-permute-start | bytes 393224 | tf_op jit(solution)/shard_map/ppermute | solution.py:525
  13.1 0.7 %copy-start = (s32[4]{0:T(128)S(1)}, s32[4]{0:T(128)}, u32[]{:S(2)}) copy-start(s32[4]{0:T(128)} %refs_0_.5) | copy-start | bytes 52
  13.1 0.7 %copy-start.1 = (s32[16,1]{0,1:T(1,128)S(1)}, s32[16,1]{0,1:T(1,128)}, u32[]{:S(2)}) copy-start(s32[16,1]{0,1:T(1,128)} %param.11) | copy-start | bytes 196
  13.1 0.7 %copy-start.3 = (s32[4]{0:T(128)S(1)}, s32[4]{0:T(128)}, u32[]{:S(2)}) copy-start(s32[4]{0:T(128)} %refs_1_.5) | copy-start | bytes 52
  16.0 11.4 %collective-permute-start.11 = (bf16[2,256,128]{2,1,0:T(8,128)(2,1)S(1)}, bf16[2,256,128]{2,1,0:T(8,128)(2,1)S(1)}, u32[]{:S(2)}, u32[]{:S(2)}) collective-permute-start(bf16[2,256,128]{2,1,0:T(8,128)(2,1)S(1)} %collective-permute-done.2.refs_4_), channel_id=1, source_target_pairs={{0,2},{2,0},{1,3},{3,1},{4,6},{6,4},{5,7},{7,5},{8,10},{10,8},{9,1... | collective-permute-start | bytes 393224 | tf_op jit(solution)/shard_map/ppermute | solution.py:529
  17.4 10.1 %collective-permute-start.6 = (bf16[2,256,128]{2,1,0:T(8,128)(2,1)S(1)}, bf16[2,256,128]{2,1,0:T(8,128)(2,1)S(1)}, u32[]{:S(2)}, u32[]{:S(2)}) collective-permute-start(bf16[2,256,128]{2,1,0:T(8,128)(2,1)S(1)} %collective-permute-done.5.refs_3_.refs_5_), channel_id=1, source_target_pairs={{0,4},{4,8},{8,12},{12,0},{1,5},{5,9},{9,13},{13,1},{2,6},{6,10},{... | collective-permute-start | bytes 393224 | tf_op jit(solution)/shard_map/ppermute | solution.py:525
  20.5 6.9 %collective-permute-start.9 = (bf16[2,256,128]{2,1,0:T(8,128)(2,1)S(1)}, bf16[2,256,128]{2,1,0:T(8,128)(2,1)S(1)}, u32[]{:S(2)}, u32[]{:S(2)}) collective-permute-start(bf16[2,256,128]{2,1,0:T(8,128)(2,1)S(1)} %collective-permute-done.8.refs_6_), channel_id=1, source_target_pairs={{0,2},{2,0},{1,3},{3,1},{4,6},{6,4},{5,7},{7,5},{8,10},{10,8},{9,1... | collective-permute-start | bytes 393224 | tf_op jit(solution)/shard_map/ppermute | solution.py:529
  23.2 5.2 %collective-permute-start.10 = (bf16[2,256,128]{2,1,0:T(8,128)(2,1)S(1)}, bf16[2,256,128]{2,1,0:T(8,128)(2,1)S(1)}, u32[]{:S(2)}, u32[]{:S(2)}) collective-permute-start(bf16[2,256,128]{2,1,0:T(8,128)(2,1)S(1)} %collective-permute-done.3.refs_4_), channel_id=1, source_target_pairs={{0,2},{2,0},{1,3},{3,1},{4,6},{6,4},{5,7},{7,5},{8,10},{10,8},{9,1... | collective-permute-start | bytes 393224 | tf_op jit(solution)/shard_map/ppermute | solution.py:529
  29.2 1.9 %collective-permute-start.12 = (bf16[8,2,2,32,128]{4,3,2,1,0:T(8,128)(2,1)S(1)}, bf16[8,2,2,32,128]{4,3,2,1,0:T(8,128)(2,1)S(1)}, u32[]{:S(2)}, u32[]{:S(2)}) collective-permute-start(bf16[8,2,2,32,128]{4,3,2,1,0:T(8,128)(2,1)S(1)} %get-tuple-element.13), channel_id=1, source_target_pairs={{0,1},{1,0},{2,3},{3,2},{4,5},{5,4},{6,7},{7,6},{8,9},{9,8},{10,11... | collective-permute-start | bytes 786440 | tf_op jit(solution)/shard_map/ppermute | solution.py:529
